TPU v7x, 32 devices: a whole 2x2x4 slice. The times are simulated.
32 devices in a mesh: group: 2 (over y), gx: 4 (over z), gy: 2 (over x), gz: 2 (over core).
Axes of the slice: x: 2, y: 2, z: 4, core: 2. Of those that a mesh axis runs over, the one named last changes fastest.
Arguments:
- tokens: bfloat16 [12, 8192], P('group', 'gx'), parts along dimension 0, may hold values from -40 to 40
- norm_gain: float32 [8192], P('gx'), may hold values from 0.1 to 1.9
- q_weight: bfloat16 [8192, 4096], P('gx', ('gy', 'gz')), may hold values from -0.0625 to 0.0625
- kv_weight: bfloat16 [8192, 512], P('gx'), may hold values from -0.0625 to 0.0625
- out_weight: bfloat16 [4096, 8192], P(('gy', 'gz'), 'gx'), may hold values from -0.09375 to 0.09375
- gate_weight: bfloat16 [8192, 16384], P('gx', ('gy', 'gz')), may hold values from -0.0625 to 0.0625
- up_weight: bfloat16 [8192, 16384], P('gx', ('gy', 'gz')), may hold values from -0.0625 to 0.0625
- down_weight: bfloat16 [16384, 8192], P(('gy', 'gz'), 'gx'), may hold values from -0.046875 to 0.046875
- kv_cache: bfloat16 [12, 2048, 512], P(('group', 'gy'), ('gx', 'gz')), parts along dimension 0, may hold values from -55 to 55
- lengths: int32 [12], P(('group', 'gy')), parts along dimension 0, may hold values from 1026 to 2048, as said below
Outputs:
- mixed: bfloat16 [12, 8192], P('group', 'gx'), parts along dimension 0
- new_kv: bfloat16 [12, 512], P(('group', 'gy')), parts along dimension 0
There are 2 independent parts, one for each index of `group`. A program takes and returns all parts, laid end to end along the dimension named above; an argument that names none is the same for every part. Nothing has to cross between parts.
Inputs may be any that keep to these rules, and one draw needn't show every extreme that they name: The new token of sequence s stands at position lengths[s]; cache positions from lengths[s] on hold no valid token; some sequence has all 2048 positions valid.
All inputs are finite; a program needn't handle non-finite values.
Results may differ from a plain program's by a relative error of at most 0.012.
Values may be sent and summed in bfloat16 or wider, within the bound.
No kernel may reach another device: no remote copies, remote signals or barrier semaphores. Data moves between devices by JAX's collectives and lax.ppermute only.
A program may use at most 128 MiB of HBM per device.

v0:
```python
import jax
import jax.numpy as jnp
from jax import lax
from jax.sharding import PartitionSpec as P

D = 8192
HEADS = 16
HEAD_DIM = 256


epsilon = 1e-05
masked_fill = -1e30
rotary_base = 10000.0


def joined(part, axis, combine):
    gathered = jax.tree.map(lambda a: lax.all_gather(a, axis), part)

    def take(source):
        return jax.tree.map(lambda a: lax.dynamic_index_in_dim(a, source, 0, False), gathered)

    return lax.fori_loop(
        1, lax.axis_size(axis), lambda source, state: combine(state, take(source)), take(0)
    )


def rotate(values, angle):
    middle = values.shape[-1] // 2
    first = values[..., :middle]
    second = values[..., middle:]
    cosine = jnp.cos(angle)
    sine_part = jnp.sin(angle)
    return jnp.concatenate(
        [first * cosine - second * sine_part, first * sine_part + second * cosine], -1
    )


def angles(lengths, head_dim):
    middle = head_dim // 2
    spread = rotary_base ** (-jnp.arange(middle, dtype=jnp.float32) / middle)
    return lengths.astype(jnp.float32)[:, None] * spread[None, :]


def combine(earlier, later):
    top = jnp.maximum(earlier[0], later[0])
    first_scale = jnp.exp(earlier[0] - top)
    second_scale = jnp.exp(later[0] - top)
    numer = earlier[1] * first_scale[..., None] + later[1] * second_scale[..., None]
    denom = earlier[2] * first_scale + later[2] * second_scale
    return (top, numer, denom)


def body(
    tokens,
    norm_gain,
    q_weight,
    kv_weight,
    out_weight,
    gate_weight,
    up_weight,
    down_weight,
    kv_cache,
    lengths,
):
    inputs = tokens.astype(jnp.float32)
    totals = lax.psum((jnp.sum(inputs, 1), jnp.sum(inputs * inputs, 1)), "gx")
    center = totals[0] / D
    spread_sq = totals[1] / D - center * center
    normed = (
        (inputs - center[:, None]) * lax.rsqrt(spread_sq + epsilon)[:, None] * norm_gain[None, :]
    ).astype(jnp.bfloat16)
    query_part = jnp.dot(normed, q_weight, preferred_element_type=jnp.float32)
    keyval_part = jnp.dot(normed, kv_weight, preferred_element_type=jnp.float32)
    gate_part = jnp.dot(normed, gate_weight, preferred_element_type=jnp.float32)
    up_part = jnp.dot(normed, up_weight, preferred_element_type=jnp.float32)
    query, keyval, gate, upward = lax.psum((query_part, keyval_part, gate_part, up_part), "gx")
    hidden = (jax.nn.silu(gate) * upward).astype(jnp.bfloat16)
    seq_dev = lengths.shape[0]
    row_groups = lax.axis_size("gy")
    block = q_weight.shape[1]
    first_row = lax.axis_index("gy") * seq_dev
    angle = angles(lengths, HEAD_DIM)
    own_keyval = lax.dynamic_slice_in_dim(keyval, first_row, seq_dev, 0)
    new_kv = jnp.concatenate(
        [rotate(own_keyval[:, :HEAD_DIM], angle), own_keyval[:, HEAD_DIM:]], 1
    ).astype(jnp.bfloat16)
    query_bf = query.astype(jnp.bfloat16)
    every_head = lax.all_gather(query_bf, ("gy", "gz"), axis=1, tiled=True)
    own_query = lax.dynamic_slice_in_dim(every_head, first_row, seq_dev, 0)
    rotated = rotate(
        own_query.astype(jnp.float32).reshape(seq_dev, HEADS, HEAD_DIM), angle[:, None, :]
    ).astype(jnp.bfloat16)
    ctx_dev = kv_cache.shape[1]
    offset = lax.axis_index(("gx", "gz")) * ctx_dev
    positions = offset + jnp.arange(ctx_dev, dtype=jnp.int32)
    live = positions[None, :] < lengths[:, None]
    scale = HEAD_DIM ** (-0.5)
    scores = (
        jnp.einsum(
            "shd,scd->shc", rotated, kv_cache[:, :, :HEAD_DIM], preferred_element_type=jnp.float32
        )
        * scale
    )
    key_new = new_kv[:, :HEAD_DIM]
    value_new = new_kv[:, HEAD_DIM:]
    own_score = (
        jnp.einsum("shd,sd->sh", rotated, key_new, preferred_element_type=jnp.float32) * scale
    )
    hidden_scores = jnp.where(live[:, None, :], scores, masked_fill)
    local_top = jnp.maximum(jnp.max(hidden_scores, 2), own_score)
    weights = jnp.where(live[:, None, :], jnp.exp(hidden_scores - local_top[..., None]), 0.0)
    numer = jnp.einsum(
        "shc,scd->shd",
        weights.astype(jnp.bfloat16),
        kv_cache[:, :, HEAD_DIM:],
        preferred_element_type=jnp.float32,
    )
    denom = jnp.sum(weights, 2)
    top, numer, denom = joined((local_top, numer, denom), ("gx", "gz"), combine)
    own_weight = jnp.exp(own_score - top)
    numer = numer + own_weight[..., None] * value_new.astype(jnp.float32)[:, None, :]
    denom = denom + own_weight
    attended = (numer / denom[..., None]).astype(jnp.bfloat16)
    grouped = attended.reshape(seq_dev, row_groups, HEADS * HEAD_DIM // row_groups)
    picked = lax.dynamic_slice_in_dim(grouped, lax.axis_index("gz") * block, block, 2)
    head_block = lax.all_to_all(picked, "gy", split_axis=1, concat_axis=0, tiled=True).reshape(
        seq_dev * row_groups, block
    )
    partial_value = jnp.dot(head_block, out_weight, preferred_element_type=jnp.float32) + jnp.dot(
        hidden, down_weight, preferred_element_type=jnp.float32
    )
    total = lax.psum(partial_value, ("gy", "gz"))
    mixed = (inputs + total).astype(jnp.bfloat16)
    return (mixed, new_kv)


def solution(mesh):
    in_specs = (
        P("group", "gx"),
        P("gx"),
        P("gx", ("gy", "gz")),
        P("gx", None),
        P(("gy", "gz"), "gx"),
        P("gx", ("gy", "gz")),
        P("gx", ("gy", "gz")),
        P(("gy", "gz"), "gx"),
        P(("group", "gy"), ("gx", "gz"), None),
        P(("group", "gy")),
    )
    out_specs = (P("group", "gx"), P(("group", "gy"), None))
    return jax.shard_map(body, mesh=mesh, in_specs=in_specs, out_specs=out_specs, check_vma=False)
```

profile of v0, /device:TPU:0, one launch (start us, length us, event | category | flops | bytes accessed | tf_op | source)
XLA Modules:
  0.0 137.4 jit_solution(9791205990848251122)
XLA Ops:
  7.2 1.1 convert_reduce_fusion
  8.3 13.5 %all-reduce.1 = (f32[6]{0:T(128)S(1)}, f32[6]{0:T(128)S(1)}) all-reduce(f32[6]{0:T(128)S(1)} %get-tuple-element.184, f32[6]{0:T(128)S(1)} %get-tuple-element.183), channel_id=1, replica_groups=mesh['group'=2,'gx'=4,'gy'=2,'gz'=2] {'gx'}, use_global_device_ids=true, to_apply=%region_3.0 | all-reduce | flops 12 | bytes 96 | tf_op jit(solution)/shard_map/psum | solution.py:66
  21.8 8.9 %fusion.29 = f32[6,4096]{1,0:T(8,128)} fusion(bf16[2048,4096]{1,0:T(8,128)(2,1)} %param.17, bf16[6,2048]{1,0:T(8,128)(2,1)} %param.12, f32[2048]{0:T(1024)} %param.13, f32[6]{0:T(128)S(1)} %get-tuple-element.220, f32[6]{0:T(128)S(1)} %get-tuple-element.219), kind=kOutput, calls=%fused_computation.63 | convolution fusion | flops 100724736 | bytes 16908336 | tf_op jit(solution)/shard_map/dot_general | solution.py:74
  30.7 1.7 %copy-done.1 = bf16[2048,4096]{1,0:T(8,128)(2,1)S(1)} copy-done((bf16[2048,4096]{1,0:T(8,128)(2,1)S(1)}, bf16[2048,4096]{1,0:T(8,128)(2,1)}, u32[]{:S(2)}) %copy-start.1) | copy-done | bytes 16777240
  32.4 3.0 %fusion.27 = f32[6,4096]{1,0:T(8,128)} fusion(bf16[2048,4096]{1,0:T(8,128)(2,1)S(1)} %copy-done.1, bf16[6,2048]{1,0:T(8,128)(2,1)S(1)} %copy-done.3, f32[2048]{0:T(1024)S(1)} %copy-done.4, f32[6]{0:T(128)S(1)} %get-tuple-element.220, f32[6]{0:T(128)S(1)} %get-tuple-element.219), kind=kOutput, calls=%fused_computation.62 | convolution fusion | flops 100724736 | bytes 16908336 | tf_op jit(solution)/shard_map/dot_general | solution.py:75
  35.4 2.9 %fusion.33 = f32[6,1024]{1,0:T(8,128)S(1)} fusion(bf16[2048,1024]{1,0:T(8,128)(2,1)} %param.14, bf16[6,2048]{1,0:T(8,128)(2,1)S(1)} %copy-done.3, f32[2048]{0:T(1024)S(1)} %copy-done.4, f32[6]{0:T(128)S(1)} %get-tuple-element.220, f32[6]{0:T(128)S(1)} %get-tuple-element.219), kind=kOutput, calls=%fused_computation.65 | convolution fusion | flops 25227264 | bytes 4251696 | tf_op jit(solution)/shard_map/dot_general | solution.py:72
  38.3 0.4 fusion.31
  38.7 16.3 %all-reduce = (bf16[6,1024]{1,0:T(8,128)(2,1)S(1)}, f32[6,512]{1,0:T(8,128)S(1)}) all-reduce(f32[6,1024]{1,0:T(8,128)S(1)} %fusion.33, f32[6,512]{1,0:T(8,128)S(1)} %fusion.31), channel_id=1, replica_groups=mesh['group'=2,'gx'=4,'gy'=2,'gz'=2] {'gx'}, use_global_device_ids=true, to_apply=%region_4.0 | all-reduce | flops 9216 | bytes 61440 | tf_op jit(solution)/shard_map/psum | solution.py:76
  55.0 5.2 %all_gather.21 = bf16[6,4096]{1,0:T(8,128)(2,1)S(1)} all-gather(bf16[6,1024]{1,0:T(8,128)(2,1)S(1)} %get-tuple-element.199), channel_id=1, replica_groups=mesh['group'=2,'gx'=4,'gy'=2,'gz'=2] {'gy','gz'}, dimensions={1}, use_global_device_ids=true | all-gather | bytes 61440 | tf_op jit(solution)/shard_map/all_gather | solution.py:88
  60.6 0.3 fusion.38
  60.9 0.2 fusion.14
  61.1 0.2 fusion.4
  61.4 12.7 %all-gather.4 = f32[8,3,16]{2,1,0:T(4,128)S(1)} all-gather(f32[1,3,16]{2,1,0:T(4,128)S(1)} %bitcast.56), channel_id=4, replica_groups=mesh['group'=2,'gx'=4,'gy'=2,'gz'=2] {'gx','gz'}, dimensions={0}, use_global_device_ids=true | all-gather | bytes 1728 | tf_op jit(solution)/shard_map/all_gather | solution.py:17
  74.1 14.5 %all-gather.1 = f32[24,16,256]{2,1,0:T(8,128)S(1)} all-gather(f32[3,16,256]{2,1,0:T(8,128)S(1)} %fusion.4), channel_id=3, replica_groups=mesh['group'=2,'gx'=4,'gy'=2,'gz'=2] {'gx','gz'}, dimensions={0}, use_global_device_ids=true | all-gather | bytes 442368 | tf_op jit(solution)/shard_map/all_gather | solution.py:17
  88.6 12.7 %all-gather.3 = f32[8,3,16]{2,1,0:T(4,128)S(1)} all-gather(f32[1,3,16]{2,1,0:T(4,128)S(1)} %bitcast.55), channel_id=2, replica_groups=mesh['group'=2,'gx'=4,'gy'=2,'gz'=2] {'gx','gz'}, dimensions={0}, use_global_device_ids=true | all-gather | bytes 1728 | tf_op jit(solution)/shard_map/all_gather | solution.py:17
  101.3 0.9 while.19
  102.5 0.6 copy.16
  103.1 3.2 %all-to-all-start = ((bf16[3,2,1024]{2,0,1:T(4,128)(2,1)}), bf16[3,2,1024]{2,0,1:T(4,128)(2,1)S(1)}, u32[]{:S(2)}, u32[]{:S(2)}) async-start(bf16[3,2,1024]{2,0,1:T(4,128)(2,1)} %copy.16), calls=%async_computation | async-start | bytes 32768 | tf_op jit(solution)/shard_map/all_to_all | solution.py:126
  106.3 0.6 pad_maximum_fusion.3
  106.9 3.2 %all-to-all-done = bf16[3,2,1024]{2,0,1:T(4,128)(2,1)S(1)} async-done(((bf16[3,2,1024]{2,0,1:T(4,128)(2,1)}), bf16[3,2,1024]{2,0,1:T(4,128)(2,1)S(1)}, u32[]{:S(2)}, u32[]{:S(2)}) %all-to-all-start) | async-done | bytes 12320 | tf_op jit(solution)/shard_map/all_to_all | solution.py:126
  110.2 8.3 %fusion.12 = f32[6,2048]{1,0:T(8,128)S(1)} fusion(bf16[4096,2048]{1,0:T(8,128)(2,1)} %param.19, f32[6,4096]{1,0:T(8,128)} %get-tuple-element.203, f32[6,4096]{1,0:T(8,128)} %get-tuple-element.204), kind=kOutput, calls=%fused_computation.24 | convolution fusion | flops 100810752 | bytes 17022976 | tf_op jit(solution)/shard_map/dot_general | solution.py:129
  118.6 0.7 convolution_add_fusion
  119.2 10.7 %psum.55 = f32[6,2048]{1,0:T(8,128)S(1)} all-reduce(f32[6,2048]{1,0:T(8,128)S(1)} %convolution_add_fusion), channel_id=1, replica_groups=mesh['group'=2,'gx'=4,'gy'=2,'gz'=2] {'gy','gz'}, use_global_device_ids=true, to_apply=%region_12.13 | all-reduce | flops 12288 | bytes 98304 | tf_op jit(solution)/shard_map/psum | solution.py:132
  129.9 0.6 fusion.11
  (51 shorter events, 1.5 us)
Async XLA Ops:
  7.2 31.1 %copy-start = (bf16[2048,512]{1,0:T(8,128)(2,1)S(1)}, bf16[2048,512]{1,0:T(8,128)(2,1)}, u32[]{:S(2)}) copy-start(bf16[2048,512]{1,0:T(8,128)(2,1)} %param.15) | copy-start | bytes 6291460
  7.2 23.5 %copy-start.3 = (bf16[6,2048]{1,0:T(8,128)(2,1)S(1)}, bf16[6,2048]{1,0:T(8,128)(2,1)}, u32[]{:S(2)}) copy-start(bf16[6,2048]{1,0:T(8,128)(2,1)} %param.12) | copy-start | bytes 73732
  7.2 23.5 %copy-start.4 = (f32[2048]{0:T(1024)S(1)}, f32[2048]{0:T(1024)}, u32[]{:S(2)}) copy-start(f32[2048]{0:T(1024)} %param.13) | copy-start | bytes 24580
  7.2 103.0 %all-reduce.5.cloned.1.call-start = ((), (), s32[]{:S(2)}) async-start(), calls=%async_computation.1 | async-start | bytes 524288 | tf_op jit(solution)/shard_map/psum | solution.py:76
  21.8 10.6 %copy-start.1 = (bf16[2048,4096]{1,0:T(8,128)(2,1)S(1)}, bf16[2048,4096]{1,0:T(8,128)(2,1)}, u32[]{:S(2)}) copy-start(bf16[2048,4096]{1,0:T(8,128)(2,1)} %param.18) | copy-start | bytes 50331652
  32.4 6.3 %copy-start.6 = (s32[3]{0:T(128)S(1)}, s32[3]{0:T(128)}, u32[]{:S(2)}) copy-start(s32[3]{0:T(128)} %param.21) | copy-start | bytes 40
  32.4 28.2 %copy-start.5 = (bf16[3,256,512]{2,1,0:T(8,128)(2,1)S(1)}, bf16[3,256,512]{2,1,0:T(8,128)(2,1)}, u32[]{:S(2)}) copy-start(bf16[3,256,512]{2,1,0:T(8,128)(2,1)} %param.20) | copy-start | bytes 2359300
  103.1 7.1 %all-to-all-start = ((bf16[3,2,1024]{2,0,1:T(4,128)(2,1)}), bf16[3,2,1024]{2,0,1:T(4,128)(2,1)S(1)}, u32[]{:S(2)}, u32[]{:S(2)}) async-start(bf16[3,2,1024]{2,0,1:T(4,128)(2,1)} %copy.16), calls=%async_computation | async-start | bytes 32768 | tf_op jit(solution)/shard_map/all_to_all | solution.py:126
  110.2 8.3 %copy-start.2 = (bf16[1024,2048]{1,0:T(8,128)(2,1)S(1)}, bf16[1024,2048]{1,0:T(8,128)(2,1)}, u32[]{:S(2)}) copy-start(bf16[1024,2048]{1,0:T(8,128)(2,1)} %param.16) | copy-start | bytes 12582916
Sparse Core Ops, SparseCore 0:
  35.5 34.2 all-reduce.4
where the time goes:
time: 138 us; the launch traced here: 137 us
  blocking collectives  85.6 us (62%)
  matrix products  24.8 us (18%)
  between operations  14.2 us (10%)
  other arithmetic  3.69 us (3%)
  waiting for transfers between devices  3.28 us (2%)
  starting transfers between devices  3.27 us (2%)
  local copies, waits for them, and re-layouts  2.41 us (2%)
    all_gather x3, blocking collectives, joined(): gathered = jax.tree.map(lambda a: lax.all_gather(a, axis), part)  39.9 us
    psum x1, blocking collectives, body(): lax.psum((query_part, keyval_part, gate_part, up_part), 'gx')  16.3 us
    psum x1, blocking collectives, body(): totals = lax.psum((jnp.sum(inputs, 1), jnp.sum(inputs * inputs, 1)), 'gx')  13.5 us
    psum x1, blocking collectives, body(): total = lax.psum(partial_value, ('gy', 'gz'))  10.7 us
    dot_general x1, matrix products, body(): gate_part = jnp.dot(normed, gate_weight, preferred_element_type=jnp.float32)  8.91 us
    dot_general x1, matrix products, body(): jnp.dot(hidden, down_weight, preferred_element_type=jnp.float32)  8.31 us
    all_gather x1, blocking collectives, body(): every_head = lax.all_gather(query_bf, ('gy', 'gz'), axis=1, tiled=True)  5.25 us
    all_to_all x1, waiting for transfers between devices, body(): lax.all_to_all(picked, 'gy', split_axis=1, concat_axis=0, tiled=True)  3.24 us
  transfers between devices with their start and end apart: 2, of which 1 were waited for; matrix products, arithmetic and copies ran while one was open for 5% of the time, Pallas kernels for 0%

commit v1 on v0

v1 whole, which is shorter than its diff:
```python
import jax
import jax.numpy as jnp
from jax import lax
from jax.sharding import PartitionSpec as P

epsilon = 1e-05
masked_fill = -1e30
rotary_base = 10000.0
PART = ("gx", "gy", "gz")
FEW = 8


def rotate(values, angle):
    middle = values.shape[-1] // 2
    first = values[..., :middle]
    second = values[..., middle:]
    cosine = jnp.cos(angle)
    sine_part = jnp.sin(angle)
    return jnp.concatenate(
        [first * cosine - second * sine_part, first * sine_part + second * cosine], -1
    )


def angles(lengths, head_dim):
    middle = head_dim // 2
    spread = rotary_base ** (-jnp.arange(middle, dtype=jnp.float32) / middle)
    return lengths.astype(jnp.float32)[:, None] * spread[None, :]


def in_thirds(values):
    high = lax.reduce_precision(values, 8, 7)
    rest = values - high
    middle = lax.reduce_precision(rest, 8, 7)
    return jnp.stack([high, middle, rest - middle], -1).astype(jnp.bfloat16)


def from_thirds(terms):
    terms = terms.astype(jnp.float32)
    return terms[..., 0] + (terms[..., 1] + terms[..., 2])


def from_others(values, axis):
    size = lax.axis_size(axis)
    return [
        lax.ppermute(values, axis, [(place, place ^ step) for place in range(size)])
        for step in range(1, size)
    ]


def body(
    tokens,
    norm_gain,
    q_weight,
    kv_weight,
    out_weight,
    gate_weight,
    up_weight,
    down_weight,
    kv_cache,
    lengths,
):
    gx, gy, gz = (lax.axis_size(axis) for axis in PART)
    cols = gy * gz
    seqs, width = tokens.shape
    seq_dev = lengths.shape[0]
    head_dim = kv_weight.shape[1] // 2
    q_dev = q_weight.shape[1]
    heads_dev = q_dev // head_dim
    heads = heads_dev * cols
    kv_dev = kv_weight.shape[1] // cols
    ctx_dev = kv_cache.shape[1]
    row = lax.axis_index("gy")
    col = lax.axis_index(("gy", "gz"))

    inputs = tokens.astype(jnp.float32)
    mean_dev = jnp.sum(inputs, 1) / width
    centred = inputs - mean_dev[:, None]
    square_dev = jnp.sum(centred * centred, 1)
    lhs = jnp.concatenate([centred * norm_gain[None, :], norm_gain[None, :]], 0).astype(jnp.bfloat16)

    def project(weight):
        return jnp.dot(lhs, weight, preferred_element_type=jnp.float32)

    kv_own = lax.dynamic_slice_in_dim(kv_weight, col * kv_dev, kv_dev, 1)
    first = jnp.concatenate([project(q_weight), project(kv_own)], 1).astype(jnp.bfloat16)
    stats = in_thirds(jnp.stack([mean_dev, square_dev])).reshape(-1)
    extra = -(-stats.shape[0] // 128) * 128
    stats = jnp.pad(stats, (0, extra - stats.shape[0]))
    by_row = first[:seqs].reshape(gy, seq_dev, -1)
    gain_row = jnp.broadcast_to(first[seqs], (gy, 1, first.shape[1]))
    by_row = jnp.concatenate([by_row, gain_row], 1)
    by_row = jnp.concatenate(
        [by_row, jnp.broadcast_to(stats, (gy, seq_dev + 1, extra))], 2
    )
    sent = jnp.broadcast_to(by_row[None, :, None], (gx, gy, gz) + by_row.shape[1:])
    sent = sent.reshape((gx * cols,) + by_row.shape[1:])
    got = lax.all_to_all(sent, PART, split_axis=0, concat_axis=0, tiled=True)
    got = got.reshape((gx, cols) + by_row.shape[1:])

    gate_part = project(gate_weight).astype(jnp.bfloat16)
    up_part = project(up_weight).astype(jnp.bfloat16)

    stats = from_thirds(got[:, 0, 0, -extra:][:, : seqs * 6].reshape(gx, 2, seqs, 3))
    means = stats[:, 0]
    center = jnp.sum(means, 0) / gx
    shift = means - center
    spread_sq = jnp.sum(stats[:, 1], 0) / (width * gx) + jnp.sum(shift * shift, 0) / gx
    inverse = lax.rsqrt(spread_sq + epsilon)

    def whole(parts, shift, inverse):
        total = 0.0
        for source in range(gx):
            part = parts[source].astype(jnp.float32)
            total += part[..., :-1, :] + shift[source][:, None] * part[..., -1:, :]
        return total * inverse[:, None]

    shift_row = lax.dynamic_slice_in_dim(shift, row * seq_dev, seq_dev, 1)
    inverse_row = lax.dynamic_slice_in_dim(inverse, row * seq_dev, seq_dev, 0)
    summed = whole([got[s, :, :, : q_dev + kv_dev] for s in range(gx)], shift_row, inverse_row)
    query = summed[..., :q_dev].astype(jnp.bfloat16)
    keyval = summed[..., q_dev:].transpose(1, 0, 2).reshape(seq_dev, -1)
    angle = angles(lengths, head_dim)
    new_kv = jnp.concatenate(
        [rotate(keyval[:, :head_dim], angle), keyval[:, head_dim:]], 1
    ).astype(jnp.bfloat16)
    query = query.reshape(cols, seq_dev, heads_dev, head_dim).transpose(1, 0, 2, 3)
    query = query.reshape(seq_dev, heads, head_dim)
    rotated = rotate(query.astype(jnp.float32), angle[:, None, :]).astype(jnp.bfloat16)

    block = lax.axis_index(("gx", "gz"))
    positions = block * ctx_dev + jnp.arange(ctx_dev, dtype=jnp.int32)
    live = positions[None, :] < lengths[:, None]
    scale = head_dim ** (-0.5)
    scores = (
        jnp.einsum(
            "shd,scd->shc", rotated, kv_cache[:, :, :head_dim], preferred_element_type=jnp.float32
        )
        * scale
    )
    own_score = (
        jnp.sum(rotated.astype(jnp.float32) * new_kv[:, None, :head_dim].astype(jnp.float32), -1)
        * scale
    )
    masked = jnp.where(live[:, None, :], scores, masked_fill)
    top = jnp.maximum(jnp.max(masked, 2), own_score)
    weights = jnp.where(live[:, None, :], jnp.exp(masked - top[..., None]), 0.0)
    own_weight = jnp.where(block == 0, jnp.exp(own_score - top), 0.0)
    numer = jnp.einsum(
        "shc,scd->shd",
        weights.astype(jnp.bfloat16),
        kv_cache[:, :, head_dim:],
        preferred_element_type=jnp.float32,
    )
    numer = numer + own_weight[..., None] * new_kv[:, None, head_dim:].astype(jnp.float32)
    denom = jnp.sum(weights, 2) + own_weight

    marks = in_thirds(jnp.stack([top, denom], -1)).reshape(seq_dev, heads, 6)
    marks = jnp.pad(marks, ((0, 0), (0, 0), (0, 122)))
    partial = jnp.concatenate([numer.astype(jnp.bfloat16), marks], 2)
    partial = partial.reshape(seq_dev, cols, heads_dev, -1).transpose(1, 0, 2, 3)
    sent = jnp.broadcast_to(partial[None], (gx,) + partial.shape)
    sent = sent.reshape(gx * cols, seq_dev * heads_dev, -1)
    got = lax.all_to_all(sent, PART, split_axis=0, concat_axis=0, tiled=True)

    both = jnp.concatenate([gate_part, up_part], 1)
    parts = [both] + from_others(both, "gx")
    place = lax.axis_index("gx")
    shifts = [
        lax.dynamic_index_in_dim(shift, place ^ step, 0, False) for step in range(gx)
    ]
    summed = whole(parts, shifts, inverse)
    ff_dev = gate_weight.shape[1]
    hidden = (jax.nn.silu(summed[:, :ff_dev]) * summed[:, ff_dev:]).astype(jnp.bfloat16)
    total = jnp.dot(hidden, down_weight, preferred_element_type=jnp.float32)

    got = got.reshape(gx, gy, gz, seq_dev, heads_dev, -1)
    marks = from_thirds(got[..., head_dim : head_dim + 6].reshape(got.shape[:-1] + (2, 3)))
    tops, denoms = marks[..., 0], marks[..., 1]
    factor = jnp.exp(tops - jnp.max(tops, (0, 2), keepdims=True))
    denom = jnp.sum(denoms * factor, (0, 2))
    numer = jnp.sum(got[..., :head_dim].astype(jnp.float32) * factor[..., None], (0, 2))
    attended = (numer / denom[..., None]).astype(jnp.bfloat16).reshape(seqs, q_dev)
    total = total + jnp.dot(attended, out_weight, preferred_element_type=jnp.float32)

    share = total.astype(jnp.bfloat16)
    for other in from_others(share, ("gy", "gz")):
        total = total + other.astype(jnp.float32)
    mixed = (inputs + total).astype(jnp.bfloat16)
    return (mixed, new_kv)


def solution(mesh):
    in_specs = (
        P("group", "gx"),
        P("gx"),
        P("gx", ("gy", "gz")),
        P("gx", None),
        P(("gy", "gz"), "gx"),
        P("gx", ("gy", "gz")),
        P("gx", ("gy", "gz")),
        P(("gy", "gz"), "gx"),
        P(("group", "gy"), ("gx", "gz"), None),
        P(("group", "gy")),
    )
    out_specs = (P("group", "gx"), P(("group", "gy"), None))
    return jax.shard_map(body, mesh=mesh, in_specs=in_specs, out_specs=out_specs, check_vma=False)
```

time: 138 us -> 70 us (0.51)
  blocking collectives: 85.6 us -> 0 us
  starting transfers between devices: 3.27 us -> 17.2 us
  between operations: 14.2 us -> 1.12 us
  other arithmetic: 3.69 us -> 10.9 us
  waiting for transfers between devices: 3.28 us -> 8.2 us
  local copies, waits for them, and re-layouts: 2.41 us -> 4.96 us
  matrix products: 24.8 us -> 27.2 us
    all_gather x4 -> x0, blocking collectives: 45.2 us -> none  [the longest x3 39.9 us: joined(): gathered = jax.tree.map(lambda a: lax.all_gather(a, axis), part)]
    psum x3 -> x0, blocking collectives: 40.4 us -> none  [the longest x1 16.3 us: body(): lax.psum((query_part, keyval_part, gate_part, up_part), 'gx')]
    ppermute x0 -> x6, starting transfers between devices: none -> 7.54 us  [from_others(): lax.ppermute(values, axis, [(place, place ^ step) for place in range(size)])]
    all_to_all x1 -> x2, starting transfers between devices: 3.24 us -> 9.65 us  [body(): got = lax.all_to_all(sent, PART, split_axis=0, concat_axis=0, tiled=True)]
    ppermute x0 -> x6, waiting for transfers between devices: none -> 2.98 us  [from_others(): lax.ppermute(values, axis, [(place, place ^ step) for place in range(size)])]
    dot_general x9 -> x8, matrix products: 24.8 us -> 27.2 us  [the longest x4 13.7 us: project(): return jnp.dot(lhs, weight, preferred_element_type=jnp.float32)]
    reduce_sum x2 -> x8, other arithmetic: 1.25 us -> 3.56 us  [the longest x1 1.24 us: body(): square_dev = jnp.sum(centred * centred, 1)]
    all_to_all x1 -> x2, waiting for transfers between devices: 3.24 us -> 5.22 us  [body(): got = lax.all_to_all(sent, PART, split_axis=0, concat_axis=0, tiled=True)]
  transfers between devices with their start and end apart: 2 -> 8, of which waited for: 1 -> 3; matrix products, arithmetic and copies ran while one was open for 5% -> 24% of each run, Pallas kernels for 0% -> 0%
where the time goes in v1:
time: 70 us; the launch traced here: 69.5 us
  matrix products  27.2 us (39%)
  starting transfers between devices  17.2 us (25%)
  other arithmetic  10.9 us (16%)
  waiting for transfers between devices  8.2 us (12%)
  local copies, waits for them, and re-layouts  4.96 us (7%)
  between operations  1.12 us (2%)
    dot_general x4, matrix products, project(): return jnp.dot(lhs, weight, preferred_element_type=jnp.float32)  13.7 us
    all_to_all x2, starting transfers between devices, body(): got = lax.all_to_all(sent, PART, split_axis=0, concat_axis=0, tiled=True)  9.65 us
    dot_general x1, matrix products, body(): total = jnp.dot(hidden, down_weight, preferred_element_type=jnp.float32)  8.05 us
    ppermute x6, starting transfers between devices, from_others(): lax.ppermute(values, axis, [(place, place ^ step) for place in range(size)])  7.54 us
    all_to_all x2, waiting for transfers between devices, body(): got = lax.all_to_all(sent, PART, split_axis=0, concat_axis=0, tiled=True)  5.22 us
    ppermute x6, waiting for transfers between devices, from_others(): lax.ppermute(values, axis, [(place, place ^ step) for place in range(size)])  2.98 us
    dot_general x1, matrix products, body(): jnp.dot(attended, out_weight, preferred_element_type=jnp.float32)  2.84 us
    another operation x5, other arithmetic  1.89 us
  transfers between devices with their start and end apart: 8, of which 3 were waited for; matrix products, arithmetic and copies ran while one was open for 24% of the time, Pallas kernels for 0%

profile of v1, /device:TPU:0, one launch (start us, length us, event | category | flops | bytes accessed | tf_op | source)
XLA Modules:
  0.0 69.5 jit_solution(3296828416635271238)
XLA Ops:
  0.7 1.0 %convert_reduce_fusion = f32[6]{0:T(128)S(1)} fusion(bf16[6,2048]{1,0:T(8,128)(2,1)} %param.10), kind=kLoop, calls=%fused_computation.26 | loop fusion | flops 24570 | bytes 24600 | tf_op jit(solution)/shard_map/reduce_sum | solution.py:76
  1.7 1.1 %convert.60 = bf16[2048]{0:T(1024)(128)(2,1)S(1)} convert(f32[2048]{0:T(1024)} %param.11) | non-fusion elementwise | flops 2048 | bytes 12288 | tf_op jit(solution)/shard_map/convert.26
  2.8 1.2 %fusion.14 = (f32[6]{0:T(128)S(1)}, bf16[6,2048]{1,0:T(8,128)(2,1)S(1)}) fusion(bf16[6,2048]{1,0:T(8,128)(2,1)} %param.10, f32[6]{0:T(128)S(1)} %get-tuple-element.42, f32[2048]{0:T(1024)} %param.11), kind=kLoop, calls=%fused_computation.32 | loop fusion | flops 73722 | bytes 57392 | tf_op jit(solution)/shard_map/reduce_sum | solution.py:78
  4.0 8.4 %convolution_convert_fusion = bf16[7,4096]{1,0:T(8,128)(2,1)S(1)} fusion(bf16[2048,4096]{1,0:T(8,128)(2,1)} %param.16, bf16[1,2048]{1,0:T(2,128)(2,1)S(1)} %broadcast_in_dim.35, bf16[6,2048]{1,0:T(8,128)(2,1)S(1)} %get-tuple-element.17), kind=kOutput, calls=%fused_computation | convolution fusion | flops 117526528 | bytes 16863232 | tf_op jit(solution)/shard_map/dot_general | solution.py:82
  12.4 2.3 %convolution_convert_fusion.1 = bf16[7,4096]{1,0:T(8,128)(2,1)S(1)} fusion(bf16[2048,4096]{1,0:T(8,128)(2,1)S(1)} %copy-done.1, bf16[1,2048]{1,0:T(2,128)(2,1)S(1)} %broadcast_in_dim.35, bf16[6,2048]{1,0:T(8,128)(2,1)S(1)} %get-tuple-element.17), kind=kOutput, calls=%fused_computation.1 | convolution fusion | flops 117526528 | bytes 16863232 | tf_op jit(solution)/shard_map/dot_general | solution.py:82
  14.7 0.7 fusion.56
  15.4 4.0 %collective-permute-start.1 = (bf16[7,8192]{1,0:T(8,128)(2,1)}, bf16[7,8192]{1,0:T(8,128)(2,1)S(1)}, u32[]{:S(2)}, u32[]{:S(2)}) collective-permute-start(bf16[7,8192]{1,0:T(8,128)(2,1)} %get-tuple-element.13), channel_id=1, source_target_pairs={{0,8},{4,12},{8,0},{12,4},{1,9},{5,13},{9,1},{13,5},{2,10},{6,14},... | collective-permute-start | bytes 344072 | tf_op jit(solution)/shard_map/ppermute | solution.py:45
  19.4 1.6 %collective-permute-start = (bf16[7,8192]{1,0:T(8,128)(2,1)}, bf16[7,8192]{1,0:T(8,128)(2,1)S(1)}, u32[]{:S(2)}, u32[]{:S(2)}) collective-permute-start(bf16[7,8192]{1,0:T(8,128)(2,1)} %get-tuple-element.13), channel_id=1, source_target_pairs={{0,4},{4,0},{8,12},{12,8},{1,5},{5,1},{9,13},{13,9},{2,6},{6,2},{1... | collective-permute-start | bytes 344072 | tf_op jit(solution)/shard_map/ppermute | solution.py:45
  21.0 2.8 %convolution_convert_fusion.2 = bf16[7,1024]{1,0:T(8,128)(2,1)S(1)} fusion(bf16[2048,1024]{1,0:T(8,128)(2,1)} %param.12, bf16[1,2048]{1,0:T(2,128)(2,1)S(1)} %broadcast_in_dim.35, bf16[6,2048]{1,0:T(8,128)(2,1)S(1)} %get-tuple-element.17), kind=kOutput, calls=%fused_computation.7 | convolution fusion | flops 29424640 | bytes 4237312 | tf_op jit(solution)/shard_map/dot_general | solution.py:82
  24.4 0.7 %broadcast_in_dim.38 = bf16[4,2,2,4,1280]{4,3,2,1,0:T(4,128)(2,1)} broadcast(bf16[2,4,1280]{2,1,0:T(4,128)(2,1)S(1)} %maximum_maximum_fusion), dimensions={1,3,4} | broadcast | bytes 184320 | tf_op jit(solution)/shard_map/broadcast_in_dim | solution.py:95
  25.1 6.1 %all-to-all-start = ((bf16[16,4,1280]{2,1,0:T(4,128)(2,1)}), bf16[16,4,1280]{2,1,0:T(4,128)(2,1)S(1)}, u32[]{:S(2)}, u32[]{:S(2)}) async-start(bf16[16,4,1280]{2,1,0:T(4,128)(2,1)} %bitcast.4), calls=%async_computation | async-start | bytes 327680 | tf_op jit(solution)/shard_map/all_to_all | solution.py:97
  34.5 5.2 %all-to-all-done = bf16[16,4,1280]{2,1,0:T(4,128)(2,1)S(1)} async-done(((bf16[16,4,1280]{2,1,0:T(4,128)(2,1)}), bf16[16,4,1280]{2,1,0:T(4,128)(2,1)S(1)}, u32[]{:S(2)}, u32[]{:S(2)}) %all-to-all-start) | async-done | bytes 163872 | tf_op jit(solution)/shard_map/all_to_all | solution.py:97
  41.1 0.8 %subtract_convert_fusion.1 = (bf16[3,128]{1,0:T(4,128)(2,1)S(1)}, bf16[3,128]{1,0:T(4,128)(2,1)S(1)}, f32[3,128]{1,0:T(4,128)S(1)}, f32[3,128]{1,0:T(4,128)S(1)}) fusion(f32[3,512]{1,0:T(4,128)S(1)} %bitcast.137, f32[128]{0:T(128)} %multiply_power_fusion, f32[3]{0:T(128)} %convert_element_type.159), kind=kLoop, calls=%fused_computation.113 | loop fusion | flops 3456 | bytes 8204 | tf_op jit(solution)/shard_map/convert.12
  42.0 1.3 %fusion.59 = (f32[3,16]{1,0:T(4,128)S(1)}, f32[3,16,256]{2,1,0:T(8,128)S(1)}) fusion(bf16[3,256,512]{2,1,0:T(8,128)(2,1)} %param.18, bf16[3,16,128]{2,1,0:T(8,128)(2,1)S(1)} %get-tuple-element.15, bf16[3,16,128]{2,1,0:T(8,128)(2,1)S(1)} %get-tuple-element.14, pred[3,256]{1,0:T(4,128)(4,1)} %broadcast_compare_fusion), kind=kOutput, calls=%fused_computation.154 | convolution fusion | flops 6377424 | bytes 468160 | tf_op jit(solution)/shard_map/shd,scd->shc/dot_general | solution.py:135
  43.4 0.9 %fusion.24 = f32[3,16]{1,0:T(4,128)S(1)} fusion(f32[3,16,256]{2,1,0:T(8,128)S(1)} %get-tuple-element.44, f32[3,16]{1,0:T(4,128)S(1)} %get-tuple-element.21, pred[3,256]{1,0:T(4,128)(4,1)} %broadcast_compare_fusion), kind=kLoop, calls=%fused_computation.51 | loop fusion | flops 36816 | bytes 50304 | tf_op jit(solution)/shard_map/reduce_sum | solution.py:155
  44.4 1.2 %fusion.1 = bf16[3,16,256]{2,1,0:T(8,128)(2,1)S(1)} fusion(bf16[3,256,512]{2,1,0:T(8,128)(2,1)} %param.18, f32[3,16,256]{2,1,0:T(8,128)S(1)} %get-tuple-element.44, f32[3,256]{1,0:T(4,128)S(1)} %get-tuple-element.4, f32[3,16]{1,0:T(4,128)S(1)} %get-tuple-element.20, f32[3,16]{1,0:T(4,128)S(1)} %get-tuple-element.21, pred[3,256]{1,0:T(4,128)(4,1)} %broadcast_compare_fusion), kind=kOutput, calls=%fused_computation.6 | convolution fusion | flops 6365184 | bytes 471424 | tf_op jit(solution)/shard_map/shc,scd->shd/dot_general | solution.py:148
  45.8 0.7 %copy.75 = bf16[16,12,384]{2,1,0:T(8,128)(2,1)} copy(bf16[16,12,384]{2,0,1:T(8,128)(2,1)S(1)} %reshape.434) | data formatting | bytes 294912 | tf_op jit(solution)/shard_map/reshape | solution.py:162
  46.5 3.5 %all-to-all-start.1 = ((bf16[16,12,384]{2,1,0:T(8,128)(2,1)}), bf16[16,12,384]{2,1,0:T(8,128)(2,1)S(1)}, u32[]{:S(2)}, u32[]{:S(2)}) async-start(bf16[16,12,384]{2,1,0:T(8,128)(2,1)} %copy.75), calls=%async_computation.1 | async-start | bytes 393216 | tf_op jit(solution)/shard_map/all_to_all | solution.py:163
  50.1 1.0 %fusion.6 = f32[6,8192]{1,0:T(8,128)S(1)} fusion(f32[7,8192]{1,0:T(8,128)S(1)} %convert_element_type.145, f32[7,8192]{1,0:T(8,128)S(1)} %convert_element_type.144, f32[7,8192]{1,0:T(8,128)S(1)} %convert_element_type.143, f32[7,8192]{1,0:T(8,128)S(1)} %get-tuple-element.12, f32[6]{0:T(128)} %copy-done.3, f32[8192]{0:T(1024)} %bitcast.133, ...), kind=kLoop, calls=%fused_computation.14 | loop fusion | flops 589824 | bytes 1114232 | tf_op jit(solution)/shard_map/mul | solution.py:115
  51.0 8.1 %fusion.16 = f32[6,2048]{1,0:T(8,128)S(1)} fusion(bf16[4096,2048]{1,0:T(8,128)(2,1)} %param.17, f32[6,8192]{1,0:T(8,128)S(1)} %fusion.6), kind=kOutput, calls=%fused_computation.34 | convolution fusion | flops 100810752 | bytes 17022976 | tf_op jit(solution)/shard_map/dot_general | solution.py:174
  60.5 2.8 %fusion.60 = (bf16[6,2048]{1,0:T(8,128)(2,1)S(1)}, f32[6,2048]{1,0:T(8,128)S(1)}) fusion(f32[6,2048]{1,0:T(8,128)S(1)} %fusion.16, bf16[6,1024]{1,0:T(8,128)(2,1)S(1)} %bitcast.134, bf16[1024,2048]{1,0:T(8,128)(2,1)} %param.14), kind=kOutput, calls=%fused_computation.155 | convolution fusion | flops 25190400 | bytes 4329472 | tf_op jit(solution)/shard_map/dot_general | solution.py:183
  63.4 1.6 %collective-permute-start.5 = (bf16[6,2048]{1,0:T(8,128)(2,1)S(1)}, bf16[6,2048]{1,0:T(8,128)(2,1)S(1)}, u32[]{:S(2)}, u32[]{:S(2)}) collective-permute-start(bf16[6,2048]{1,0:T(8,128)(2,1)S(1)} %get-tuple-element.45), channel_id=1, source_target_pairs={{0,3},{1,2},{2,1},{3,0},{4,7},{5,6},{6,5},{7,4},{8,11},{9,10},{10,... | collective-permute-start | bytes 73736 | tf_op jit(solution)/shard_map/ppermute | solution.py:45
  65.9 0.8 %collective-permute-done.5 = bf16[6,2048]{1,0:T(8,128)(2,1)S(1)} collective-permute-done((bf16[6,2048]{1,0:T(8,128)(2,1)S(1)}, bf16[6,2048]{1,0:T(8,128)(2,1)S(1)}, u32[]{:S(2)}, u32[]{:S(2)}) %collective-permute-start.5) | collective-permute-done | bytes 24608 | tf_op jit(solution)/shard_map/ppermute | solution.py:45
  66.7 2.1 %collective-permute-done.4 = bf16[6,2048]{1,0:T(8,128)(2,1)S(1)} collective-permute-done((bf16[6,2048]{1,0:T(8,128)(2,1)S(1)}, bf16[6,2048]{1,0:T(8,128)(2,1)S(1)}, u32[]{:S(2)}, u32[]{:S(2)}) %collective-permute-start.4) | collective-permute-done | bytes 24608 | tf_op jit(solution)/shard_map/ppermute | solution.py:45
  (103 shorter events, 8.4 us)
Async XLA Ops:
  0.6 23.2 %copy-start = (bf16[2048,512]{1,0:T(8,128)(2,1)S(1)}, bf16[2048,512]{1,0:T(8,128)(2,1)}, u32[]{:S(2)}) copy-start(bf16[2048,512]{1,0:T(8,128)(2,1)} %param.13) | copy-start | bytes 6291460
  0.6 11.8 %copy-start.1 = (bf16[2048,4096]{1,0:T(8,128)(2,1)S(1)}, bf16[2048,4096]{1,0:T(8,128)(2,1)}, u32[]{:S(2)}) copy-start(bf16[2048,4096]{1,0:T(8,128)(2,1)} %param.15) | copy-start | bytes 50331652
  12.4 18.9 %copy-start.4 = (s32[3]{0:T(128)S(1)}, s32[3]{0:T(128)}, u32[]{:S(2)}) copy-start(s32[3]{0:T(128)} %param.19) | copy-start | bytes 40
  15.4 17.7 %collective-permute-start.1 = (bf16[7,8192]{1,0:T(8,128)(2,1)}, bf16[7,8192]{1,0:T(8,128)(2,1)S(1)}, u32[]{:S(2)}, u32[]{:S(2)}) collective-permute-start(bf16[7,8192]{1,0:T(8,128)(2,1)} %get-tuple-element.13), channel_id=1, source_target_pairs={{0,8},{4,12},{8,0},{12,4},{1,9},{5,13},{9,1},{13,5},{2,10},{6,14},... | collective-permute-start | bytes 344072 | tf_op jit(solution)/shard_map/ppermute | solution.py:45
  19.4 13.7 %collective-permute-start = (bf16[7,8192]{1,0:T(8,128)(2,1)}, bf16[7,8192]{1,0:T(8,128)(2,1)S(1)}, u32[]{:S(2)}, u32[]{:S(2)}) collective-permute-start(bf16[7,8192]{1,0:T(8,128)(2,1)} %get-tuple-element.13), channel_id=1, source_target_pairs={{0,4},{4,0},{8,12},{12,8},{1,5},{5,1},{9,13},{13,9},{2,6},{6,2},{1... | collective-permute-start | bytes 344072 | tf_op jit(solution)/shard_map/ppermute | solution.py:45
  21.0 12.8 %collective-permute-start.2 = (bf16[7,8192]{1,0:T(8,128)(2,1)}, bf16[7,8192]{1,0:T(8,128)(2,1)S(1)}, u32[]{:S(2)}, u32[]{:S(2)}) collective-permute-start(bf16[7,8192]{1,0:T(8,128)(2,1)} %get-tuple-element.13), channel_id=1, source_target_pairs={{0,12},{4,8},{8,4},{12,0},{1,13},{5,9},{9,5},{13,1},{2,14},{6,10},... | collective-permute-start | bytes 344072 | tf_op jit(solution)/shard_map/ppermute | solution.py:45
  25.1 14.6 %all-to-all-start = ((bf16[16,4,1280]{2,1,0:T(4,128)(2,1)}), bf16[16,4,1280]{2,1,0:T(4,128)(2,1)S(1)}, u32[]{:S(2)}, u32[]{:S(2)}) async-start(bf16[16,4,1280]{2,1,0:T(4,128)(2,1)} %bitcast.4), calls=%async_computation | async-start | bytes 327680 | tf_op jit(solution)/shard_map/all_to_all | solution.py:97
  40.2 0.6 copy-start.3
  45.6 23.2 %copy-start.2 = (bf16[6,2048]{1,0:T(8,128)(2,1)S(1)}, bf16[6,2048]{1,0:T(8,128)(2,1)}, u32[]{:S(2)}) copy-start(bf16[6,2048]{1,0:T(8,128)(2,1)} %param.10) | copy-start | bytes 73732
  46.5 12.6 %all-to-all-start.1 = ((bf16[16,12,384]{2,1,0:T(8,128)(2,1)}), bf16[16,12,384]{2,1,0:T(8,128)(2,1)S(1)}, u32[]{:S(2)}, u32[]{:S(2)}) async-start(bf16[16,12,384]{2,1,0:T(8,128)(2,1)} %copy.75), calls=%async_computation.1 | async-start | bytes 393216 | tf_op jit(solution)/shard_map/all_to_all | solution.py:163
  63.4 3.3 %collective-permute-start.5 = (bf16[6,2048]{1,0:T(8,128)(2,1)S(1)}, bf16[6,2048]{1,0:T(8,128)(2,1)S(1)}, u32[]{:S(2)}, u32[]{:S(2)}) collective-permute-start(bf16[6,2048]{1,0:T(8,128)(2,1)S(1)} %get-tuple-element.45), channel_id=1, source_target_pairs={{0,3},{1,2},{2,1},{3,0},{4,7},{5,6},{6,5},{7,4},{8,11},{9,10},{10,... | collective-permute-start | bytes 73736 | tf_op jit(solution)/shard_map/ppermute | solution.py:45
  64.9 3.9 %collective-permute-start.4 = (bf16[6,2048]{1,0:T(8,128)(2,1)S(1)}, bf16[6,2048]{1,0:T(8,128)(2,1)S(1)}, u32[]{:S(2)}, u32[]{:S(2)}) collective-permute-start(bf16[6,2048]{1,0:T(8,128)(2,1)S(1)} %get-tuple-element.45), channel_id=1, source_target_pairs={{0,2},{1,3},{2,0},{3,1},{4,6},{5,7},{6,4},{7,5},{8,10},{9,11},{10,... | collective-permute-start | bytes 73736 | tf_op jit(solution)/shard_map/ppermute | solution.py:45
  65.3 3.6 %collective-permute-start.3 = (bf16[6,2048]{1,0:T(8,128)(2,1)S(1)}, bf16[6,2048]{1,0:T(8,128)(2,1)S(1)}, u32[]{:S(2)}, u32[]{:S(2)}) collective-permute-start(bf16[6,2048]{1,0:T(8,128)(2,1)S(1)} %get-tuple-element.45), channel_id=1, source_target_pairs={{0,1},{1,0},{2,3},{3,2},{4,5},{5,4},{6,7},{7,6},{8,9},{9,8},{10,11... | collective-permute-start | bytes 73736 | tf_op jit(solution)/shard_map/ppermute | solution.py:45

commit v2 on v0

v2 whole, which is shorter than its diff:
```python
import functools

import jax
import jax.numpy as jnp
from jax import lax
from jax.experimental import pallas as pl
from jax.experimental.pallas import tpu as pltpu
from jax.sharding import PartitionSpec as P

epsilon = 1e-05
masked_fill = -1e30
rotary_base = 10000.0
PART = ("gx", "gy", "gz")
FEW = 8
F32 = jnp.float32
BF16 = jnp.bfloat16
VMEM = pl.BlockSpec(memory_space=pltpu.VMEM)
SMEM = pl.BlockSpec(memory_space=pltpu.SMEM)
ANY = pl.BlockSpec(memory_space=pl.ANY)


def angles(lengths, head_dim):
    middle = head_dim // 2
    spread = rotary_base ** (-jnp.arange(middle, dtype=F32) / middle)
    return lengths.astype(F32)[:, None] * spread[None, :]


def iota(shape, dim):
    return lax.broadcasted_iota(jnp.int32, shape, dim)


def thirds(values):
    high = values.astype(BF16).astype(F32)
    rest = values - high
    middle = rest.astype(BF16).astype(F32)
    return high, middle, rest - middle


def from_lanes(row, first, count):
    lane = iota(row.shape, 1)
    return jnp.sum(jnp.where((lane >= first) & (lane < first + count), row, 0.0), 1, keepdims=True)


def rotated_halves(values, cosine, sine):
    middle = values.shape[-1] // 2
    first, second = values[:, :middle], values[:, middle:]
    return jnp.concatenate(
        [first * cosine - second * sine, first * sine + second * cosine], 1
    )


def cost(flops, nbytes):
    return pl.CostEstimate(flops=flops, bytes_accessed=nbytes, transcendentals=0)


def params():
    return pltpu.CompilerParams(vmem_limit_bytes=24 * 2**20)


def first_kernel(dims, tokens, gain, q_hbm, kv_hbm, sent, lhs, rows, wq, wkv, q_sem, kv_sem):
    gx, gy, gz, seq_dev, pieces = dims
    depth = q_hbm.shape[0] // pieces
    kv_dev = wkv.shape[1]
    cols = gy * gz
    col = lax.axis_index("gy") * gz + lax.axis_index("gz")
    kv_own = kv_hbm
    if kv_hbm.shape[1] != kv_dev:
        kv_own = kv_hbm.at[:, pl.ds(pl.multiple_of(col * kv_dev, kv_dev), kv_dev)]
    kv_copy = pltpu.make_async_copy(kv_own, wkv, kv_sem)
    q_copies = []
    for piece in range(pieces):
        part = pl.ds(piece * depth, depth)
        copy = pltpu.make_async_copy(q_hbm.at[part], wq.at[part], q_sem.at[piece])
        copy.start()
        q_copies.append(copy)
    kv_copy.start()

    inputs = tokens[...].astype(F32)
    seqs, width = inputs.shape
    mean = jnp.sum(inputs, 1, keepdims=True) / width
    centred = inputs - mean
    square = jnp.sum(centred * centred, 1, keepdims=True)
    scaled = centred * gain[...]
    each = seq_dev + 1
    for a in range(gy):
        rows[a * each : a * each + seq_dev, :] = scaled[a * seq_dev : (a + 1) * seq_dev]
        rows[a * each + seq_dev : (a + 1) * each, :] = gain[...]
    lhs[...] = rows[...].astype(BF16)

    lanes = sent.shape[2] - wq.shape[1] - kv_dev
    lane = iota((seqs, lanes), 1)
    first = iota((seqs, lanes), 0) * 6
    marks = jnp.zeros((seqs, lanes), F32)
    for place, term in enumerate(thirds(mean) + thirds(square)):
        marks = jnp.where(lane == first + place, term, marks)
    marks = jnp.broadcast_to(jnp.sum(marks, 0, keepdims=True), (each, lanes))

    total = jnp.zeros((gy * each, wq.shape[1]), F32)
    for piece in range(pieces):
        part = slice(piece * depth, (piece + 1) * depth)
        q_copies[piece].wait()
        total += jnp.dot(lhs[:, part], wq[part, :], preferred_element_type=F32)
    kv_copy.wait()
    keyval = jnp.dot(lhs[...], wkv[...], preferred_element_type=F32)
    whole = jnp.concatenate([total, keyval], 1)
    for a in range(gy):
        piece = jnp.concatenate([whole[a * each : (a + 1) * each], marks], 1).astype(BF16)
        for i in range(gx):
            for b in range(gz):
                sent[(i * gy + a) * gz + b] = piece


def attention_kernel(dims, got, cache, lengths, tables, sent, new_kv, stats, qs, ks, vs):
    gx, gy, gz, seq_dev, q_dev, kv_dev, features = dims
    cols = gy * gz
    each = seq_dev + 1
    ctx_dev = cache.shape[1]
    head_dim = cache.shape[2] // 2
    heads_dev = q_dev // head_dim
    heads = heads_dev * cols
    width = q_dev + kv_dev
    row = lax.axis_index("gy")
    block = lax.axis_index("gx") * gz + lax.axis_index("gz")

    marks = [got[i * cols][:, width:].astype(F32)[:1] for i in range(gx)]
    lanes = marks[0].shape[1]

    def centre(count, sequence, valid):
        first = sequence * 6
        means, squares = [], 0.0
        for i in range(gx):
            mine = jnp.broadcast_to(marks[i], (count, lanes))
            means.append(jnp.where(valid, from_lanes(mine, first, 3), 0.0))
            squares += from_lanes(mine, first + 3, 3)
        center = sum(means) / gx
        shifts = [mean - center for mean in means]
        spread = squares / features + sum(s * s for s in shifts) / gx
        return shifts, jnp.where(valid, lax.rsqrt(spread + epsilon), 0.0)

    rows = gy * each
    place = iota((rows, 1), 0)
    shifts, inverse = centre(rows, place // each * seq_dev + place % each, place % each < seq_dev)
    for i in range(gx):
        stats[i] = jnp.broadcast_to(shifts[i], stats.shape[1:])
    stats[gx] = jnp.broadcast_to(inverse, stats.shape[1:])

    place = iota((each, 1), 0)
    shifts, inverse = centre(each, row * seq_dev + place, place < seq_dev)

    cosine, sine = tables[0], tables[1]
    keyval = []
    for c in range(cols):
        total = 0.0
        for i in range(gx):
            part = got[i * cols + c][:, :width].astype(F32)
            total += part + shifts[i] * part[seq_dev:]
        total = total * inverse
        keyval.append(total[:, q_dev:])
        query = total[:, :q_dev].astype(BF16).astype(F32)
        for h in range(heads_dev):
            turned = rotated_halves(query[:, h * head_dim : (h + 1) * head_dim], cosine, sine)
            head = c * heads_dev + h
            qs[head * each : (head + 1) * each, :] = turned
    keyval = jnp.concatenate(keyval, 1)
    fresh = jnp.concatenate(
        [rotated_halves(keyval[:, :head_dim], cosine, sine), keyval[:, head_dim:]], 1
    ).astype(BF16)
    new_kv[...] = fresh[:seq_dev]
    fresh = fresh.astype(F32)
    for head in range(heads):
        ks[head * each : (head + 1) * each, :] = fresh[:, :head_dim]
        vs[head * each : (head + 1) * each, :] = fresh[:, head_dim:]

    many = heads * each
    scale = head_dim ** (-0.5)
    queries = qs[...].astype(BF16)
    own = jnp.sum(queries.astype(F32) * ks[...], 1, keepdims=True) * scale
    place = iota((many, 1), 0) % each
    position = block * ctx_dev + iota((many, ctx_dev), 1)
    scores = jnp.full((many, ctx_dev), masked_fill, F32)
    for s in range(seq_dev):
        found = lax.dot_general(
            queries, cache[s, :, :head_dim], (((1,), (1,)), ((), ())), preferred_element_type=F32
        )
        live = (place == s) & (position < lengths[s])
        scores = jnp.where(live, found * scale, scores)
    top = jnp.maximum(jnp.max(scores, 1, keepdims=True), own)
    weights = jnp.where(scores > 0.5 * masked_fill, jnp.exp(scores - top), 0.0)
    own_weight = jnp.where(block == 0, jnp.exp(own - top), 0.0)
    denom = jnp.sum(weights, 1, keepdims=True) + own_weight
    numer = own_weight * vs[...]
    for s in range(seq_dev):
        mine = jnp.where(place == s, weights, 0.0).astype(BF16)
        numer += jnp.dot(mine, cache[s, :, head_dim:], preferred_element_type=F32)

    lane = iota((many, head_dim), 1)
    terms = jnp.zeros((many, head_dim), F32)
    for j, term in enumerate(thirds(top) + thirds(denom)):
        terms = jnp.where((lane == place * 6 + j) & (place < seq_dev), term, terms)
    spare = jnp.zeros((many, head_dim), F32)
    for step in range(1, each):
        spare += pltpu.roll(terms, step, 0)
    out = jnp.where(place == seq_dev, spare, numer)
    count = heads_dev * each
    for c in range(cols):
        piece = out[c * count : (c + 1) * count].astype(BF16)
        for i in range(gx):
            sent[i * cols + c] = piece


def hidden_kernel(gx, seq_dev, stats, *refs):
    parts, hidden = refs[:-1], refs[-1]
    rows, ff_dev = hidden.shape
    each = seq_dev + 1
    place = lax.axis_index("gx")
    slab = min(ff_dev, 1024)
    inverse = stats[gx][:, :1]
    shifts = [stats[place ^ step][:, :1] for step in range(gx)]
    for start in range(0, ff_dev, slab):
        sums = []
        for base in (start, ff_dev + start):
            total = 0.0
            for step in range(gx):
                part = parts[step][:, base : base + slab].astype(F32)
                total += part + shifts[step] * part[seq_dev : each]
            sums.append(total * inverse)
        gate, upward = sums
        hidden[:, start : start + slab] = (gate / (1.0 + jnp.exp(-gate)) * upward).astype(BF16)


def out_kernel(dims, got, out_weight, partial, total, share, att):
    gx, gy, gz, seq_dev = dims
    each = seq_dev + 1
    count, head_dim = got.shape[1:]
    heads_dev = count // each
    place = iota((count, 1), 0) % each
    lanes = min(128, head_dim)
    for a in range(gy):
        values, tops, denoms = [], [], []
        for i in range(gx):
            for b in range(gz):
                piece = got[(i * gy + a) * gz + b].astype(F32)
                spare = jnp.where(place == seq_dev, piece[:, :lanes], 0.0)
                marks = spare
                for step in range(1, each):
                    marks += pltpu.roll(spare, count - step, 0)
                values.append(piece)
                tops.append(from_lanes(marks, place * 6, 3))
                denoms.append(from_lanes(marks, place * 6 + 3, 3))
        top = functools.reduce(jnp.maximum, tops)
        numer, denom = 0.0, 0.0
        for value, mine, part in zip(values, tops, denoms):
            factor = jnp.exp(mine - top)
            numer += value * factor
            denom += part * factor
        ratio = jnp.where(place < seq_dev, numer / jnp.where(place < seq_dev, denom, 1.0), 0.0)
        for h in range(heads_dev):
            att[a * each : (a + 1) * each, h * head_dim : (h + 1) * head_dim] = ratio[
                h * each : (h + 1) * each
            ]
    result = partial[...] + jnp.dot(
        att[...].astype(BF16), out_weight[...], preferred_element_type=F32
    )
    for a in range(gy):
        total[a * seq_dev : (a + 1) * seq_dev, :] = result[a * each : a * each + seq_dev]
    share[...] = total[...].astype(BF16)


def from_others(values, axis):
    size = lax.axis_size(axis)
    return [
        lax.ppermute(values, axis, [(place, place ^ step) for place in range(size)])
        for step in range(1, size)
    ]


def body(
    tokens,
    norm_gain,
    q_weight,
    kv_weight,
    out_weight,
    gate_weight,
    up_weight,
    down_weight,
    kv_cache,
    lengths,
):
    gx, gy, gz = (lax.axis_size(axis) for axis in PART)
    cols = gy * gz
    seqs, width = tokens.shape
    seq_dev = lengths.shape[0]
    head_dim = kv_weight.shape[1] // 2
    q_dev = q_weight.shape[1]
    heads_dev = q_dev // head_dim
    kv_dev = kv_weight.shape[1] // cols
    ff_dev = gate_weight.shape[1]
    each = seq_dev + 1
    rows = gy * each
    many = heads_dev * cols * each
    lanes = -(-seqs * 6 // 128) * 128
    pieces = max(1, width // 256)

    kv_own = kv_weight
    if kv_dev % 128:
        col = lax.axis_index(("gy", "gz"))
        kv_own = lax.dynamic_slice_in_dim(kv_weight, col * kv_dev, kv_dev, 1)
    sent, lhs = pl.pallas_call(
        functools.partial(first_kernel, (gx, gy, gz, seq_dev, pieces)),
        out_shape=(
            jax.ShapeDtypeStruct((gx * cols, each, q_dev + kv_dev + lanes), BF16),
            jax.ShapeDtypeStruct((rows, width), BF16),
        ),
        in_specs=[VMEM, VMEM, ANY, ANY],
        out_specs=(VMEM, VMEM),
        scratch_shapes=[
            pltpu.VMEM((rows, width), F32),
            pltpu.VMEM((width, q_dev), BF16),
            pltpu.VMEM((width, kv_dev), BF16),
            pltpu.SemaphoreType.DMA((pieces,)),
            pltpu.SemaphoreType.DMA,
        ],
        compiler_params=params(),
        cost_estimate=cost(2 * rows * width * (q_dev + kv_dev), 2 * width * (q_dev + kv_dev)),
        name="norm_query",
    )(tokens, norm_gain[None, :], q_weight, kv_own)
    got = lax.all_to_all(sent, PART, split_axis=0, concat_axis=0, tiled=True)

    gate_part = jnp.dot(lhs, gate_weight, preferred_element_type=F32).astype(BF16)
    up_part = jnp.dot(lhs, up_weight, preferred_element_type=F32).astype(BF16)
    both = jnp.concatenate([gate_part, up_part], 1)
    if gx <= FEW:
        parts = [both] + from_others(both, "gx")
    else:
        gathered = lax.all_gather(both, "gx")
        here = lax.axis_index("gx")
        parts = [lax.dynamic_index_in_dim(gathered, here ^ step, 0, False) for step in range(gx)]

    angle = jnp.pad(angles(lengths, head_dim), ((0, 1), (0, 0)))
    tables = jnp.stack([jnp.cos(angle), jnp.sin(angle)])
    sent, new_kv, stats = pl.pallas_call(
        functools.partial(attention_kernel, (gx, gy, gz, seq_dev, q_dev, kv_dev, gx * width)),
        out_shape=(
            jax.ShapeDtypeStruct((gx * cols, heads_dev * each, head_dim), BF16),
            jax.ShapeDtypeStruct((seq_dev, 2 * head_dim), BF16),
            jax.ShapeDtypeStruct((gx + 1, rows, 128), F32),
        ),
        in_specs=[VMEM, VMEM, SMEM, VMEM],
        out_specs=(VMEM, VMEM, VMEM),
        scratch_shapes=[pltpu.VMEM((many, head_dim), F32)] * 3,
        compiler_params=params(),
        cost_estimate=cost(4 * many * head_dim * seq_dev * kv_cache.shape[1], 2 * kv_cache.size),
        name="attention",
    )(got, kv_cache, lengths, tables)
    got = lax.all_to_all(sent, PART, split_axis=0, concat_axis=0, tiled=True)

    hidden = pl.pallas_call(
        functools.partial(hidden_kernel, gx, seq_dev),
        out_shape=jax.ShapeDtypeStruct((rows, ff_dev), BF16),
        in_specs=[VMEM] * (gx + 1),
        out_specs=VMEM,
        compiler_params=params(),
        cost_estimate=cost(16 * rows * ff_dev, 4 * gx * rows * ff_dev),
        name="hidden",
    )(stats, *parts)
    partial = jnp.dot(hidden, down_weight, preferred_element_type=F32)

    total, share = pl.pallas_call(
        functools.partial(out_kernel, (gx, gy, gz, seq_dev)),
        out_shape=(
            jax.ShapeDtypeStruct((seqs, width), F32),
            jax.ShapeDtypeStruct((seqs, width), BF16),
        ),
        in_specs=[VMEM] * 3,
        out_specs=(VMEM, VMEM),
        scratch_shapes=[pltpu.VMEM((rows, q_dev), F32)],
        compiler_params=params(),
        cost_estimate=cost(2 * rows * q_dev * width, 2 * q_dev * width),
        name="out_projection",
    )(got, out_weight, partial)
    for other in from_others(share, ("gy", "gz")):
        total = total + other.astype(F32)
    mixed = (tokens.astype(F32) + total).astype(BF16)
    return (mixed, new_kv)


def solution(mesh):
    in_specs = (
        P("group", "gx"),
        P("gx"),
        P("gx", ("gy", "gz")),
        P("gx", None),
        P(("gy", "gz"), "gx"),
        P("gx", ("gy", "gz")),
        P("gx", ("gy", "gz")),
        P(("gy", "gz"), "gx"),
        P(("group", "gy"), ("gx", "gz"), None),
        P(("group", "gy")),
    )
    out_specs = (P("group", "gx"), P(("group", "gy"), None))
    return jax.shard_map(body, mesh=mesh, in_specs=in_specs, out_specs=out_specs, check_vma=False)
```

time: 138 us -> 63.2 us (0.46)
  blocking collectives: 85.6 us -> 0 us
  starting transfers between devices: 3.27 us -> 17.7 us
  between operations: 14.2 us -> 0.75 us
  waiting for transfers between devices: 3.28 us -> 11.9 us
  matrix products: 24.8 us -> 19.1 us
  Pallas kernels: 0 us -> 5.12 us
  local copies, waits for them, and re-layouts: 2.41 us -> 7.48 us
  other arithmetic: 3.69 us -> 0.75 us
    all_gather x4 -> x0, blocking collectives: 45.2 us -> none  [the longest x3 39.9 us: joined(): gathered = jax.tree.map(lambda a: lax.all_gather(a, axis), part)]
    psum x3 -> x0, blocking collectives: 40.4 us -> none  [the longest x1 16.3 us: body(): lax.psum((query_part, keyval_part, gate_part, up_part), 'gx')]
    ppermute x0 -> x6, starting transfers between devices: none -> 7.86 us  [from_others(): lax.ppermute(values, axis, [(place, place ^ step) for place in range(size)])]
    all_to_all x1 -> x2, starting transfers between devices: 3.24 us -> 9.79 us  [body(): got = lax.all_to_all(sent, PART, split_axis=0, concat_axis=0, tiled=True)]
    dot_general x9 -> x3, matrix products: 24.8 us -> 19.1 us  [the longest x1 8.79 us: body(): up_part = jnp.dot(lhs, up_weight, preferred_element_type=F32).astype(BF16)]
    pallas_call x0 -> x4, Pallas kernels: none -> 5.12 us  [the longest x1 2.23 us: body(): pl.pallas_call(functools.partial(first_kernel, (gx, gy, gz, seq_dev, piec...]
    unnamed x16 -> x18, local copies, waits for them, and re-layouts: 2.35 us -> 7.44 us
    all_to_all x1 -> x2, waiting for transfers between devices: 3.24 us -> 8.3 us  [body(): got = lax.all_to_all(sent, PART, split_axis=0, concat_axis=0, tiled=True)]
  transfers between devices with their start and end apart: 2 -> 8, of which waited for: 1 -> 3; matrix products, arithmetic and copies ran while one was open for 5% -> 13% of each run, Pallas kernels for 0% -> 3%
where the time goes in v2:
time: 63.2 us; the launch traced here: 62.7 us
  matrix products  19.1 us (30%)
  starting transfers between devices  17.7 us (28%)
  waiting for transfers between devices  11.9 us (19%)
  local copies, waits for them, and re-layouts  7.48 us (12%)
  Pallas kernels  5.12 us (8%)
  other arithmetic  0.75 us (1%)
  between operations  0.75 us (1%)
    all_to_all x2, starting transfers between devices, body(): got = lax.all_to_all(sent, PART, split_axis=0, concat_axis=0, tiled=True)  9.79 us
    dot_general x1, matrix products, body(): up_part = jnp.dot(lhs, up_weight, preferred_element_type=F32).astype(BF16)  8.79 us
    all_to_all x2, waiting for transfers between devices, body(): got = lax.all_to_all(sent, PART, split_axis=0, concat_axis=0, tiled=True)  8.3 us
    dot_general x1, matrix products, body(): partial = jnp.dot(hidden, down_weight, preferred_element_type=F32)  8.04 us
    ppermute x6, starting transfers between devices, from_others(): lax.ppermute(values, axis, [(place, place ^ step) for place in range(size)])  7.86 us
    unnamed x18, local copies, waits for them, and re-layouts  7.44 us
    ppermute x6, waiting for transfers between devices, from_others(): lax.ppermute(values, axis, [(place, place ^ step) for place in range(size)])  3.55 us
    dot_general x1, matrix products, body(): jnp.dot(lhs, gate_weight, preferred_element_type=F32).astype(BF16)  2.27 us
  transfers between devices with their start and end apart: 8, of which 3 were waited for; matrix products, arithmetic and copies ran while one was open for 13% of the time, Pallas kernels for 3%

profile of v2, /device:TPU:0, one launch (start us, length us, event | category | flops | bytes accessed | tf_op | source)
XLA Modules:
  0.0 62.7 jit_solution(5163471691034038219)
XLA Ops:
  0.6 2.2 %copy-done = bf16[2048,1024]{1,0:T(8,128)(2,1)S(1)} copy-done((bf16[2048,1024]{1,0:T(8,128)(2,1)S(1)}, bf16[2048,1024]{1,0:T(8,128)(2,1)}, u32[]{:S(2)}) %copy-start) | copy-done | bytes 4194328
  2.8 1.6 %copy-done.2 = bf16[2048,512]{1,0:T(8,128)(2,1)S(1)} copy-done((bf16[2048,512]{1,0:T(8,128)(2,1)S(1)}, bf16[2048,512]{1,0:T(8,128)(2,1)}, u32[]{:S(2)}) %copy-start.2) | copy-done | bytes 2097176
  4.4 0.8 %copy-done.4 = bf16[6,2048]{1,0:T(8,128)(2,1)S(1)} copy-done((bf16[6,2048]{1,0:T(8,128)(2,1)S(1)}, bf16[6,2048]{1,0:T(8,128)(2,1)}, u32[]{:S(2)}) %copy-start.4) | copy-done | bytes 24600
  5.2 0.7 %copy-done.6 = f32[2048]{0:T(1024)S(1)} copy-done((f32[2048]{0:T(1024)S(1)}, f32[2048]{0:T(1024)}, u32[]{:S(2)}) %copy-start.6) | copy-done | bytes 8216
  5.9 2.2 %norm_query.1 = (bf16[16,4,1280]{2,1,0:T(4,128)(2,1)}, bf16[8,2048]{1,0:T(8,128)(2,1)S(1)}) custom-call(bf16[6,2048]{1,0:T(8,128)(2,1)S(1)} %copy-done.4, f32[1,2048]{1,0:T(1,128)S(1)} %bitcast.11, bf16[2048,1024]{1,0:T(8,128)(2,1)S(1)} %copy-done, bf16[2048,512]{1,0:T(8,128)(2,1)S(1)} %copy-done.2), custom_call_target="tpu_custom_call" | custom-call | flops 37748736 | bytes 4718592 | tf_op jit(solution)/shard_map/norm_query/pallas_call | solution.py:308
  8.1 8.8 %convolution_convert_fusion = bf16[8,4096]{1,0:T(8,128)(2,1)S(1)} fusion(bf16[8,2048]{1,0:T(8,128)(2,1)S(1)} %get-tuple-element.12, bf16[2048,4096]{1,0:T(8,128)(2,1)} %param.16), kind=kOutput, calls=%fused_computation | convolution fusion | flops 134250496 | bytes 16875520 | tf_op jit(solution)/shard_map/dot_general | solution.py:330
  16.9 0.0 copy-start.3
  16.9 2.3 %convolution_convert_fusion.1 = bf16[8,4096]{1,0:T(8,128)(2,1)S(1)} fusion(bf16[8,2048]{1,0:T(8,128)(2,1)S(1)} %get-tuple-element.12, bf16[2048,4096]{1,0:T(8,128)(2,1)S(1)} %copy-done.8), kind=kOutput, calls=%fused_computation.1 | convolution fusion | flops 134250496 | bytes 16875520 | tf_op jit(solution)/shard_map/dot_general | solution.py:329
  19.2 5.1 %collective-permute-start.2 = (bf16[8,8192]{1,0:T(8,128)(2,1)S(1)}, bf16[8,8192]{1,0:T(8,128)(2,1)S(1)}, u32[]{:S(2)}, u32[]{:S(2)}) collective-permute-start(bf16[8,8192]{1,0:T(8,128)(2,1)S(1)} %pad_maximum_fusion.refs_0_), channel_id=1, source_target_pairs={{0,12},{4,8},{8,4},{12,0},{1,13},{5,9},{9,5},{13,1},{2,14},{6,10},... | collective-permute-start | bytes 393224 | tf_op jit(solution)/shard_map/ppermute | solution.py:272
  24.3 0.6 %collective-permute-start = (bf16[8,8192]{1,0:T(8,128)(2,1)S(1)}, bf16[8,8192]{1,0:T(8,128)(2,1)S(1)}, u32[]{:S(2)}, u32[]{:S(2)}) collective-permute-start(bf16[8,8192]{1,0:T(8,128)(2,1)S(1)} %pad_maximum_fusion.refs_0_), channel_id=1, source_target_pairs={{0,4},{4,0},{8,12},{12,8},{1,5},{5,1},{9,13},{13,9},{2,6},{6,2},{1... | collective-permute-start | bytes 393224 | tf_op jit(solution)/shard_map/ppermute | solution.py:272
  25.0 6.1 %all-to-all-start = ((bf16[16,4,1280]{2,1,0:T(4,128)(2,1)}), bf16[16,4,1280]{2,1,0:T(4,128)(2,1)S(1)}, u32[]{:S(2)}, u32[]{:S(2)}) async-start(bf16[16,4,1280]{2,1,0:T(4,128)(2,1)} %get-tuple-element.9), calls=%async_computation | async-start | bytes 327680 | tf_op jit(solution)/shard_map/all_to_all | solution.py:327
  31.1 0.1 broadcast_multiply_fusion
  31.2 8.3 %all-to-all-done.got = bf16[16,4,1280]{2,1,0:T(4,128)(2,1)S(1)} async-done(((bf16[16,4,1280]{2,1,0:T(4,128)(2,1)}), bf16[16,4,1280]{2,1,0:T(4,128)(2,1)S(1)}, u32[]{:S(2)}, u32[]{:S(2)}) %all-to-all-start) | async-done | bytes 163872 | tf_op jit(solution)/shard_map/all_to_all | solution.py:327
  39.5 1.8 %attention.1 = (bf16[16,16,256]{2,1,0:T(8,128)(2,1)}, bf16[3,512]{1,0:T(4,128)(2,1)}, f32[5,8,128]{2,1,0:T(8,128)S(1)}) custom-call(bf16[16,4,1280]{2,1,0:T(4,128)(2,1)S(1)} %all-to-all-done.got, bf16[3,256,512]{2,1,0:T(8,128)(2,1)S(1)} %copy-done.3, s32[3]{0:T(128)S(1)} %copy-done.7, f32[2,4,128]{2,1,0:T(4,128)S(1)} %pad_maximum_fusion.1.tables), custom_call_target="tpu_custom_call" | custom-call | flops 50331648 | bytes 786432 | tf_op jit(solution)/shard_map/attention/pallas_call | solution.py:341
  41.3 3.7 %all-to-all-start.1 = ((bf16[16,16,256]{2,1,0:T(8,128)(2,1)}), bf16[16,16,256]{2,1,0:T(8,128)(2,1)S(1)}, u32[]{:S(2)}, u32[]{:S(2)}) async-start(bf16[16,16,256]{2,1,0:T(8,128)(2,1)} %get-tuple-element.10), calls=%async_computation.1 | async-start | bytes 262144 | tf_op jit(solution)/shard_map/all_to_all | solution.py:355
  45.1 0.3 hidden.1
  45.4 8.0 %fusion.partial = f32[8,2048]{1,0:T(8,128)S(1)} fusion(bf16[8,4096]{1,0:T(8,128)(2,1)S(1)} %hidden.1, bf16[4096,2048]{1,0:T(8,128)(2,1)} %param.17), kind=kOutput, calls=%fused_computation.9 | convolution fusion | flops 134217728 | bytes 16908288 | tf_op jit(solution)/shard_map/dot_general | solution.py:366
  53.4 2.2 %copy-done.1 = bf16[1024,2048]{1,0:T(8,128)(2,1)S(1)} copy-done((bf16[1024,2048]{1,0:T(8,128)(2,1)S(1)}, bf16[1024,2048]{1,0:T(8,128)(2,1)}, u32[]{:S(2)}) %copy-start.1) | copy-done | bytes 4194328
  55.6 0.8 %out_projection.1 = (f32[6,2048]{1,0:T(8,128)S(1)}, bf16[6,2048]{1,0:T(8,128)(2,1)S(1)}) custom-call(bf16[16,16,256]{2,1,0:T(8,128)(2,1)S(1)} %all-to-all-done.1.got, bf16[1024,2048]{1,0:T(8,128)(2,1)S(1)} %copy-done.1, f32[8,2048]{1,0:T(8,128)S(1)} %fusion.partial), custom_call_target="tpu_custom_call" | custom-call | flops 33554432 | bytes 4194304 | tf_op jit(solution)/shard_map/out_projection/pallas_call | solution.py:368
  56.4 1.7 %collective-permute-start.5 = (bf16[6,2048]{1,0:T(8,128)(2,1)S(1)}, bf16[6,2048]{1,0:T(8,128)(2,1)S(1)}, u32[]{:S(2)}, u32[]{:S(2)}) collective-permute-start(bf16[6,2048]{1,0:T(8,128)(2,1)S(1)} %get-tuple-element.14), channel_id=1, source_target_pairs={{0,3},{1,2},{2,1},{3,0},{4,7},{5,6},{6,5},{7,4},{8,11},{9,10},{10,... | collective-permute-start | bytes 73736 | tf_op jit(solution)/shard_map/ppermute | solution.py:272
  58.1 0.4 collective-permute-start.4
  58.5 1.4 %collective-permute-done.5 = bf16[6,2048]{1,0:T(8,128)(2,1)S(1)} collective-permute-done((bf16[6,2048]{1,0:T(8,128)(2,1)S(1)}, bf16[6,2048]{1,0:T(8,128)(2,1)S(1)}, u32[]{:S(2)}, u32[]{:S(2)}) %collective-permute-start.5) | collective-permute-done | bytes 24608 | tf_op jit(solution)/shard_map/ppermute | solution.py:272
  59.9 2.1 %collective-permute-done.4 = bf16[6,2048]{1,0:T(8,128)(2,1)S(1)} collective-permute-done((bf16[6,2048]{1,0:T(8,128)(2,1)S(1)}, bf16[6,2048]{1,0:T(8,128)(2,1)S(1)}, u32[]{:S(2)}, u32[]{:S(2)}) %collective-permute-start.4) | collective-permute-done | bytes 24608 | tf_op jit(solution)/shard_map/ppermute | solution.py:272
  62.1 0.6 %add_convert_fusion = bf16[6,2048]{1,0:T(8,128)(2,1)} fusion(bf16[6,2048]{1,0:T(8,128)(2,1)S(1)} %collective-permute-done.5, bf16[6,2048]{1,0:T(8,128)(2,1)S(1)} %collective-permute-done.4, f32[6,2048]{1,0:T(8,128)S(1)} %get-tuple-element.13, bf16[6,2048]{1,0:T(8,128)(2,1)S(1)} %collective-permute-done.3, bf16[6,2048]{1,0:T(8,128)(2,1)S(1)} %copy-done.5), kind=kLoop, calls=%fused_computation.3 | loop fusion | flops 110592 | bytes 172032 | tf_op jit(solution)/shard_map/convert_element_type | solution.py:383
  (24 shorter events, 0.1 us)
Async XLA Ops:
  0.6 2.2 %copy-start = (bf16[2048,1024]{1,0:T(8,128)(2,1)S(1)}, bf16[2048,1024]{1,0:T(8,128)(2,1)}, u32[]{:S(2)}) copy-start(bf16[2048,1024]{1,0:T(8,128)(2,1)} %q_hbm.1) | copy-start | bytes 12582916
  2.8 1.6 %copy-start.2 = (bf16[2048,512]{1,0:T(8,128)(2,1)S(1)}, bf16[2048,512]{1,0:T(8,128)(2,1)}, u32[]{:S(2)}) copy-start(bf16[2048,512]{1,0:T(8,128)(2,1)} %kv_hbm.1) | copy-start | bytes 6291460
  4.4 0.8 %copy-start.4 = (bf16[6,2048]{1,0:T(8,128)(2,1)S(1)}, bf16[6,2048]{1,0:T(8,128)(2,1)}, u32[]{:S(2)}) copy-start(bf16[6,2048]{1,0:T(8,128)(2,1)} %tokens.1) | copy-start | bytes 73732
  5.2 0.7 %copy-start.6 = (f32[2048]{0:T(1024)S(1)}, f32[2048]{0:T(1024)}, u32[]{:S(2)}) copy-start(f32[2048]{0:T(1024)} %param.11) | copy-start | bytes 24580
  5.9 11.0 %copy-start.8 = (bf16[2048,4096]{1,0:T(8,128)(2,1)S(1)}, bf16[2048,4096]{1,0:T(8,128)(2,1)}, u32[]{:S(2)}) copy-start(bf16[2048,4096]{1,0:T(8,128)(2,1)} %param.15) | copy-start | bytes 50331652
  16.9 14.1 %copy-start.7 = (s32[3]{0:T(128)S(1)}, s32[3]{0:T(128)}, u32[]{:S(2)}) copy-start(s32[3]{0:T(128)} %lengths.1) | copy-start | bytes 40
  16.9 22.6 %copy-start.3 = (bf16[3,256,512]{2,1,0:T(8,128)(2,1)S(1)}, bf16[3,256,512]{2,1,0:T(8,128)(2,1)}, u32[]{:S(2)}) copy-start(bf16[3,256,512]{2,1,0:T(8,128)(2,1)} %cache.1) | copy-start | bytes 2359300
  19.2 42.9 %copy-start.5 = (bf16[6,2048]{1,0:T(8,128)(2,1)S(1)}, bf16[6,2048]{1,0:T(8,128)(2,1)}, u32[]{:S(2)}) copy-start(bf16[6,2048]{1,0:T(8,128)(2,1)} %tokens.1) | copy-start | bytes 73732
  19.2 25.9 %collective-permute-start.2 = (bf16[8,8192]{1,0:T(8,128)(2,1)S(1)}, bf16[8,8192]{1,0:T(8,128)(2,1)S(1)}, u32[]{:S(2)}, u32[]{:S(2)}) collective-permute-start(bf16[8,8192]{1,0:T(8,128)(2,1)S(1)} %pad_maximum_fusion.refs_0_), channel_id=1, source_target_pairs={{0,12},{4,8},{8,4},{12,0},{1,13},{5,9},{9,5},{13,1},{2,14},{6,10},... | collective-permute-start | bytes 393224 | tf_op jit(solution)/shard_map/ppermute | solution.py:272
  24.3 20.7 %collective-permute-start.1 = (bf16[8,8192]{1,0:T(8,128)(2,1)S(1)}, bf16[8,8192]{1,0:T(8,128)(2,1)S(1)}, u32[]{:S(2)}, u32[]{:S(2)}) collective-permute-start(bf16[8,8192]{1,0:T(8,128)(2,1)S(1)} %pad_maximum_fusion.refs_0_), channel_id=1, source_target_pairs={{0,8},{4,12},{8,0},{12,4},{1,9},{5,13},{9,1},{13,5},{2,10},{6,14},... | collective-permute-start | bytes 393224 | tf_op jit(solution)/shard_map/ppermute | solution.py:272
  24.3 20.8 %collective-permute-start = (bf16[8,8192]{1,0:T(8,128)(2,1)S(1)}, bf16[8,8192]{1,0:T(8,128)(2,1)S(1)}, u32[]{:S(2)}, u32[]{:S(2)}) collective-permute-start(bf16[8,8192]{1,0:T(8,128)(2,1)S(1)} %pad_maximum_fusion.refs_0_), channel_id=1, source_target_pairs={{0,4},{4,0},{8,12},{12,8},{1,5},{5,1},{9,13},{13,9},{2,6},{6,2},{1... | collective-permute-start | bytes 393224 | tf_op jit(solution)/shard_map/ppermute | solution.py:272
  25.0 14.5 %all-to-all-start = ((bf16[16,4,1280]{2,1,0:T(4,128)(2,1)}), bf16[16,4,1280]{2,1,0:T(4,128)(2,1)S(1)}, u32[]{:S(2)}, u32[]{:S(2)}) async-start(bf16[16,4,1280]{2,1,0:T(4,128)(2,1)} %get-tuple-element.9), calls=%async_computation | async-start | bytes 327680 | tf_op jit(solution)/shard_map/all_to_all | solution.py:327
  41.3 12.1 %all-to-all-start.1 = ((bf16[16,16,256]{2,1,0:T(8,128)(2,1)}), bf16[16,16,256]{2,1,0:T(8,128)(2,1)S(1)}, u32[]{:S(2)}, u32[]{:S(2)}) async-start(bf16[16,16,256]{2,1,0:T(8,128)(2,1)} %get-tuple-element.10), calls=%async_computation.1 | async-start | bytes 262144 | tf_op jit(solution)/shard_map/all_to_all | solution.py:355
  53.4 2.2 %copy-start.1 = (bf16[1024,2048]{1,0:T(8,128)(2,1)S(1)}, bf16[1024,2048]{1,0:T(8,128)(2,1)}, u32[]{:S(2)}) copy-start(bf16[1024,2048]{1,0:T(8,128)(2,1)} %out_weight.1) | copy-start | bytes 12582916
  56.4 3.5 %collective-permute-start.5 = (bf16[6,2048]{1,0:T(8,128)(2,1)S(1)}, bf16[6,2048]{1,0:T(8,128)(2,1)S(1)}, u32[]{:S(2)}, u32[]{:S(2)}) collective-permute-start(bf16[6,2048]{1,0:T(8,128)(2,1)S(1)} %get-tuple-element.14), channel_id=1, source_target_pairs={{0,3},{1,2},{2,1},{3,0},{4,7},{5,6},{6,5},{7,4},{8,11},{9,10},{10,... | collective-permute-start | bytes 73736 | tf_op jit(solution)/shard_map/ppermute | solution.py:272
  58.1 3.9 %collective-permute-start.4 = (bf16[6,2048]{1,0:T(8,128)(2,1)S(1)}, bf16[6,2048]{1,0:T(8,128)(2,1)S(1)}, u32[]{:S(2)}, u32[]{:S(2)}) collective-permute-start(bf16[6,2048]{1,0:T(8,128)(2,1)S(1)} %get-tuple-element.14), channel_id=1, source_target_pairs={{0,2},{1,3},{2,0},{3,1},{4,6},{5,7},{6,4},{7,5},{8,10},{9,11},{10,... | collective-permute-start | bytes 73736 | tf_op jit(solution)/shard_map/ppermute | solution.py:272
  58.5 3.5 %collective-permute-start.3 = (bf16[6,2048]{1,0:T(8,128)(2,1)S(1)}, bf16[6,2048]{1,0:T(8,128)(2,1)S(1)}, u32[]{:S(2)}, u32[]{:S(2)}) collective-permute-start(bf16[6,2048]{1,0:T(8,128)(2,1)S(1)} %get-tuple-element.14), channel_id=1, source_target_pairs={{0,1},{1,0},{2,3},{3,2},{4,5},{5,4},{6,7},{7,6},{8,9},{9,8},{10,11... | collective-permute-start | bytes 73736 | tf_op jit(solution)/shard_map/ppermute | solution.py:272

commit v3 on v2

v3 whole, which is shorter than its diff:
```python
import functools

import jax
import jax.numpy as jnp
from jax import lax
from jax.experimental import pallas as pl
from jax.experimental.pallas import tpu as pltpu
from jax.sharding import PartitionSpec as P

epsilon = 1e-05
masked_fill = -1e30
rotary_base = 10000.0
PART = ("gx", "gy", "gz")
FEW = 8
LIMIT = 3
F32 = jnp.float32
BF16 = jnp.bfloat16
VMEM = pl.BlockSpec(memory_space=pltpu.VMEM)
SMEM = pl.BlockSpec(memory_space=pltpu.SMEM)
ANY = pl.BlockSpec(memory_space=pl.ANY)
HBM = pl.BlockSpec(memory_space=pltpu.HBM)
MIB = 2**20


def iota(shape, dim):
    return lax.broadcasted_iota(jnp.int32, shape, dim)


def thirds(values):
    high = values.astype(BF16).astype(F32)
    rest = values - high
    middle = rest.astype(BF16).astype(F32)
    return high, middle, rest - middle


def from_lanes(row, first, count):
    lane = iota(row.shape, 1)
    return jnp.sum(jnp.where((lane >= first) & (lane < first + count), row, 0.0), 1, keepdims=True)


def rotated_halves(values, cosine, sine):
    middle = values.shape[-1] // 2
    first, second = values[:, :middle], values[:, middle:]
    return jnp.concatenate(
        [first * cosine - second * sine, first * sine + second * cosine], 1
    )


def cost(flops, nbytes):
    return pl.CostEstimate(flops=int(flops), bytes_accessed=int(nbytes), transcendentals=0)


def params(mebibytes):
    return pltpu.CompilerParams(vmem_limit_bytes=mebibytes * MIB)


def exponent_kernel(table):
    table[...] = iota(table.shape, 1).astype(F32) / -table.shape[1]


def first_kernel(dims, tokens, gain, q_weight, kv_weight, after, sums, lhs, rows):
    gy, gz, seq_dev, kv_dev = dims
    inputs = tokens[...].astype(F32)
    seqs, width = inputs.shape
    mean = jnp.sum(inputs, 1, keepdims=True) / width
    centred = inputs - mean
    square = jnp.sum(centred * centred, 1, keepdims=True)
    scaled = centred * gain[...]
    each = seq_dev + 1
    for a in range(gy):
        rows[a * each : a * each + seq_dev, :] = scaled[a * seq_dev : (a + 1) * seq_dev]
        rows[a * each + seq_dev : (a + 1) * each, :] = gain[...]
    lhs[...] = rows[...].astype(BF16)

    lanes = sums.shape[1] - q_weight.shape[1] - kv_dev
    lane = iota((seqs, lanes), 1)
    first = iota((seqs, lanes), 0) * 6
    marks = jnp.zeros((seqs, lanes), F32)
    for place, term in enumerate(thirds(mean) + thirds(square)):
        marks = jnp.where(lane == first + place, term, marks)
    marks = jnp.broadcast_to(jnp.sum(marks, 0, keepdims=True), (gy * each, lanes))

    values = lhs[...]
    query = jnp.dot(values, q_weight[...], preferred_element_type=F32)
    kv_own = kv_weight[...]
    if kv_weight.shape[1] != kv_dev:
        col = lax.axis_index("gy") * gz + lax.axis_index("gz")
        kv_own = kv_weight[:, pl.ds(pl.multiple_of(col * kv_dev, kv_dev), kv_dev)]
    keyval = jnp.dot(values, kv_own, preferred_element_type=F32)
    sums[...] = jnp.concatenate([query, keyval, marks], 1).astype(BF16)


def sum_kernel(dims, *refs):
    gx, gy, seq_dev, width, features = dims
    parts, (whole, stats) = refs[:gx], refs[gx:]
    each = seq_dev + 1
    rows = gy * each
    place = iota((rows, 1), 0)
    valid = place % each < seq_dev
    first = (place // each * seq_dev + place % each) * 6
    means, squares = [], 0.0
    for part in parts:
        marks = part[:, width:].astype(F32)
        means.append(jnp.where(valid, from_lanes(marks, first, 3), 0.0))
        squares += from_lanes(marks, first + 3, 3)
    center = sum(means) / gx
    shifts = [mean - center for mean in means]
    spread = squares / features + sum(s * s for s in shifts) / gx
    inverse = jnp.where(valid, lax.rsqrt(spread + epsilon), 0.0)
    for step in range(gx):
        stats[step] = jnp.broadcast_to(shifts[step], stats.shape[1:])
    stats[gx] = jnp.broadcast_to(inverse, stats.shape[1:])
    whole[...] = (shifted_sum([p[:, :width] for p in parts], shifts, seq_dev) * inverse).astype(BF16)


def shifted_sum(parts, shifts, seq_dev):
    total = 0.0
    for part, shift in zip(parts, shifts):
        part = part.astype(F32)
        total += part + shift * part[seq_dev : seq_dev + 1]
    return total


def product(lhs, weight, store, slab=512):
    slab = min(slab, weight.shape[1])

    def step(index, _):
        part = pl.ds(pl.multiple_of(index * slab, slab), slab)
        store(part, jnp.dot(lhs, weight[:, part], preferred_element_type=F32))
        return 0

    lax.fori_loop(0, weight.shape[1] // slab, step, 0)


def partial_kernel(lhs, weight, *refs):
    sums = refs[-1]
    def store(part, value):
        sums[:, part] = value.astype(BF16)

    product(lhs[...], weight, store)


def attention_kernel(dims, *refs):
    gy, gz, seq_dev, q_dev, kv_dev = dims
    cols = gy * gz
    parts, (cache, lengths, tables, after) = refs[:cols], refs[cols : cols + 4]
    pieces, (new_kv, qs, ks, vs, kvs) = refs[cols + 4 : 2 * cols + 4], refs[2 * cols + 4 :]
    each = seq_dev + 1
    ctx_dev = cache.shape[1]
    head_dim = cache.shape[2] // 2
    heads_dev = q_dev // head_dim
    heads = heads_dev * cols
    row = lax.axis_index("gy")
    col = row * gz + lax.axis_index("gz")
    block = lax.axis_index("gx") * gz + lax.axis_index("gz")

    cosine, sine = tables[0], tables[1]
    for step in range(cols):
        part = parts[step][...].astype(F32)
        mine = part[:each]
        for a in range(1, gy):
            mine = jnp.where(row == a, part[a * each : (a + 1) * each], mine)
        kvs[step] = mine[:, q_dev:]
        for h in range(heads_dev):
            turned = rotated_halves(mine[:, h * head_dim : (h + 1) * head_dim], cosine, sine)
            head = step * heads_dev + h
            qs[head * each : (head + 1) * each, :] = turned
    keyval = jnp.concatenate([kvs[col ^ c] for c in range(cols)], 1)
    fresh = jnp.concatenate(
        [rotated_halves(keyval[:, :head_dim], cosine, sine), keyval[:, head_dim:]], 1
    ).astype(BF16)
    new_kv[...] = fresh[:seq_dev]
    fresh = fresh.astype(F32)
    for head in range(heads):
        ks[head * each : (head + 1) * each, :] = fresh[:, :head_dim]
        vs[head * each : (head + 1) * each, :] = fresh[:, head_dim:]

    many = heads * each
    scale = head_dim ** (-0.5)
    queries = qs[...].astype(BF16)
    own = jnp.sum(queries.astype(F32) * ks[...], 1, keepdims=True) * scale
    place = iota((many, 1), 0) % each
    position = block * ctx_dev + iota((many, ctx_dev), 1)
    scores = jnp.full((many, ctx_dev), masked_fill, F32)
    for s in range(seq_dev):
        found = lax.dot_general(
            queries, cache[s, :, :head_dim], (((1,), (1,)), ((), ())), preferred_element_type=F32
        )
        live = (place == s) & (position < lengths[s])
        scores = jnp.where(live, found * scale, scores)
    top = jnp.maximum(jnp.max(scores, 1, keepdims=True), own)
    weights = jnp.where(scores > 0.5 * masked_fill, jnp.exp(scores - top), 0.0)
    own_weight = jnp.where(block == 0, jnp.exp(own - top), 0.0)
    denom = jnp.sum(weights, 1, keepdims=True) + own_weight
    numer = own_weight * vs[...]
    for s in range(seq_dev):
        mine = jnp.where(place == s, weights, 0.0).astype(BF16)
        numer += jnp.dot(mine, cache[s, :, head_dim:], preferred_element_type=F32)

    lane = iota((many, head_dim), 1)
    terms = jnp.zeros((many, head_dim), F32)
    for j, term in enumerate(thirds(top) + thirds(denom)):
        terms = jnp.where((lane == place * 6 + j) & (place < seq_dev), term, terms)
    spare = jnp.zeros((many, head_dim), F32)
    for step in range(1, each):
        spare += pltpu.roll(terms, step, 0)
    out = jnp.where(place == seq_dev, spare, numer)
    count = heads_dev * each
    for step in range(cols):
        pieces[step][...] = out[step * count : (step + 1) * count].astype(BF16)


def down_kernel(dims, stats, *refs):
    gx, seq_dev = dims
    parts, (down, result, hidden) = refs[:gx], refs[gx:]
    rows, ff_dev = hidden.shape
    slab = min(ff_dev, 1024)
    inverse = stats[gx][:, :1]
    shifts = [stats[step][:, :1] for step in range(gx)]
    for start in range(0, ff_dev, slab):
        sums = []
        for base in (0, rows):
            found = [part[base : base + rows, start : start + slab] for part in parts]
            sums.append(shifted_sum(found, shifts, seq_dev) * inverse)
        gate, upward = sums
        hidden[:, start : start + slab] = (gate / (1.0 + jnp.exp(-gate)) * upward).astype(BF16)

    def store(part, value):
        result[:, part] = value

    product(hidden[...], down, store)


def out_kernel(dims, *refs):
    gx, gy, gz, seq_dev = dims
    parts, (out_weight, partial, total, share, turned, att) = refs[:gx], refs[gx:]
    each = seq_dev + 1
    count, head_dim = parts[0].shape[1:]
    heads_dev = count // each
    place = iota((count, 1), 0) % each
    lanes = min(128, head_dim)
    row = lax.axis_index("gy")
    for a in range(gy):
        values, tops, denoms = [], [], []
        for part in parts:
            for b in range(gz):
                piece = part[a * gz + b].astype(F32)
                spare = jnp.where(place == seq_dev, piece[:, :lanes], 0.0)
                marks = spare
                for step in range(1, each):
                    marks += pltpu.roll(spare, count - step, 0)
                values.append(piece)
                tops.append(from_lanes(marks, place * 6, 3))
                denoms.append(from_lanes(marks, place * 6 + 3, 3))
        top = functools.reduce(jnp.maximum, tops)
        numer, denom = 0.0, 0.0
        for value, mine, part in zip(values, tops, denoms):
            factor = jnp.exp(mine - top)
            numer += value * factor
            denom += part * factor
        ratio = jnp.where(place < seq_dev, numer / jnp.where(place < seq_dev, denom, 1.0), 0.0)
        for h in range(heads_dev):
            turned[row ^ a, :, h * head_dim : (h + 1) * head_dim] = ratio[
                h * each : (h + 1) * each
            ]
    for a in range(gy):
        att[a * each : (a + 1) * each, :] = turned[a]
    result = partial[...] + jnp.dot(
        att[...].astype(BF16), out_weight[...], preferred_element_type=F32
    )
    for a in range(gy):
        total[a * seq_dev : (a + 1) * seq_dev, :] = result[a * each : a * each + seq_dev]
    share[...] = total[...].astype(BF16)


def with_others(values, axis):
    size = lax.axis_size(axis)
    if size <= FEW:
        return [values] + [
            lax.ppermute(values, axis, [(place, place ^ step) for place in range(size)])
            for step in range(1, size)
        ]
    gathered = lax.all_gather(values, axis)
    here = lax.axis_index(axis)
    return [lax.dynamic_index_in_dim(gathered, here ^ step, 0, False) for step in range(size)]


def body(
    tokens,
    norm_gain,
    q_weight,
    kv_weight,
    out_weight,
    gate_weight,
    up_weight,
    down_weight,
    kv_cache,
    lengths,
):
    gx, gy, gz = (lax.axis_size(axis) for axis in PART)
    cols = gy * gz
    seqs, width = tokens.shape
    seq_dev = lengths.shape[0]
    head_dim = kv_weight.shape[1] // 2
    q_dev = q_weight.shape[1]
    heads_dev = q_dev // head_dim
    kv_dev = kv_weight.shape[1] // cols
    ff_dev = gate_weight.shape[1]
    each = seq_dev + 1
    rows = gy * each
    many = heads_dev * cols * each
    lanes = -(-seqs * 6 // 128) * 128

    kv_own = kv_weight
    if kv_dev % 128:
        col = lax.axis_index(("gy", "gz"))
        kv_own = lax.dynamic_slice_in_dim(kv_weight, col * kv_dev, kv_dev, 1)
    exponents = pl.pallas_call(
        exponent_kernel,
        out_shape=jax.ShapeDtypeStruct((1, head_dim // 2), F32),
        out_specs=VMEM,
        compiler_params=params(LIMIT),
        cost_estimate=cost(7e9, 0),
        name="exponents",
    )()
    sums, lhs = pl.pallas_call(
        functools.partial(first_kernel, (gy, gz, seq_dev, kv_dev)),
        out_shape=(
            jax.ShapeDtypeStruct((rows, q_dev + kv_dev + lanes), BF16),
            jax.ShapeDtypeStruct((rows, width), BF16),
        ),
        in_specs=[VMEM] * 4 + [ANY],
        out_specs=(VMEM, VMEM),
        scratch_shapes=[pltpu.VMEM((rows, width), F32)],
        compiler_params=params(LIMIT),
        cost_estimate=cost(7e9, 0),
        name="norm_query",
    )(tokens, norm_gain[None, :], q_weight, kv_own, exponents)
    sums = with_others(sums, "gx")
    query, stats = pl.pallas_call(
        functools.partial(sum_kernel, (gx, gy, seq_dev, q_dev + kv_dev, gx * width)),
        out_shape=(
            jax.ShapeDtypeStruct((rows, q_dev + kv_dev), BF16),
            jax.ShapeDtypeStruct((gx + 1, rows, 128), F32),
        ),
        in_specs=[VMEM] * gx,
        out_specs=(VMEM, VMEM),
        compiler_params=params(LIMIT),
        name="query_sum",
    )(*sums)
    queries = with_others(query, ("gy", "gz"))

    def partial_sums(weight, name, *after):
        return pl.pallas_call(
            partial_kernel,
            out_shape=jax.ShapeDtypeStruct((rows, ff_dev), BF16),
            in_specs=[VMEM, VMEM] + [ANY] * len(after),
            out_specs=VMEM,
            compiler_params=params(LIMIT),
            cost_estimate=cost(6e9, 16.8e6),
            name=name,
        )(lhs, weight, *after)

    gate = partial_sums(gate_weight, "gate")
    both = jnp.concatenate([gate, partial_sums(up_weight, "up", query)], 0)
    parts = with_others(both, "gx")

    angle = lengths.astype(F32)[:, None] * rotary_base**exponents
    angle = jnp.pad(angle, ((0, 1), (0, 0)))
    tables = jnp.stack([jnp.cos(angle), jnp.sin(angle)])
    piece = jax.ShapeDtypeStruct((heads_dev * each, head_dim), BF16)
    *pieces, new_kv = pl.pallas_call(
        functools.partial(attention_kernel, (gy, gz, seq_dev, q_dev, kv_dev)),
        out_shape=(piece,) * cols + (jax.ShapeDtypeStruct((seq_dev, 2 * head_dim), BF16),),
        in_specs=[VMEM] * (cols + 1) + [SMEM, VMEM, ANY],
        out_specs=(VMEM,) * (cols + 1),
        scratch_shapes=[pltpu.VMEM((many, head_dim), F32)] * 3
        + [pltpu.VMEM((cols, each, kv_dev), F32)],
        compiler_params=params(LIMIT),
        cost_estimate=cost(7e9, 2e6),
        name="attention",
    )(*queries, kv_cache, lengths, tables, both)
    pieces = pieces[:1] + [
        lax.ppermute(pieces[step], ("gy", "gz"), [(place, place ^ step) for place in range(cols)])
        for step in range(1, cols)
    ]
    pieces = with_others(jnp.stack(pieces), "gx")

    partial = pl.pallas_call(
        functools.partial(down_kernel, (gx, seq_dev)),
        out_shape=jax.ShapeDtypeStruct((rows, width), F32),
        in_specs=[VMEM] * (gx + 2),
        out_specs=VMEM,
        scratch_shapes=[pltpu.VMEM((rows, ff_dev), BF16)],
        compiler_params=params(LIMIT),
        cost_estimate=cost(4e9, 16.8e6),
        name="hidden_down",
    )(stats, *parts, down_weight)
    total, share = pl.pallas_call(
        functools.partial(out_kernel, (gx, gy, gz, seq_dev)),
        out_shape=(
            jax.ShapeDtypeStruct((seqs, width), F32),
            jax.ShapeDtypeStruct((seqs, width), BF16),
        ),
        in_specs=[VMEM] * (gx + 2),
        out_specs=(VMEM, VMEM),
        scratch_shapes=[pltpu.VMEM((gy, each, q_dev), F32), pltpu.VMEM((rows, q_dev), F32)],
        compiler_params=params(LIMIT),
        cost_estimate=cost(1e9, 4e6),
        name="out_projection",
    )(*pieces, out_weight, partial)
    for other in with_others(share, ("gy", "gz"))[1:]:
        total = total + other.astype(F32)
    mixed = (tokens.astype(F32) + total).astype(BF16)
    return (mixed, new_kv)


def solution(mesh):
    in_specs = (
        P("group", "gx"),
        P("gx"),
        P("gx", ("gy", "gz")),
        P("gx", None),
        P(("gy", "gz"), "gx"),
        P("gx", ("gy", "gz")),
        P("gx", ("gy", "gz")),
        P(("gy", "gz"), "gx"),
        P(("group", "gy"), ("gx", "gz"), None),
        P(("group", "gy")),
    )
    out_specs = (P("group", "gx"), P(("group", "gy"), None))
    return jax.shard_map(body, mesh=mesh, in_specs=in_specs, out_specs=out_specs, check_vma=False)
```

time: 63.2 us -> 45.6 us (0.72)
  matrix products: 19.1 us -> 0 us
  Pallas kernels: 5.12 us -> 12.5 us
  local copies, waits for them, and re-layouts: 7.48 us -> 2.97 us
  waiting for transfers between devices: 11.9 us -> 7.98 us
  starting transfers between devices: 17.7 us -> 19.9 us
    dot_general x3 -> x0, matrix products: 19.1 us -> none  [the longest x1 8.79 us: body(): up_part = jnp.dot(lhs, up_weight, preferred_element_type=F32).astype(BF16)]
    ppermute x6 -> x18, starting transfers between devices: 7.86 us -> 19.9 us  [the longest x15 17.5 us: with_others(): lax.ppermute(values, axis, [(place, place ^ step) for place in range(size)])]
    all_to_all x2 -> x0, starting transfers between devices: 9.79 us -> none  [body(): got = lax.all_to_all(sent, PART, split_axis=0, concat_axis=0, tiled=True)]
    all_to_all x2 -> x0, waiting for transfers between devices: 8.3 us -> none  [body(): got = lax.all_to_all(sent, PART, split_axis=0, concat_axis=0, tiled=True)]
    pallas_call x3 -> x7, Pallas kernels: 4.31 us -> 11.7 us  [the longest x2 6.19 us: partial_sums(): pl.pallas_call(partial_kernel, out_shape=jax.ShapeDtypeStruct((rows, ff_d...]
    unnamed x18 -> x38, local copies, waits for them, and re-layouts: 7.44 us -> 2.92 us
    ppermute x6 -> x18, waiting for transfers between devices: 3.55 us -> 7.98 us  [the longest x15 5.84 us: with_others(): lax.ppermute(values, axis, [(place, place ^ step) for place in range(size)])]
  transfers between devices with their start and end apart: 8 -> 18, of which waited for: 3 -> 6; matrix products, arithmetic and copies ran while one was open for 13% -> 0% of each run, Pallas kernels for 3% -> 24%
where the time goes in v3:
time: 45.6 us; the launch traced here: 45.1 us
  starting transfers between devices  19.9 us (44%)
  Pallas kernels  12.5 us (27%)
  waiting for transfers between devices  7.98 us (18%)
  local copies, waits for them, and re-layouts  2.97 us (7%)
  between operations  0.94 us (2%)
  other arithmetic  0.75 us (2%)
    ppermute x15, starting transfers between devices, with_others(): lax.ppermute(values, axis, [(place, place ^ step) for place in range(size)])  17.5 us
    pallas_call x2, Pallas kernels, partial_sums(): pl.pallas_call(partial_kernel, out_shape=jax.ShapeDtypeStruct((rows, ff_d...  6.19 us
    ppermute x15, waiting for transfers between devices, with_others(): lax.ppermute(values, axis, [(place, place ^ step) for place in range(size)])  5.84 us
    unnamed x38, local copies, waits for them, and re-layouts  2.92 us
    pallas_call x1, Pallas kernels, body(): pl.pallas_call(functools.partial(down_kernel, (gx, seq_dev)), out_shape=j...  2.89 us
    ppermute x3, starting transfers between devices, body(): lax.ppermute(pieces[step], ('gy', 'gz'), [(place, place ^ step) for place...  2.43 us
    ppermute x3, waiting for transfers between devices, body(): lax.ppermute(pieces[step], ('gy', 'gz'), [(place, place ^ step) for place...  2.14 us
    pallas_call x1, Pallas kernels, body(): pl.pallas_call(functools.partial(attention_kernel, (gy, gz, seq_dev, q_de...  1.66 us
  transfers between devices with their start and end apart: 18, of which 6 were waited for; matrix products, arithmetic and copies ran while one was open for 0% of the time, Pallas kernels for 24%

profile of v3, /device:TPU:0, one launch (start us, length us, event | category | flops | bytes accessed | tf_op | source)
XLA Modules:
  0.0 45.1 jit_solution(13762350823015272662)
XLA Ops:
  1.4 1.5 %copy-done.2 = bf16[2048,1024]{1,0:T(8,128)(2,1)S(1)} copy-done((bf16[2048,1024]{1,0:T(8,128)(2,1)S(1)}, bf16[2048,1024]{1,0:T(8,128)(2,1)}, u32[]{:S(2)}) %copy-start.2) | copy-done | bytes 4194328
  2.9 0.7 %copy-done.3 = bf16[2048,512]{1,0:T(8,128)(2,1)S(1)} copy-done((bf16[2048,512]{1,0:T(8,128)(2,1)S(1)}, bf16[2048,512]{1,0:T(8,128)(2,1)}, u32[]{:S(2)}) %copy-start.3) | copy-done | bytes 2097176
  3.6 0.8 %norm_query.1 = (bf16[8,1280]{1,0:T(8,128)(2,1)S(1)}, bf16[8,2048]{1,0:T(8,128)(2,1)S(1)}) custom-call(bf16[6,2048]{1,0:T(8,128)(2,1)S(1)} %copy-done.1, f32[1,2048]{1,0:T(1,128)S(1)} %bitcast.18, bf16[2048,1024]{1,0:T(8,128)(2,1)S(1)} %copy-done.2, bf16[2048,512]{1,0:T(8,128)(2,1)S(1)} %copy-done.3, f32[1,128]{1,0:T(1,128)S(1)} %exponents.1.after), custom_call_target="tpu_custom_call" | custom-call | flops 7000000000 | tf_op jit(solution)/shard_map/norm_query/pallas_call | solution.py:326
  4.4 3.1 %collective-permute-start = (bf16[8,1280]{1,0:T(8,128)(2,1)S(1)}, bf16[8,1280]{1,0:T(8,128)(2,1)S(1)}, u32[]{:S(2)}, u32[]{:S(2)}) collective-permute-start(bf16[8,1280]{1,0:T(8,128)(2,1)S(1)} %get-tuple-element.13.refs_0_), channel_id=1, source_target_pairs={{0,4},{4,0},{8,12},{12,8},{1,5},{5,1},{9,13},{13,9},{2,6},{6,2},{1... | collective-permute-start | bytes 61448 | tf_op jit(solution)/shard_map/ppermute | solution.py:280
  7.4 2.6 %collective-permute-start.1 = (bf16[8,1280]{1,0:T(8,128)(2,1)S(1)}, bf16[8,1280]{1,0:T(8,128)(2,1)S(1)}, u32[]{:S(2)}, u32[]{:S(2)}) collective-permute-start(bf16[8,1280]{1,0:T(8,128)(2,1)S(1)} %get-tuple-element.13.refs_0_), channel_id=1, source_target_pairs={{0,8},{4,12},{8,0},{12,4},{1,9},{5,13},{9,1},{13,5},{2,10},{6,14},... | collective-permute-start | bytes 61448 | tf_op jit(solution)/shard_map/ppermute | solution.py:280
  10.2 3.1 %gate.1 = bf16[8,4096]{1,0:T(8,128)(2,1)S(1)} custom-call(bf16[8,2048]{1,0:T(8,128)(2,1)S(1)} %get-tuple-element.15.lhs, bf16[2048,4096]{1,0:T(8,128)(2,1)S(1)} %bitcast.15), custom_call_target="tpu_custom_call" | custom-call | flops 6000000000 | bytes 16800000 | tf_op jit(solution)/shard_map/gate/pallas_call | solution.py:354
  13.4 2.2 %collective-permute-done.2.refs_3_ = bf16[8,1280]{1,0:T(8,128)(2,1)S(1)} collective-permute-done((bf16[8,1280]{1,0:T(8,128)(2,1)S(1)}, bf16[8,1280]{1,0:T(8,128)(2,1)S(1)}, u32[]{:S(2)}, u32[]{:S(2)}) %collective-permute-start.2) | collective-permute-done | bytes 20512 | tf_op jit(solution)/shard_map/ppermute | solution.py:280
  15.8 1.6 %collective-permute-start.4 = (bf16[8,1152]{1,0:T(8,128)(2,1)S(1)}, bf16[8,1152]{1,0:T(8,128)(2,1)S(1)}, u32[]{:S(2)}, u32[]{:S(2)}) collective-permute-start(bf16[8,1152]{1,0:T(8,128)(2,1)S(1)} %get-tuple-element.14.refs_0_), channel_id=1, source_target_pairs={{0,2},{1,3},{2,0},{3,1},{4,6},{5,7},{6,4},{7,5},{8,10},{9,11},{10,... | collective-permute-start | bytes 55304 | tf_op jit(solution)/shard_map/ppermute | solution.py:280
  17.7 3.1 %up.1 = bf16[8,4096]{1,0:T(8,128)(2,1)S(1)} custom-call(bf16[8,2048]{1,0:T(8,128)(2,1)S(1)} %get-tuple-element.15.lhs, bf16[2048,4096]{1,0:T(8,128)(2,1)S(1)} %bitcast.17, bf16[8,1152]{1,0:T(8,128)(2,1)S(1)} %get-tuple-element.14.refs_0_), custom_call_target="tpu_custom_call" | custom-call | flops 6000000000 | bytes 16800000 | tf_op jit(solution)/shard_map/up/pallas_call | solution.py:354
  21.0 2.1 %collective-permute-start.13 = (bf16[16,4096]{1,0:T(8,128)(2,1)S(1)}, bf16[16,4096]{1,0:T(8,128)(2,1)S(1)}, u32[]{:S(2)}, u32[]{:S(2)}) collective-permute-start(bf16[16,4096]{1,0:T(8,128)(2,1)S(1)} %pad_maximum_fusion.refs_7_.refs_0_), channel_id=1, source_target_pairs={{0,8},{4,12},{8,0},{12,4},{1,9},{5,13},{9,1},{13,5},{2,10},{6,14},... | collective-permute-start | bytes 393224 | tf_op jit(solution)/shard_map/ppermute | solution.py:280
  23.1 2.2 %collective-permute-start.14 = (bf16[16,4096]{1,0:T(8,128)(2,1)S(1)}, bf16[16,4096]{1,0:T(8,128)(2,1)S(1)}, u32[]{:S(2)}, u32[]{:S(2)}) collective-permute-start(bf16[16,4096]{1,0:T(8,128)(2,1)S(1)} %pad_maximum_fusion.refs_7_.refs_0_), channel_id=1, source_target_pairs={{0,12},{4,8},{8,4},{12,0},{1,13},{5,9},{9,5},{13,1},{2,14},{6,10},... | collective-permute-start | bytes 393224 | tf_op jit(solution)/shard_map/ppermute | solution.py:280
  25.4 1.7 %attention.1 = (bf16[16,256]{1,0:T(8,128)(2,1)S(1)}, bf16[16,256]{1,0:T(8,128)(2,1)S(1)}, bf16[16,256]{1,0:T(8,128)(2,1)S(1)}, bf16[16,256]{1,0:T(8,128)(2,1)S(1)}, bf16[3,512]{1,0:T(4,128)(2,1)}) custom-call(bf16[8,1152]{1,0:T(8,128)(2,1)S(1)} %get-tuple-element.14.refs_0_, bf16[8,1152]{1,0:T(8,128)(2,1)S(1)} %collective-permute-done.3.refs_1_, ...), custom_call_target="tpu_custom_call" | custom-call | flops 7000000000 | bytes 2000000 | tf_op jit(solution)/shard_map/attention/pallas_call | solution.py:372
  27.0 1.5 %collective-permute-start.7 = (bf16[16,256]{1,0:T(8,128)(2,1)S(1)}, bf16[16,256]{1,0:T(8,128)(2,1)S(1)}, u32[]{:S(2)}, u32[]{:S(2)}) collective-permute-start(bf16[16,256]{1,0:T(8,128)(2,1)S(1)} %get-tuple-element.18), channel_id=1, source_target_pairs={{0,2},{1,3},{2,0},{3,1},{4,6},{5,7},{6,4},{7,5},{8,10},{9,11},{10,... | collective-permute-start | bytes 24584 | tf_op jit(solution)/shard_map/ppermute | solution.py:384
  28.5 0.9 %collective-permute-start.8 = (bf16[16,256]{1,0:T(8,128)(2,1)S(1)}, bf16[16,256]{1,0:T(8,128)(2,1)S(1)}, u32[]{:S(2)}, u32[]{:S(2)}) collective-permute-start(bf16[16,256]{1,0:T(8,128)(2,1)S(1)} %get-tuple-element.19), channel_id=1, source_target_pairs={{0,3},{1,2},{2,1},{3,0},{4,7},{5,6},{6,5},{7,4},{8,11},{9,10},{10,... | collective-permute-start | bytes 24584 | tf_op jit(solution)/shard_map/ppermute | solution.py:384
  29.5 1.2 %collective-permute-done.7 = bf16[16,256]{1,0:T(8,128)(2,1)S(1)} collective-permute-done((bf16[16,256]{1,0:T(8,128)(2,1)S(1)}, bf16[16,256]{1,0:T(8,128)(2,1)S(1)}, u32[]{:S(2)}, u32[]{:S(2)}) %collective-permute-start.7) | collective-permute-done | bytes 8224 | tf_op jit(solution)/shard_map/ppermute | solution.py:384
  30.7 0.9 %collective-permute-done.8 = bf16[16,256]{1,0:T(8,128)(2,1)S(1)} collective-permute-done((bf16[16,256]{1,0:T(8,128)(2,1)S(1)}, bf16[16,256]{1,0:T(8,128)(2,1)S(1)}, u32[]{:S(2)}, u32[]{:S(2)}) %collective-permute-start.8) | collective-permute-done | bytes 8224 | tf_op jit(solution)/shard_map/ppermute | solution.py:384
  31.7 1.6 %collective-permute-start.11 = (bf16[4,16,256]{2,1,0:T(8,128)(2,1)S(1)}, bf16[4,16,256]{2,1,0:T(8,128)(2,1)S(1)}, u32[]{:S(2)}, u32[]{:S(2)}) collective-permute-start(bf16[4,16,256]{2,1,0:T(8,128)(2,1)S(1)} %pad_maximum_fusion.1.refs_0_), channel_id=1, source_target_pairs={{0,12},{4,8},{8,4},{12,0},{1,13},{5,9},{9,5},{13,1},{2,14},{6,10},... | collective-permute-start | bytes 98312 | tf_op jit(solution)/shard_map/ppermute | solution.py:280
  33.3 1.8 %collective-permute-start.9 = (bf16[4,16,256]{2,1,0:T(8,128)(2,1)S(1)}, bf16[4,16,256]{2,1,0:T(8,128)(2,1)S(1)}, u32[]{:S(2)}, u32[]{:S(2)}) collective-permute-start(bf16[4,16,256]{2,1,0:T(8,128)(2,1)S(1)} %pad_maximum_fusion.1.refs_0_), channel_id=1, source_target_pairs={{0,4},{4,0},{8,12},{12,8},{1,5},{5,1},{9,13},{13,9},{2,6},{6,2},{1... | collective-permute-start | bytes 98312 | tf_op jit(solution)/shard_map/ppermute | solution.py:280
  35.2 2.9 %hidden_down.1.refs_5_ = f32[8,2048]{1,0:T(8,128)S(1)} custom-call(f32[5,8,128]{2,1,0:T(8,128)S(1)} %get-tuple-element.20.stats, bf16[16,4096]{1,0:T(8,128)(2,1)S(1)} %pad_maximum_fusion.refs_7_.refs_0_, bf16[16,4096]{1,0:T(8,128)(2,1)S(1)} %collective-permute-done.12.refs_1_, bf16[16,4096]{1,0:T(8,128)(2,1)S(1)} %collective-permute-done.13.refs_2_, ...), custom_call_target="tpu_custom_call" | custom-call | flops 4000000000 | bytes 16800000 | tf_op jit(solution)/shard_map/hidden_down/pallas_call | solution.py:389
  38.6 0.8 %out_projection.1 = (f32[6,2048]{1,0:T(8,128)S(1)}, bf16[6,2048]{1,0:T(8,128)(2,1)S(1)}) custom-call(bf16[4,16,256]{2,1,0:T(8,128)(2,1)S(1)} %pad_maximum_fusion.1.refs_0_, bf16[4,16,256]{2,1,0:T(8,128)(2,1)S(1)} %collective-permute-done.9.refs_1_, bf16[4,16,256]{2,1,0:T(8,128)(2,1)S(1)} %collective-permute-done.10.refs_2_, ...), custom_call_target="tpu_custom_call" | custom-call | flops 1000000000 | bytes 4000000 | tf_op jit(solution)/shard_map/out_projection/pallas_call | solution.py:399
  39.5 1.6 %collective-permute-start.16 = (bf16[6,2048]{1,0:T(8,128)(2,1)S(1)}, bf16[6,2048]{1,0:T(8,128)(2,1)S(1)}, u32[]{:S(2)}, u32[]{:S(2)}) collective-permute-start(bf16[6,2048]{1,0:T(8,128)(2,1)S(1)} %get-tuple-element.22), channel_id=1, source_target_pairs={{0,2},{1,3},{2,0},{3,1},{4,6},{5,7},{6,4},{7,5},{8,10},{9,11},{10,... | collective-permute-start | bytes 73736 | tf_op jit(solution)/shard_map/ppermute | solution.py:280
  41.4 2.1 %collective-permute-done.16 = bf16[6,2048]{1,0:T(8,128)(2,1)S(1)} collective-permute-done((bf16[6,2048]{1,0:T(8,128)(2,1)S(1)}, bf16[6,2048]{1,0:T(8,128)(2,1)S(1)}, u32[]{:S(2)}, u32[]{:S(2)}) %collective-permute-start.16) | collective-permute-done | bytes 24608 | tf_op jit(solution)/shard_map/ppermute | solution.py:280
  43.5 0.9 %collective-permute-done.17 = bf16[6,2048]{1,0:T(8,128)(2,1)S(1)} collective-permute-done((bf16[6,2048]{1,0:T(8,128)(2,1)S(1)}, bf16[6,2048]{1,0:T(8,128)(2,1)S(1)}, u32[]{:S(2)}, u32[]{:S(2)}) %collective-permute-start.17) | collective-permute-done | bytes 24608 | tf_op jit(solution)/shard_map/ppermute | solution.py:280
  44.4 0.6 %add_convert_fusion = bf16[6,2048]{1,0:T(8,128)(2,1)} fusion(bf16[6,2048]{1,0:T(8,128)(2,1)S(1)} %collective-permute-done.17, bf16[6,2048]{1,0:T(8,128)(2,1)S(1)} %collective-permute-done.16, f32[6,2048]{1,0:T(8,128)S(1)} %get-tuple-element.21, bf16[6,2048]{1,0:T(8,128)(2,1)S(1)} %collective-permute-done.15, bf16[6,2048]{1,0:T(8,128)(2,1)S(1)} %copy-done.1), kind=kLoop, calls=%fused_computation.1 | loop fusion | flops 110592 | bytes 172032 | tf_op jit(solution)/shard_map/convert_element_type | solution.py:414
  (69 shorter events, 2.5 us)
Async XLA Ops:
  3.6 14.1 %slice-start.9 = ((s8[16777216]{0:T(1024)(128)(4,1)}), s8[4194304]{0:T(1024)(128)(4,1)S(1)}, s32[]{:S(2)}) async-start(s8[16777216]{0:T(1024)(128)(4,1)} %bitcast.16), calls=%async_computation.9 | async-start | bytes 8388608
  4.4 9.0 %collective-permute-start = (bf16[8,1280]{1,0:T(8,128)(2,1)S(1)}, bf16[8,1280]{1,0:T(8,128)(2,1)S(1)}, u32[]{:S(2)}, u32[]{:S(2)}) collective-permute-start(bf16[8,1280]{1,0:T(8,128)(2,1)S(1)} %get-tuple-element.13.refs_0_), channel_id=1, source_target_pairs={{0,4},{4,0},{8,12},{12,8},{1,5},{5,1},{9,13},{13,9},{2,6},{6,2},{1... | collective-permute-start | bytes 61448 | tf_op jit(solution)/shard_map/ppermute | solution.py:280
  7.4 5.9 %collective-permute-start.1 = (bf16[8,1280]{1,0:T(8,128)(2,1)S(1)}, bf16[8,1280]{1,0:T(8,128)(2,1)S(1)}, u32[]{:S(2)}, u32[]{:S(2)}) collective-permute-start(bf16[8,1280]{1,0:T(8,128)(2,1)S(1)} %get-tuple-element.13.refs_0_), channel_id=1, source_target_pairs={{0,8},{4,12},{8,0},{12,4},{1,9},{5,13},{9,1},{13,5},{2,10},{6,14},... | collective-permute-start | bytes 61448 | tf_op jit(solution)/shard_map/ppermute | solution.py:280
  10.0 5.6 %collective-permute-start.2 = (bf16[8,1280]{1,0:T(8,128)(2,1)S(1)}, bf16[8,1280]{1,0:T(8,128)(2,1)S(1)}, u32[]{:S(2)}, u32[]{:S(2)}) collective-permute-start(bf16[8,1280]{1,0:T(8,128)(2,1)S(1)} %get-tuple-element.13.refs_0_), channel_id=1, source_target_pairs={{0,12},{4,8},{8,4},{12,0},{1,13},{5,9},{9,5},{13,1},{2,14},{6,10},... | collective-permute-start | bytes 61448 | tf_op jit(solution)/shard_map/ppermute | solution.py:280
  15.7 7.4 %collective-permute-start.3 = (bf16[8,1152]{1,0:T(8,128)(2,1)S(1)}, bf16[8,1152]{1,0:T(8,128)(2,1)S(1)}, u32[]{:S(2)}, u32[]{:S(2)}) collective-permute-start(bf16[8,1152]{1,0:T(8,128)(2,1)S(1)} %get-tuple-element.14.refs_0_), channel_id=1, source_target_pairs={{0,1},{1,0},{2,3},{3,2},{4,5},{5,4},{6,7},{7,6},{8,9},{9,8},{10,11... | collective-permute-start | bytes 55304 | tf_op jit(solution)/shard_map/ppermute | solution.py:280
  15.8 9.5 %collective-permute-start.4 = (bf16[8,1152]{1,0:T(8,128)(2,1)S(1)}, bf16[8,1152]{1,0:T(8,128)(2,1)S(1)}, u32[]{:S(2)}, u32[]{:S(2)}) collective-permute-start(bf16[8,1152]{1,0:T(8,128)(2,1)S(1)} %get-tuple-element.14.refs_0_), channel_id=1, source_target_pairs={{0,2},{1,3},{2,0},{3,1},{4,6},{5,7},{6,4},{7,5},{8,10},{9,11},{10,... | collective-permute-start | bytes 55304 | tf_op jit(solution)/shard_map/ppermute | solution.py:280
  17.4 8.0 %collective-permute-start.5 = (bf16[8,1152]{1,0:T(8,128)(2,1)S(1)}, bf16[8,1152]{1,0:T(8,128)(2,1)S(1)}, u32[]{:S(2)}, u32[]{:S(2)}) collective-permute-start(bf16[8,1152]{1,0:T(8,128)(2,1)S(1)} %get-tuple-element.14.refs_0_), channel_id=1, source_target_pairs={{0,3},{1,2},{2,1},{3,0},{4,7},{5,6},{6,5},{7,4},{8,11},{9,10},{10,... | collective-permute-start | bytes 55304 | tf_op jit(solution)/shard_map/ppermute | solution.py:280
  17.7 17.5 %slice-start = ((s8[16777216]{0:T(1024)(128)(4,1)}), s8[4194304]{0:T(1024)(128)(4,1)S(1)}, s32[]{:S(2)}) async-start(s8[16777216]{0:T(1024)(128)(4,1)} %bitcast.11), calls=%async_computation | async-start | bytes 8388608
  17.7 17.5 %slice-start.1 = ((s8[16777216]{0:T(1024)(128)(4,1)}), s8[4194304]{0:T(1024)(128)(4,1)S(1)}, s32[]{:S(2)}) async-start(s8[16777216]{0:T(1024)(128)(4,1)} %bitcast.11), calls=%async_computation.1 | async-start | bytes 8388608
  20.9 14.3 %slice-start.2 = ((s8[16777216]{0:T(1024)(128)(4,1)}), s8[4194304]{0:T(1024)(128)(4,1)S(1)}, s32[]{:S(2)}) async-start(s8[16777216]{0:T(1024)(128)(4,1)} %bitcast.11), calls=%async_computation.2 | async-start | bytes 8388608
  20.9 14.3 %slice-start.3 = ((s8[16777216]{0:T(1024)(128)(4,1)}), s8[4194304]{0:T(1024)(128)(4,1)S(1)}, s32[]{:S(2)}) async-start(s8[16777216]{0:T(1024)(128)(4,1)} %bitcast.11), calls=%async_computation.3 | async-start | bytes 8388608
  20.9 17.7 %copy-start = (bf16[1024,2048]{1,0:T(8,128)(2,1)S(1)}, bf16[1024,2048]{1,0:T(8,128)(2,1)}, u32[]{:S(2)}) copy-start(bf16[1024,2048]{1,0:T(8,128)(2,1)} %refs_4_.5) | copy-start | bytes 12582916
  20.9 12.4 %collective-permute-start.12 = (bf16[16,4096]{1,0:T(8,128)(2,1)S(1)}, bf16[16,4096]{1,0:T(8,128)(2,1)S(1)}, u32[]{:S(2)}, u32[]{:S(2)}) collective-permute-start(bf16[16,4096]{1,0:T(8,128)(2,1)S(1)} %pad_maximum_fusion.refs_7_.refs_0_), channel_id=1, source_target_pairs={{0,4},{4,0},{8,12},{12,8},{1,5},{5,1},{9,13},{13,9},{2,6},{6,2},{1... | collective-permute-start | bytes 393224 | tf_op jit(solution)/shard_map/ppermute | solution.py:280
  21.0 14.2 %collective-permute-start.13 = (bf16[16,4096]{1,0:T(8,128)(2,1)S(1)}, bf16[16,4096]{1,0:T(8,128)(2,1)S(1)}, u32[]{:S(2)}, u32[]{:S(2)}) collective-permute-start(bf16[16,4096]{1,0:T(8,128)(2,1)S(1)} %pad_maximum_fusion.refs_7_.refs_0_), channel_id=1, source_target_pairs={{0,8},{4,12},{8,0},{12,4},{1,9},{5,13},{9,1},{13,5},{2,10},{6,14},... | collective-permute-start | bytes 393224 | tf_op jit(solution)/shard_map/ppermute | solution.py:280
  23.1 12.1 %collective-permute-start.14 = (bf16[16,4096]{1,0:T(8,128)(2,1)S(1)}, bf16[16,4096]{1,0:T(8,128)(2,1)S(1)}, u32[]{:S(2)}, u32[]{:S(2)}) collective-permute-start(bf16[16,4096]{1,0:T(8,128)(2,1)S(1)} %pad_maximum_fusion.refs_7_.refs_0_), channel_id=1, source_target_pairs={{0,12},{4,8},{8,4},{12,0},{1,13},{5,9},{9,5},{13,1},{2,14},{6,10},... | collective-permute-start | bytes 393224 | tf_op jit(solution)/shard_map/ppermute | solution.py:280
  27.0 1.5 %collective-permute-start.6 = (bf16[16,256]{1,0:T(8,128)(2,1)S(1)}, bf16[16,256]{1,0:T(8,128)(2,1)S(1)}, u32[]{:S(2)}, u32[]{:S(2)}) collective-permute-start(bf16[16,256]{1,0:T(8,128)(2,1)S(1)} %get-tuple-element.17), channel_id=1, source_target_pairs={{0,1},{1,0},{2,3},{3,2},{4,5},{5,4},{6,7},{7,6},{8,9},{9,8},{10,11... | collective-permute-start | bytes 24584 | tf_op jit(solution)/shard_map/ppermute | solution.py:384
  27.0 3.7 %collective-permute-start.7 = (bf16[16,256]{1,0:T(8,128)(2,1)S(1)}, bf16[16,256]{1,0:T(8,128)(2,1)S(1)}, u32[]{:S(2)}, u32[]{:S(2)}) collective-permute-start(bf16[16,256]{1,0:T(8,128)(2,1)S(1)} %get-tuple-element.18), channel_id=1, source_target_pairs={{0,2},{1,3},{2,0},{3,1},{4,6},{5,7},{6,4},{7,5},{8,10},{9,11},{10,... | collective-permute-start | bytes 24584 | tf_op jit(solution)/shard_map/ppermute | solution.py:384
  28.5 3.1 %collective-permute-start.8 = (bf16[16,256]{1,0:T(8,128)(2,1)S(1)}, bf16[16,256]{1,0:T(8,128)(2,1)S(1)}, u32[]{:S(2)}, u32[]{:S(2)}) collective-permute-start(bf16[16,256]{1,0:T(8,128)(2,1)S(1)} %get-tuple-element.19), channel_id=1, source_target_pairs={{0,3},{1,2},{2,1},{3,0},{4,7},{5,6},{6,5},{7,4},{8,11},{9,10},{10,... | collective-permute-start | bytes 24584 | tf_op jit(solution)/shard_map/ppermute | solution.py:384
  31.6 7.0 %collective-permute-start.10 = (bf16[4,16,256]{2,1,0:T(8,128)(2,1)S(1)}, bf16[4,16,256]{2,1,0:T(8,128)(2,1)S(1)}, u32[]{:S(2)}, u32[]{:S(2)}) collective-permute-start(bf16[4,16,256]{2,1,0:T(8,128)(2,1)S(1)} %pad_maximum_fusion.1.refs_0_), channel_id=1, source_target_pairs={{0,8},{4,12},{8,0},{12,4},{1,9},{5,13},{9,1},{13,5},{2,10},{6,14},... | collective-permute-start | bytes 98312 | tf_op jit(solution)/shard_map/ppermute | solution.py:280
  31.7 6.9 %collective-permute-start.11 = (bf16[4,16,256]{2,1,0:T(8,128)(2,1)S(1)}, bf16[4,16,256]{2,1,0:T(8,128)(2,1)S(1)}, u32[]{:S(2)}, u32[]{:S(2)}) collective-permute-start(bf16[4,16,256]{2,1,0:T(8,128)(2,1)S(1)} %pad_maximum_fusion.1.refs_0_), channel_id=1, source_target_pairs={{0,12},{4,8},{8,4},{12,0},{1,13},{5,9},{9,5},{13,1},{2,14},{6,10},... | collective-permute-start | bytes 98312 | tf_op jit(solution)/shard_map/ppermute | solution.py:280
  33.3 5.3 %collective-permute-start.9 = (bf16[4,16,256]{2,1,0:T(8,128)(2,1)S(1)}, bf16[4,16,256]{2,1,0:T(8,128)(2,1)S(1)}, u32[]{:S(2)}, u32[]{:S(2)}) collective-permute-start(bf16[4,16,256]{2,1,0:T(8,128)(2,1)S(1)} %pad_maximum_fusion.1.refs_0_), channel_id=1, source_target_pairs={{0,4},{4,0},{8,12},{12,8},{1,5},{5,1},{9,13},{13,9},{2,6},{6,2},{1... | collective-permute-start | bytes 98312 | tf_op jit(solution)/shard_map/ppermute | solution.py:280
  39.5 1.9 %collective-permute-start.15 = (bf16[6,2048]{1,0:T(8,128)(2,1)S(1)}, bf16[6,2048]{1,0:T(8,128)(2,1)S(1)}, u32[]{:S(2)}, u32[]{:S(2)}) collective-permute-start(bf16[6,2048]{1,0:T(8,128)(2,1)S(1)} %get-tuple-element.22), channel_id=1, source_target_pairs={{0,1},{1,0},{2,3},{3,2},{4,5},{5,4},{6,7},{7,6},{8,9},{9,8},{10,11... | collective-permute-start | bytes 73736 | tf_op jit(solution)/shard_map/ppermute | solution.py:280
  39.5 4.0 %collective-permute-start.16 = (bf16[6,2048]{1,0:T(8,128)(2,1)S(1)}, bf16[6,2048]{1,0:T(8,128)(2,1)S(1)}, u32[]{:S(2)}, u32[]{:S(2)}) collective-permute-start(bf16[6,2048]{1,0:T(8,128)(2,1)S(1)} %get-tuple-element.22), channel_id=1, source_target_pairs={{0,2},{1,3},{2,0},{3,1},{4,6},{5,7},{6,4},{7,5},{8,10},{9,11},{10,... | collective-permute-start | bytes 73736 | tf_op jit(solution)/shard_map/ppermute | solution.py:280
  41.1 3.3 %collective-permute-start.17 = (bf16[6,2048]{1,0:T(8,128)(2,1)S(1)}, bf16[6,2048]{1,0:T(8,128)(2,1)S(1)}, u32[]{:S(2)}, u32[]{:S(2)}) collective-permute-start(bf16[6,2048]{1,0:T(8,128)(2,1)S(1)} %get-tuple-element.22), channel_id=1, source_target_pairs={{0,3},{1,2},{2,1},{3,0},{4,7},{5,6},{6,5},{7,4},{8,11},{9,10},{10,... | collective-permute-start | bytes 73736 | tf_op jit(solution)/shard_map/ppermute | solution.py:280
  (13 other events, 96.0 us)

commit v4 on v3

v4 whole, which is shorter than its diff:
```python
import functools

import jax
import jax.numpy as jnp
from jax import lax
from jax.experimental import pallas as pl
from jax.experimental.pallas import tpu as pltpu
from jax.sharding import PartitionSpec as P

epsilon = 1e-05
masked_fill = -1e30
rotary_base = 10000.0
FEW = 8
LIMIT = 3
F32 = jnp.float32
BF16 = jnp.bfloat16
VMEM = pl.BlockSpec(memory_space=pltpu.VMEM)
SMEM = pl.BlockSpec(memory_space=pltpu.SMEM)
ANY = pl.BlockSpec(memory_space=pl.ANY)
HBM = pl.BlockSpec(memory_space=pltpu.HBM)
MIB = 2**20


def iota(shape, dim):
    return lax.broadcasted_iota(jnp.int32, shape, dim)


def thirds(values):
    high = values.astype(BF16).astype(F32)
    rest = values - high
    middle = rest.astype(BF16).astype(F32)
    return high, middle, rest - middle


def from_lanes(row, first, count):
    lane = iota(row.shape, 1)
    return jnp.sum(jnp.where((lane >= first) & (lane < first + count), row, 0.0), 1, keepdims=True)


def rotated_halves(values, cosine, sine):
    middle = values.shape[-1] // 2
    first, second = values[:, :middle], values[:, middle:]
    return jnp.concatenate(
        [first * cosine - second * sine, first * sine + second * cosine], 1
    )


def cost(flops, nbytes):
    return pl.CostEstimate(flops=int(flops), bytes_accessed=int(nbytes), transcendentals=0)


def params(mebibytes):
    return pltpu.CompilerParams(vmem_limit_bytes=mebibytes * MIB)


def exponent_kernel(table):
    table[...] = iota(table.shape, 1).astype(F32) / -table.shape[1]


def first_kernel(dims, tokens, gain, q_weight, kv_weight, after, sums, lhs, rows):
    gy, seq_dev = dims
    inputs = tokens[...].astype(F32)
    seqs, width = inputs.shape
    mean = jnp.sum(inputs, 1, keepdims=True) / width
    centred = inputs - mean
    square = jnp.sum(centred * centred, 1, keepdims=True)
    scaled = centred * gain[...]
    each = seq_dev + 1
    for a in range(gy):
        rows[a * each : a * each + seq_dev, :] = scaled[a * seq_dev : (a + 1) * seq_dev]
        rows[a * each + seq_dev : (a + 1) * each, :] = gain[...]
    lhs[...] = rows[...].astype(BF16)

    lanes = sums.shape[1] - q_weight.shape[1] - kv_weight.shape[1]
    lane = iota((seqs, lanes), 1)
    first = iota((seqs, lanes), 0) * 6
    marks = jnp.zeros((seqs, lanes), F32)
    for place, term in enumerate(thirds(mean) + thirds(square)):
        marks = jnp.where(lane == first + place, term, marks)
    marks = jnp.broadcast_to(jnp.sum(marks, 0, keepdims=True), (gy * each, lanes))

    values = lhs[...]
    query = jnp.dot(values, q_weight[...], preferred_element_type=F32)
    keyval = jnp.dot(values, kv_weight[...], preferred_element_type=F32)
    sums[...] = jnp.concatenate([query, keyval, marks], 1).astype(BF16)


def centring(dims, parts, width):
    gx, gy, seq_dev, features = dims
    each = seq_dev + 1
    place = iota((gy * each, 1), 0)
    valid = place % each < seq_dev
    first = (place // each * seq_dev + place % each) * 6
    means, squares = [], 0.0
    for part in parts:
        marks = part[:, width:].astype(F32)
        means.append(jnp.where(valid, from_lanes(marks, first, 3), 0.0))
        squares += from_lanes(marks, first + 3, 3)
    center = sum(means) / gx
    shifts = [mean - center for mean in means]
    spread = squares / features + sum(s * s for s in shifts) / gx
    return shifts, jnp.where(valid, lax.rsqrt(spread + epsilon), 0.0)


def shifted_sum(parts, shifts, seq_dev):
    total = 0.0
    for part, shift in zip(parts, shifts):
        part = part.astype(F32)
        total += part + shift * part[seq_dev : seq_dev + 1]
    return total


def product(lhs, weight, store, slab=512):
    slab = min(slab, weight.shape[1])

    def step(index, _):
        part = pl.ds(pl.multiple_of(index * slab, slab), slab)
        store(part, jnp.dot(lhs, weight[:, part], preferred_element_type=F32))
        return 0

    lax.fori_loop(0, weight.shape[1] // slab, step, 0)


def gate_kernel(lhs, weight, sums):
    def store(part, value):
        sums[:, part] = value.astype(BF16)

    product(lhs[...], weight, store)


def up_kernel(lhs, weight, gate, after, both):
    rows = lhs.shape[0]
    both[:rows, :] = gate[...]

    def store(part, value):
        both[rows:, part] = value.astype(BF16)

    product(lhs[...], weight, store)


def query_kernel(dims, *refs):
    gx, gy, seq_dev, q_dev, features = dims
    parts, (query, keyval, stats) = refs[:gx], refs[gx:]
    width = q_dev + keyval.shape[1]
    shifts, inverse = centring((gx, gy, seq_dev, features), parts, width)
    for step in range(gx):
        stats[step] = jnp.broadcast_to(shifts[step], stats.shape[1:])
    stats[gx] = jnp.broadcast_to(inverse, stats.shape[1:])
    whole = shifted_sum([part[:, :width] for part in parts], shifts, seq_dev) * inverse
    query[...] = whole[:, :q_dev].astype(BF16)
    keyval[...] = whole[:, q_dev:]


def attention_kernel(dims, *refs):
    gy, gz, seq_dev = dims
    each = seq_dev + 1
    parts, refs = refs[:gy], refs[gy:]
    caches, refs = refs[:gz], refs[gz:]
    lengths, keyval, tables, after = refs[:4]
    pieces, (new_kv, qs, ks, vs) = refs[4 : 4 + gy], refs[4 + gy :]
    ctx_dev, head_dim = caches[0].shape[1], caches[0].shape[2] // 2
    heads_dev = parts[0].shape[1] // head_dim
    row = lax.axis_index("gy")

    def own_rows(values):
        mine = values[:each]
        for a in range(1, gy):
            mine = jnp.where(row == a, values[a * each : (a + 1) * each], mine)
        return mine

    cosine, sine = tables[0], tables[1]
    fresh = own_rows(keyval[...])
    fresh = jnp.concatenate(
        [rotated_halves(fresh[:, :head_dim], cosine, sine), fresh[:, head_dim:]], 1
    ).astype(BF16)
    new_kv[...] = fresh[:seq_dev]
    fresh = fresh.astype(F32)
    for da in range(gy):
        query = own_rows(parts[da][...].astype(F32))
        for h in range(heads_dev):
            start = (da * heads_dev + h) * each
            part = slice(start, start + each)
            qs[part, :] = rotated_halves(query[:, h * head_dim : (h + 1) * head_dim], cosine, sine)
            ks[part, :] = fresh[:, :head_dim]
            vs[part, :] = fresh[:, head_dim:]

    count = heads_dev * each
    many = gy * count
    scale = head_dim ** (-0.5)
    queries = qs[...].astype(BF16)
    own = jnp.sum(queries.astype(F32) * ks[...], 1, keepdims=True) * scale
    sequence = iota((many, 1), 0) % each
    scores = []
    for db in range(gz):
        block = lax.axis_index("gx") * gz + (lax.axis_index("gz") ^ db)
        positions = block * ctx_dev + iota((many, ctx_dev), 1)
        found = jnp.full((many, ctx_dev), masked_fill, F32)
        for s in range(seq_dev):
            value = lax.dot_general(
                queries,
                caches[db][s, :, :head_dim],
                (((1,), (1,)), ((), ())),
                preferred_element_type=F32,
            )
            found = jnp.where((positions < lengths[s]) & (sequence == s), value * scale, found)
        scores.append(found)
    top = own
    for found in scores:
        top = jnp.maximum(top, jnp.max(found, 1, keepdims=True))
    own_weight = jnp.where(lax.axis_index("gx") == 0, jnp.exp(own - top), 0.0)
    denom = own_weight
    numer = own_weight * vs[...]
    for db in range(gz):
        weights = jnp.where(scores[db] > 0.5 * masked_fill, jnp.exp(scores[db] - top), 0.0)
        denom += jnp.sum(weights, 1, keepdims=True)
        for s in range(seq_dev):
            mine = jnp.where(sequence == s, weights, 0.0).astype(BF16)
            numer += jnp.dot(mine, caches[db][s, :, head_dim:], preferred_element_type=F32)

    lane = iota((many, head_dim), 1)
    terms = jnp.zeros((many, head_dim), F32)
    for j, term in enumerate(thirds(top) + thirds(denom)):
        terms = jnp.where((lane == sequence * 6 + j) & (sequence < seq_dev), term, terms)
    spare = jnp.zeros((many, head_dim), F32)
    for step in range(1, each):
        spare += pltpu.roll(terms, step, 0)
    out = jnp.where(sequence == seq_dev, spare, numer)
    for da in range(gy):
        pieces[da][...] = out[da * count : (da + 1) * count].astype(BF16)


def down_kernel(dims, stats, *refs):
    gx, seq_dev = dims
    parts, (down, result, hidden) = refs[:gx], refs[gx:]
    rows, ff_dev = hidden.shape
    slab = min(ff_dev, 1024)
    inverse = stats[gx][:, :1]
    shifts = [stats[step][:, :1] for step in range(gx)]
    for start in range(0, ff_dev, slab):
        sums = []
        for base in (0, rows):
            found = [part[base : base + rows, start : start + slab] for part in parts]
            sums.append(shifted_sum(found, shifts, seq_dev) * inverse)
        gate, upward = sums
        hidden[:, start : start + slab] = (gate / (1.0 + jnp.exp(-gate)) * upward).astype(BF16)

    def store(part, value):
        result[:, part] = value

    product(hidden[...], down, store)


def out_kernel(dims, *refs):
    gx, gy, seq_dev = dims
    parts, (out_weight, partial, total, share, turned, att) = refs[:gx], refs[gx:]
    each = seq_dev + 1
    count, head_dim = parts[0].shape[1:]
    sequence = iota((count, 1), 0) % each
    valid = sequence < seq_dev
    lanes = min(128, head_dim)
    row = lax.axis_index("gy")
    for da in range(gy):
        values, tops, denoms = [], [], []
        for part in parts:
            piece = part[da].astype(F32)
            spare = jnp.where(valid, 0.0, piece[:, :lanes])
            marks = spare
            for step in range(1, each):
                marks += pltpu.roll(spare, count - step, 0)
            values.append(piece)
            tops.append(from_lanes(marks, sequence * 6, 3))
            denoms.append(from_lanes(marks, sequence * 6 + 3, 3))
        top = functools.reduce(jnp.maximum, tops)
        numer, denom = 0.0, 0.0
        for value, mine, part in zip(values, tops, denoms):
            factor = jnp.exp(mine - top)
            numer += value * factor
            denom += part * factor
        ratio = jnp.where(valid, numer / jnp.where(valid, denom, 1.0), 0.0)
        for h in range(count // each):
            turned[row ^ da, :, h * head_dim : (h + 1) * head_dim] = ratio[
                h * each : (h + 1) * each
            ]
    for a in range(gy):
        att[a * each : (a + 1) * each, :] = turned[a]
    result = partial[...] + jnp.dot(
        att[...].astype(BF16), out_weight[...], preferred_element_type=F32
    )
    for a in range(gy):
        total[a * seq_dev : (a + 1) * seq_dev, :] = result[a * each : a * each + seq_dev]
    share[...] = total[...].astype(BF16)


def with_others(values, axis):
    size = lax.axis_size(axis)
    if size <= FEW:
        return [values] + [
            lax.ppermute(values, axis, [(place, place ^ step) for place in range(size)])
            for step in range(1, size)
        ]
    gathered = lax.all_gather(values, axis)
    here = lax.axis_index(axis)
    return [lax.dynamic_index_in_dim(gathered, here ^ step, 0, False) for step in range(size)]


def body(
    tokens,
    norm_gain,
    q_weight,
    kv_weight,
    out_weight,
    gate_weight,
    up_weight,
    down_weight,
    kv_cache,
    lengths,
):
    gx, gy, gz = (lax.axis_size(axis) for axis in ("gx", "gy", "gz"))
    seqs, width = tokens.shape
    seq_dev = lengths.shape[0]
    head_dim = kv_weight.shape[1] // 2
    q_dev = q_weight.shape[1]
    ff_dev = gate_weight.shape[1]
    each = seq_dev + 1
    rows = gy * each
    count = q_dev // head_dim * each
    lanes = -(-seqs * 6 // 128) * 128

    caches = with_others(kv_cache, "gz")

    exponents = pl.pallas_call(
        exponent_kernel,
        out_shape=jax.ShapeDtypeStruct((1, head_dim // 2), F32),
        out_specs=VMEM,
        compiler_params=params(LIMIT),
        cost_estimate=cost(7e9, 0),
        name="exponents",
    )()
    sums, lhs = pl.pallas_call(
        functools.partial(first_kernel, (gy, seq_dev)),
        out_shape=(
            jax.ShapeDtypeStruct((rows, q_dev + 2 * head_dim + lanes), BF16),
            jax.ShapeDtypeStruct((rows, width), BF16),
        ),
        in_specs=[VMEM] * 4 + [ANY],
        out_specs=(VMEM, VMEM),
        scratch_shapes=[pltpu.VMEM((rows, width), F32)],
        compiler_params=params(LIMIT),
        cost_estimate=cost(7e9, 0),
        name="norm_query",
    )(tokens, norm_gain[None, :], q_weight, kv_weight, exponents)
    sums = with_others(sums, "gx")

    gate = pl.pallas_call(
        gate_kernel,
        out_shape=jax.ShapeDtypeStruct((rows, ff_dev), BF16),
        in_specs=[VMEM, VMEM],
        out_specs=VMEM,
        compiler_params=params(LIMIT),
        cost_estimate=cost(6e9, 16.8e6),
        name="gate",
    )(lhs, gate_weight)
    query, keyval, stats = pl.pallas_call(
        functools.partial(query_kernel, (gx, gy, seq_dev, q_dev, gx * width)),
        out_shape=(
            jax.ShapeDtypeStruct((rows, q_dev), BF16),
            jax.ShapeDtypeStruct((rows, 2 * head_dim), F32),
            jax.ShapeDtypeStruct((gx + 1, rows, 128), F32),
        ),
        in_specs=[VMEM] * gx,
        out_specs=(VMEM,) * 3,
        compiler_params=params(LIMIT),
        cost_estimate=cost(1e8, 1e5),
        name="query_sum",
    )(*sums)
    queries = with_others(query, "gy")
    both = pl.pallas_call(
        up_kernel,
        out_shape=jax.ShapeDtypeStruct((2 * rows, ff_dev), BF16),
        in_specs=[VMEM] * 3 + [ANY],
        out_specs=VMEM,
        compiler_params=params(LIMIT),
        cost_estimate=cost(6e9, 16.8e6),
        name="up",
    )(lhs, up_weight, gate, query)
    parts = with_others(both, "gx")

    angle = lengths.astype(F32)[:, None] * rotary_base**exponents
    angle = jnp.pad(angle, ((0, 1), (0, 0)))
    tables = jnp.stack([jnp.cos(angle), jnp.sin(angle)])
    *pieces, new_kv = pl.pallas_call(
        functools.partial(attention_kernel, (gy, gz, seq_dev)),
        out_shape=(jax.ShapeDtypeStruct((count, head_dim), BF16),) * gy
        + (jax.ShapeDtypeStruct((seq_dev, 2 * head_dim), BF16),),
        in_specs=[VMEM] * (gz + gy) + [SMEM, VMEM, VMEM, ANY],
        out_specs=(VMEM,) * (gy + 1),
        scratch_shapes=[pltpu.VMEM((gy * count, head_dim), F32)] * 3,
        compiler_params=params(LIMIT),
        cost_estimate=cost(7e9, 2e6),
        name="attention",
    )(*queries, *caches, lengths, keyval, tables, both)
    pieces = pieces[:1] + [
        lax.ppermute(pieces[step], "gy", [(place, place ^ step) for place in range(gy)])
        for step in range(1, gy)
    ]
    pieces = with_others(jnp.stack(pieces), "gx")

    partial = pl.pallas_call(
        functools.partial(down_kernel, (gx, seq_dev)),
        out_shape=jax.ShapeDtypeStruct((rows, width), F32),
        in_specs=[VMEM] * (gx + 2),
        out_specs=VMEM,
        scratch_shapes=[pltpu.VMEM((rows, ff_dev), BF16)],
        compiler_params=params(LIMIT),
        cost_estimate=cost(4e9, 16.8e6),
        name="hidden_down",
    )(stats, *parts, down_weight)
    total, share = pl.pallas_call(
        functools.partial(out_kernel, (gx, gy, seq_dev)),
        out_shape=(
            jax.ShapeDtypeStruct((seqs, width), F32),
            jax.ShapeDtypeStruct((seqs, width), BF16),
        ),
        in_specs=[VMEM] * (gx + 2),
        out_specs=(VMEM, VMEM),
        scratch_shapes=[pltpu.VMEM((gy, each, q_dev), F32), pltpu.VMEM((rows, q_dev), F32)],
        compiler_params=params(LIMIT if gx <= FEW else 4 * LIMIT),
        cost_estimate=cost(1e9, 4e6),
        name="out_projection",
    )(*pieces, out_weight, partial)
    for other in with_others(share, ("gy", "gz"))[1:]:
        total = total + other.astype(F32)
    mixed = (tokens.astype(F32) + total).astype(BF16)
    return (mixed, new_kv)


def solution(mesh):
    in_specs = (
        P("group", "gx"),
        P("gx"),
        P("gx", ("gy", "gz")),
        P("gx", None),
        P(("gy", "gz"), "gx"),
        P("gx", ("gy", "gz")),
        P("gx", ("gy", "gz")),
        P(("gy", "gz"), "gx"),
        P(("group", "gy"), ("gx", "gz"), None),
        P(("group", "gy")),
    )
    out_specs = (P("group", "gx"), P(("group", "gy"), None))
    return jax.shard_map(body, mesh=mesh, in_specs=in_specs, out_specs=out_specs, check_vma=False)
```

time: 45.6 us -> 42.9 us (0.941)
  starting transfers between devices: 19.9 us -> 18.4 us
  waiting for transfers between devices: 7.98 us -> 6.8 us
    ppermute x15 -> x14, waiting for transfers between devices: 5.84 us -> 3.68 us  [with_others(): lax.ppermute(values, axis, [(place, place ^ step) for place in range(size)])]
    ppermute x3 -> x1, starting transfers between devices: 2.43 us -> 0.54 us  [body(): lax.ppermute(pieces[step], 'gy', [(place, place ^ step) for place in rang...]
    ppermute x3 -> x1, waiting for transfers between devices: 2.14 us -> 3.11 us  [body(): lax.ppermute(pieces[step], 'gy', [(place, place ^ step) for place in rang...]
    ppermute x15 -> x14, starting transfers between devices: 17.5 us -> 17.9 us  [with_others(): lax.ppermute(values, axis, [(place, place ^ step) for place in range(size)])]
  transfers between devices with their start and end apart: 18 -> 15, of which waited for: 6 -> 5; matrix products, arithmetic and copies ran while one was open for 0% -> 0% of each run, Pallas kernels for 24% -> 26%
where the time goes in v4:
time: 42.9 us; the launch traced here: 42.8 us
  starting transfers between devices  18.4 us (43%)
  Pallas kernels  12.8 us (30%)
  waiting for transfers between devices  6.8 us (16%)
  local copies, waits for them, and re-layouts  3.14 us (7%)
  between operations  0.9 us (2%)
  other arithmetic  0.73 us (2%)
    ppermute x14, starting transfers between devices, with_others(): lax.ppermute(values, axis, [(place, place ^ step) for place in range(size)])  17.9 us
    ppermute x14, waiting for transfers between devices, with_others(): lax.ppermute(values, axis, [(place, place ^ step) for place in range(size)])  3.68 us
    ppermute x1, waiting for transfers between devices, body(): lax.ppermute(pieces[step], 'gy', [(place, place ^ step) for place in rang...  3.11 us
    pallas_call x1, Pallas kernels, body(): pl.pallas_call(up_kernel, out_shape=jax.ShapeDtypeStruct((2 * rows, ff_de...  3.1 us
    pallas_call x1, Pallas kernels, body(): pl.pallas_call(gate_kernel, out_shape=jax.ShapeDtypeStruct((rows, ff_dev)...  3.1 us
    unnamed x38, local copies, waits for them, and re-layouts  3.09 us
    pallas_call x1, Pallas kernels, body(): pl.pallas_call(functools.partial(down_kernel, (gx, seq_dev)), out_shape=j...  2.89 us
    pallas_call x1, Pallas kernels, body(): pl.pallas_call(functools.partial(attention_kernel, (gy, gz, seq_dev)), ou...  1.78 us
  transfers between devices with their start and end apart: 15, of which 5 were waited for; matrix products, arithmetic and copies ran while one was open for 0% of the time, Pallas kernels for 26%

profile of v4, /device:TPU:0, one launch (start us, length us, event | category | flops | bytes accessed | tf_op | source)
XLA Modules:
  0.0 42.8 jit_solution(1597927927207536759)
XLA Ops:
  0.7 0.7 %copy-done.1 = bf16[6,2048]{1,0:T(8,128)(2,1)S(1)} copy-done((bf16[6,2048]{1,0:T(8,128)(2,1)S(1)}, bf16[6,2048]{1,0:T(8,128)(2,1)}, u32[]{:S(2)}) %copy-start.1) | copy-done | bytes 24600
  1.4 1.1 %copy-done.3 = bf16[2048,512]{1,0:T(8,128)(2,1)S(1)} copy-done((bf16[2048,512]{1,0:T(8,128)(2,1)S(1)}, bf16[2048,512]{1,0:T(8,128)(2,1)}, u32[]{:S(2)}) %copy-start.3) | copy-done | bytes 2097176
  2.5 1.2 %copy-done.2 = bf16[2048,1024]{1,0:T(8,128)(2,1)S(1)} copy-done((bf16[2048,1024]{1,0:T(8,128)(2,1)S(1)}, bf16[2048,1024]{1,0:T(8,128)(2,1)}, u32[]{:S(2)}) %copy-start.2) | copy-done | bytes 4194328
  3.8 1.0 %norm_query.1 = (bf16[8,1664]{1,0:T(8,128)(2,1)S(1)}, bf16[8,2048]{1,0:T(8,128)(2,1)S(1)}) custom-call(bf16[6,2048]{1,0:T(8,128)(2,1)S(1)} %copy-done.1, f32[1,2048]{1,0:T(1,128)S(1)} %bitcast.16, bf16[2048,1024]{1,0:T(8,128)(2,1)S(1)} %copy-done.2, bf16[2048,512]{1,0:T(8,128)(2,1)S(1)} %copy-done.3, f32[1,128]{1,0:T(1,128)S(1)} %exponents.1.after), custom_call_target="tpu_custom_call" | custom-call | flops 7000000000 | tf_op jit(solution)/shard_map/norm_query/pallas_call | solution.py:339
  4.8 5.1 %collective-permute-start.2 = (bf16[8,1664]{1,0:T(8,128)(2,1)S(1)}, bf16[8,1664]{1,0:T(8,128)(2,1)S(1)}, u32[]{:S(2)}, u32[]{:S(2)}) collective-permute-start(bf16[8,1664]{1,0:T(8,128)(2,1)S(1)} %get-tuple-element.12.refs_0_), channel_id=1, source_target_pairs={{0,12},{4,8},{8,4},{12,0},{1,13},{5,9},{9,5},{13,1},{2,14},{6,10},... | collective-permute-start | bytes 79880 | tf_op jit(solution)/shard_map/ppermute | solution.py:298
  9.8 0.6 %collective-permute-start = (bf16[8,1664]{1,0:T(8,128)(2,1)S(1)}, bf16[8,1664]{1,0:T(8,128)(2,1)S(1)}, u32[]{:S(2)}, u32[]{:S(2)}) collective-permute-start(bf16[8,1664]{1,0:T(8,128)(2,1)S(1)} %get-tuple-element.12.refs_0_), channel_id=1, source_target_pairs={{0,4},{4,0},{8,12},{12,8},{1,5},{5,1},{9,13},{13,9},{2,6},{6,2},{1... | collective-permute-start | bytes 79880 | tf_op jit(solution)/shard_map/ppermute | solution.py:298
  10.6 3.1 %gate.1 = bf16[8,4096]{1,0:T(8,128)(2,1)S(1)} custom-call(bf16[8,2048]{1,0:T(8,128)(2,1)S(1)} %get-tuple-element.15.lhs, bf16[2048,4096]{1,0:T(8,128)(2,1)S(1)} %bitcast.13), custom_call_target="tpu_custom_call" | custom-call | flops 6000000000 | bytes 16800000 | tf_op jit(solution)/shard_map/gate/pallas_call | solution.py:354
  13.7 0.8 %collective-permute-done.1.refs_2_ = bf16[8,1664]{1,0:T(8,128)(2,1)S(1)} collective-permute-done((bf16[8,1664]{1,0:T(8,128)(2,1)S(1)}, bf16[8,1664]{1,0:T(8,128)(2,1)S(1)}, u32[]{:S(2)}, u32[]{:S(2)}) %collective-permute-start.1) | collective-permute-done | bytes 26656 | tf_op jit(solution)/shard_map/ppermute | solution.py:298
  14.7 1.6 %collective-permute-start.3 = (bf16[8,1024]{1,0:T(8,128)(2,1)S(1)}, bf16[8,1024]{1,0:T(8,128)(2,1)S(1)}, u32[]{:S(2)}, u32[]{:S(2)}) collective-permute-start(bf16[8,1024]{1,0:T(8,128)(2,1)S(1)} %get-tuple-element.13.after.refs_0_), channel_id=1, source_target_pairs={{0,2},{2,0},{1,3},{3,1},{4,6},{6,4},{5,7},{7,5},{8,10},{10,8},{9,1... | collective-permute-start | bytes 49160 | tf_op jit(solution)/shard_map/ppermute | solution.py:298
  16.3 3.1 %up.1.refs_7_.refs_0_ = bf16[16,4096]{1,0:T(8,128)(2,1)S(1)} custom-call(bf16[8,2048]{1,0:T(8,128)(2,1)S(1)} %get-tuple-element.15.lhs, bf16[2048,4096]{1,0:T(8,128)(2,1)S(1)} %bitcast.15, bf16[8,4096]{1,0:T(8,128)(2,1)S(1)} %gate.1, bf16[8,1024]{1,0:T(8,128)(2,1)S(1)} %get-tuple-element.13.after.refs_0_), custom_call_target="tpu_custom_call" | custom-call | flops 6000000000 | bytes 16800000 | tf_op jit(solution)/shard_map/up/pallas_call | solution.py:377
  19.4 3.0 %collective-permute-start.11 = (bf16[16,4096]{1,0:T(8,128)(2,1)S(1)}, bf16[16,4096]{1,0:T(8,128)(2,1)S(1)}, u32[]{:S(2)}, u32[]{:S(2)}) collective-permute-start(bf16[16,4096]{1,0:T(8,128)(2,1)S(1)} %up.1.refs_7_.refs_0_), channel_id=1, source_target_pairs={{0,12},{4,8},{8,4},{12,0},{1,13},{5,9},{9,5},{13,1},{2,14},{6,10},... | collective-permute-start | bytes 393224 | tf_op jit(solution)/shard_map/ppermute | solution.py:298
  22.4 1.4 %collective-permute-start.9 = (bf16[16,4096]{1,0:T(8,128)(2,1)S(1)}, bf16[16,4096]{1,0:T(8,128)(2,1)S(1)}, u32[]{:S(2)}, u32[]{:S(2)}) collective-permute-start(bf16[16,4096]{1,0:T(8,128)(2,1)S(1)} %up.1.refs_7_.refs_0_), channel_id=1, source_target_pairs={{0,4},{4,0},{8,12},{12,8},{1,5},{5,1},{9,13},{13,9},{2,6},{6,2},{1... | collective-permute-start | bytes 393224 | tf_op jit(solution)/shard_map/ppermute | solution.py:298
  23.8 1.8 %attention.1 = (bf16[16,256]{1,0:T(8,128)(2,1)S(1)}, bf16[16,256]{1,0:T(8,128)(2,1)S(1)}, bf16[3,512]{1,0:T(4,128)(2,1)}) custom-call(bf16[8,1024]{1,0:T(8,128)(2,1)S(1)} %get-tuple-element.13.after.refs_0_, bf16[8,1024]{1,0:T(8,128)(2,1)S(1)} %collective-permute-done.3.refs_1_, bf16[3,256,512]{2,1,0:T(8,128)(2,1)S(1)} %copy-done.4, ...), custom_call_target="tpu_custom_call" | custom-call | flops 7000000000 | bytes 2000000 | tf_op jit(solution)/shard_map/attention/pallas_call | solution.py:391
  25.6 0.5 %collective-permute-start.5 = (bf16[16,256]{1,0:T(8,128)(2,1)S(1)}, bf16[16,256]{1,0:T(8,128)(2,1)S(1)}, u32[]{:S(2)}, u32[]{:S(2)}) collective-permute-start(bf16[16,256]{1,0:T(8,128)(2,1)S(1)} %get-tuple-element.17), channel_id=1, source_target_pairs={{0,2},{2,0},{1,3},{3,1},{4,6},{6,4},{5,7},{7,5},{8,10},{10,8},{9,1... | collective-permute-start | bytes 24584 | tf_op jit(solution)/shard_map/ppermute | solution.py:403
  26.2 3.1 %collective-permute-done.5 = bf16[16,256]{1,0:T(8,128)(2,1)S(1)} collective-permute-done((bf16[16,256]{1,0:T(8,128)(2,1)S(1)}, bf16[16,256]{1,0:T(8,128)(2,1)S(1)}, u32[]{:S(2)}, u32[]{:S(2)}) %collective-permute-start.5) | collective-permute-done | bytes 8224 | tf_op jit(solution)/shard_map/ppermute | solution.py:403
  29.3 3.0 %collective-permute-start.8 = (bf16[2,16,256]{2,1,0:T(8,128)(2,1)S(1)}, bf16[2,16,256]{2,1,0:T(8,128)(2,1)S(1)}, u32[]{:S(2)}, u32[]{:S(2)}) collective-permute-start(bf16[2,16,256]{2,1,0:T(8,128)(2,1)S(1)} %pad_maximum_fusion.refs_0_), channel_id=1, source_target_pairs={{0,12},{4,8},{8,4},{12,0},{1,13},{5,9},{9,5},{13,1},{2,14},{6,10},... | collective-permute-start | bytes 49160 | tf_op jit(solution)/shard_map/ppermute | solution.py:298
  32.3 1.4 %collective-permute-start.6 = (bf16[2,16,256]{2,1,0:T(8,128)(2,1)S(1)}, bf16[2,16,256]{2,1,0:T(8,128)(2,1)S(1)}, u32[]{:S(2)}, u32[]{:S(2)}) collective-permute-start(bf16[2,16,256]{2,1,0:T(8,128)(2,1)S(1)} %pad_maximum_fusion.refs_0_), channel_id=1, source_target_pairs={{0,4},{4,0},{8,12},{12,8},{1,5},{5,1},{9,13},{13,9},{2,6},{6,2},{1... | collective-permute-start | bytes 49160 | tf_op jit(solution)/shard_map/ppermute | solution.py:298
  34.1 2.9 %hidden_down.1.refs_5_ = f32[8,2048]{1,0:T(8,128)S(1)} custom-call(f32[5,8,128]{2,1,0:T(8,128)S(1)} %get-tuple-element.18.stats, bf16[16,4096]{1,0:T(8,128)(2,1)S(1)} %up.1.refs_7_.refs_0_, bf16[16,4096]{1,0:T(8,128)(2,1)S(1)} %collective-permute-done.9.refs_1_, bf16[16,4096]{1,0:T(8,128)(2,1)S(1)} %collective-permute-done.10.refs_2_, ...), custom_call_target="tpu_custom_call" | custom-call | flops 4000000000 | bytes 16800000 | tf_op jit(solution)/shard_map/hidden_down/pallas_call | solution.py:408
  37.0 0.8 %out_projection.1 = (f32[6,2048]{1,0:T(8,128)S(1)}, bf16[6,2048]{1,0:T(8,128)(2,1)S(1)}) custom-call(bf16[2,16,256]{2,1,0:T(8,128)(2,1)S(1)} %pad_maximum_fusion.refs_0_, bf16[2,16,256]{2,1,0:T(8,128)(2,1)S(1)} %collective-permute-done.6.refs_1_, bf16[2,16,256]{2,1,0:T(8,128)(2,1)S(1)} %collective-permute-done.7.refs_2_, ...), custom_call_target="tpu_custom_call" | custom-call | flops 1000000000 | bytes 4000000 | tf_op jit(solution)/shard_map/out_projection/pallas_call | solution.py:418
  37.9 1.0 %collective-permute-start.13 = (bf16[6,2048]{1,0:T(8,128)(2,1)S(1)}, bf16[6,2048]{1,0:T(8,128)(2,1)S(1)}, u32[]{:S(2)}, u32[]{:S(2)}) collective-permute-start(bf16[6,2048]{1,0:T(8,128)(2,1)S(1)} %get-tuple-element.20), channel_id=1, source_target_pairs={{0,2},{1,3},{2,0},{3,1},{4,6},{5,7},{6,4},{7,5},{8,10},{9,11},{10,... | collective-permute-start | bytes 73736 | tf_op jit(solution)/shard_map/ppermute | solution.py:298
  38.9 0.8 %collective-permute-start.12 = (bf16[6,2048]{1,0:T(8,128)(2,1)S(1)}, bf16[6,2048]{1,0:T(8,128)(2,1)S(1)}, u32[]{:S(2)}, u32[]{:S(2)}) collective-permute-start(bf16[6,2048]{1,0:T(8,128)(2,1)S(1)} %get-tuple-element.20), channel_id=1, source_target_pairs={{0,1},{1,0},{2,3},{3,2},{4,5},{5,4},{6,7},{7,6},{8,9},{9,8},{10,11... | collective-permute-start | bytes 73736 | tf_op jit(solution)/shard_map/ppermute | solution.py:298
  39.7 1.5 %collective-permute-done.14 = bf16[6,2048]{1,0:T(8,128)(2,1)S(1)} collective-permute-done((bf16[6,2048]{1,0:T(8,128)(2,1)S(1)}, bf16[6,2048]{1,0:T(8,128)(2,1)S(1)}, u32[]{:S(2)}, u32[]{:S(2)}) %collective-permute-start.14) | collective-permute-done | bytes 24608 | tf_op jit(solution)/shard_map/ppermute | solution.py:298
  41.2 1.0 %collective-permute-done.13 = bf16[6,2048]{1,0:T(8,128)(2,1)S(1)} collective-permute-done((bf16[6,2048]{1,0:T(8,128)(2,1)S(1)}, bf16[6,2048]{1,0:T(8,128)(2,1)S(1)}, u32[]{:S(2)}, u32[]{:S(2)}) %collective-permute-start.13) | collective-permute-done | bytes 24608 | tf_op jit(solution)/shard_map/ppermute | solution.py:298
  42.2 0.6 %add_convert_fusion = bf16[6,2048]{1,0:T(8,128)(2,1)} fusion(bf16[6,2048]{1,0:T(8,128)(2,1)S(1)} %collective-permute-done.14, bf16[6,2048]{1,0:T(8,128)(2,1)S(1)} %collective-permute-done.13, f32[6,2048]{1,0:T(8,128)S(1)} %get-tuple-element.19, bf16[6,2048]{1,0:T(8,128)(2,1)S(1)} %collective-permute-done.12, bf16[6,2048]{1,0:T(8,128)(2,1)S(1)} %copy-done.1), kind=kLoop, calls=%fused_computation | loop fusion | flops 110592 | bytes 172032 | tf_op jit(solution)/shard_map/convert_element_type | solution.py:433
  (62 shorter events, 0.8 us)
Async XLA Ops:
  0.7 9.9 %slice-start.4 = ((s8[16777216]{0:T(1024)(128)(4,1)}), s8[4194304]{0:T(1024)(128)(4,1)S(1)}, s32[]{:S(2)}) async-start(s8[16777216]{0:T(1024)(128)(4,1)} %bitcast.12), calls=%async_computation.4 | async-start | bytes 8388608
  3.7 12.5 %slice-start.8 = ((s8[16777216]{0:T(1024)(128)(4,1)}), s8[4194304]{0:T(1024)(128)(4,1)S(1)}, s32[]{:S(2)}) async-start(s8[16777216]{0:T(1024)(128)(4,1)} %bitcast.14), calls=%async_computation.8 | async-start | bytes 8388608
  3.7 12.5 %slice-start.9 = ((s8[16777216]{0:T(1024)(128)(4,1)}), s8[4194304]{0:T(1024)(128)(4,1)S(1)}, s32[]{:S(2)}) async-start(s8[16777216]{0:T(1024)(128)(4,1)} %bitcast.14), calls=%async_computation.9 | async-start | bytes 8388608
  3.7 12.5 %slice-start.10 = ((s8[16777216]{0:T(1024)(128)(4,1)}), s8[4194304]{0:T(1024)(128)(4,1)S(1)}, s32[]{:S(2)}) async-start(s8[16777216]{0:T(1024)(128)(4,1)} %bitcast.14), calls=%async_computation.10 | async-start | bytes 8388608
  4.8 9.0 %collective-permute-start.2 = (bf16[8,1664]{1,0:T(8,128)(2,1)S(1)}, bf16[8,1664]{1,0:T(8,128)(2,1)S(1)}, u32[]{:S(2)}, u32[]{:S(2)}) collective-permute-start(bf16[8,1664]{1,0:T(8,128)(2,1)S(1)} %get-tuple-element.12.refs_0_), channel_id=1, source_target_pairs={{0,12},{4,8},{8,4},{12,0},{1,13},{5,9},{9,5},{13,1},{2,14},{6,10},... | collective-permute-start | bytes 79880 | tf_op jit(solution)/shard_map/ppermute | solution.py:298
  9.8 4.7 %collective-permute-start.1 = (bf16[8,1664]{1,0:T(8,128)(2,1)S(1)}, bf16[8,1664]{1,0:T(8,128)(2,1)S(1)}, u32[]{:S(2)}, u32[]{:S(2)}) collective-permute-start(bf16[8,1664]{1,0:T(8,128)(2,1)S(1)} %get-tuple-element.12.refs_0_), channel_id=1, source_target_pairs={{0,8},{4,12},{8,0},{12,4},{1,9},{5,13},{9,1},{13,5},{2,10},{6,14},... | collective-permute-start | bytes 79880 | tf_op jit(solution)/shard_map/ppermute | solution.py:298
  9.8 4.7 %collective-permute-start = (bf16[8,1664]{1,0:T(8,128)(2,1)S(1)}, bf16[8,1664]{1,0:T(8,128)(2,1)S(1)}, u32[]{:S(2)}, u32[]{:S(2)}) collective-permute-start(bf16[8,1664]{1,0:T(8,128)(2,1)S(1)} %get-tuple-element.12.refs_0_), channel_id=1, source_target_pairs={{0,4},{4,0},{8,12},{12,8},{1,5},{5,1},{9,13},{13,9},{2,6},{6,2},{1... | collective-permute-start | bytes 79880 | tf_op jit(solution)/shard_map/ppermute | solution.py:298
  10.4 13.4 %collective-permute-start.4 = (bf16[3,256,512]{2,1,0:T(8,128)(2,1)S(1)}, bf16[3,256,512]{2,1,0:T(8,128)(2,1)S(1)}, u32[]{:S(2)}, u32[]{:S(2)}) collective-permute-start(bf16[3,256,512]{2,1,0:T(8,128)(2,1)S(1)} %copy-done.4), channel_id=1, source_target_pairs={{0,1},{1,0},{2,3},{3,2},{4,5},{5,4},{6,7},{7,6},{8,9},{9,8},{10,11... | collective-permute-start | bytes 2359304 | tf_op jit(solution)/shard_map/ppermute | solution.py:298
  14.7 9.1 %collective-permute-start.3 = (bf16[8,1024]{1,0:T(8,128)(2,1)S(1)}, bf16[8,1024]{1,0:T(8,128)(2,1)S(1)}, u32[]{:S(2)}, u32[]{:S(2)}) collective-permute-start(bf16[8,1024]{1,0:T(8,128)(2,1)S(1)} %get-tuple-element.13.after.refs_0_), channel_id=1, source_target_pairs={{0,2},{2,0},{1,3},{3,1},{4,6},{6,4},{5,7},{7,5},{8,10},{10,8},{9,1... | collective-permute-start | bytes 49160 | tf_op jit(solution)/shard_map/ppermute | solution.py:298
  16.3 17.8 %slice-start = ((s8[16777216]{0:T(1024)(128)(4,1)}), s8[4194304]{0:T(1024)(128)(4,1)S(1)}, s32[]{:S(2)}) async-start(s8[16777216]{0:T(1024)(128)(4,1)} %bitcast.9), calls=%async_computation | async-start | bytes 8388608
  16.3 17.8 %slice-start.1 = ((s8[16777216]{0:T(1024)(128)(4,1)}), s8[4194304]{0:T(1024)(128)(4,1)S(1)}, s32[]{:S(2)}) async-start(s8[16777216]{0:T(1024)(128)(4,1)} %bitcast.9), calls=%async_computation.1 | async-start | bytes 8388608
  19.4 12.9 %collective-permute-start.11 = (bf16[16,4096]{1,0:T(8,128)(2,1)S(1)}, bf16[16,4096]{1,0:T(8,128)(2,1)S(1)}, u32[]{:S(2)}, u32[]{:S(2)}) collective-permute-start(bf16[16,4096]{1,0:T(8,128)(2,1)S(1)} %up.1.refs_7_.refs_0_), channel_id=1, source_target_pairs={{0,12},{4,8},{8,4},{12,0},{1,13},{5,9},{9,5},{13,1},{2,14},{6,10},... | collective-permute-start | bytes 393224 | tf_op jit(solution)/shard_map/ppermute | solution.py:298
  22.4 11.6 %collective-permute-start.10 = (bf16[16,4096]{1,0:T(8,128)(2,1)S(1)}, bf16[16,4096]{1,0:T(8,128)(2,1)S(1)}, u32[]{:S(2)}, u32[]{:S(2)}) collective-permute-start(bf16[16,4096]{1,0:T(8,128)(2,1)S(1)} %up.1.refs_7_.refs_0_), channel_id=1, source_target_pairs={{0,8},{4,12},{8,0},{12,4},{1,9},{5,13},{9,1},{13,5},{2,10},{6,14},... | collective-permute-start | bytes 393224 | tf_op jit(solution)/shard_map/ppermute | solution.py:298
  22.4 11.6 %collective-permute-start.9 = (bf16[16,4096]{1,0:T(8,128)(2,1)S(1)}, bf16[16,4096]{1,0:T(8,128)(2,1)S(1)}, u32[]{:S(2)}, u32[]{:S(2)}) collective-permute-start(bf16[16,4096]{1,0:T(8,128)(2,1)S(1)} %up.1.refs_7_.refs_0_), channel_id=1, source_target_pairs={{0,4},{4,0},{8,12},{12,8},{1,5},{5,1},{9,13},{13,9},{2,6},{6,2},{1... | collective-permute-start | bytes 393224 | tf_op jit(solution)/shard_map/ppermute | solution.py:298
  23.8 10.2 %slice-start.2 = ((s8[16777216]{0:T(1024)(128)(4,1)}), s8[4194304]{0:T(1024)(128)(4,1)S(1)}, s32[]{:S(2)}) async-start(s8[16777216]{0:T(1024)(128)(4,1)} %bitcast.9), calls=%async_computation.2 | async-start | bytes 8388608
  23.8 10.2 %slice-start.3 = ((s8[16777216]{0:T(1024)(128)(4,1)}), s8[4194304]{0:T(1024)(128)(4,1)S(1)}, s32[]{:S(2)}) async-start(s8[16777216]{0:T(1024)(128)(4,1)} %bitcast.9), calls=%async_computation.3 | async-start | bytes 8388608
  23.8 13.2 %copy-start = (bf16[1024,2048]{1,0:T(8,128)(2,1)S(1)}, bf16[1024,2048]{1,0:T(8,128)(2,1)}, u32[]{:S(2)}) copy-start(bf16[1024,2048]{1,0:T(8,128)(2,1)} %refs_4_.5) | copy-start | bytes 12582916
  25.6 3.7 %collective-permute-start.5 = (bf16[16,256]{1,0:T(8,128)(2,1)S(1)}, bf16[16,256]{1,0:T(8,128)(2,1)S(1)}, u32[]{:S(2)}, u32[]{:S(2)}) collective-permute-start(bf16[16,256]{1,0:T(8,128)(2,1)S(1)} %get-tuple-element.17), channel_id=1, source_target_pairs={{0,2},{2,0},{1,3},{3,1},{4,6},{6,4},{5,7},{7,5},{8,10},{10,8},{9,1... | collective-permute-start | bytes 24584 | tf_op jit(solution)/shard_map/ppermute | solution.py:403
  29.3 7.7 %collective-permute-start.8 = (bf16[2,16,256]{2,1,0:T(8,128)(2,1)S(1)}, bf16[2,16,256]{2,1,0:T(8,128)(2,1)S(1)}, u32[]{:S(2)}, u32[]{:S(2)}) collective-permute-start(bf16[2,16,256]{2,1,0:T(8,128)(2,1)S(1)} %pad_maximum_fusion.refs_0_), channel_id=1, source_target_pairs={{0,12},{4,8},{8,4},{12,0},{1,13},{5,9},{9,5},{13,1},{2,14},{6,10},... | collective-permute-start | bytes 49160 | tf_op jit(solution)/shard_map/ppermute | solution.py:298
  32.3 4.7 %collective-permute-start.7 = (bf16[2,16,256]{2,1,0:T(8,128)(2,1)S(1)}, bf16[2,16,256]{2,1,0:T(8,128)(2,1)S(1)}, u32[]{:S(2)}, u32[]{:S(2)}) collective-permute-start(bf16[2,16,256]{2,1,0:T(8,128)(2,1)S(1)} %pad_maximum_fusion.refs_0_), channel_id=1, source_target_pairs={{0,8},{4,12},{8,0},{12,4},{1,9},{5,13},{9,1},{13,5},{2,10},{6,14},... | collective-permute-start | bytes 49160 | tf_op jit(solution)/shard_map/ppermute | solution.py:298
  32.3 4.7 %collective-permute-start.6 = (bf16[2,16,256]{2,1,0:T(8,128)(2,1)S(1)}, bf16[2,16,256]{2,1,0:T(8,128)(2,1)S(1)}, u32[]{:S(2)}, u32[]{:S(2)}) collective-permute-start(bf16[2,16,256]{2,1,0:T(8,128)(2,1)S(1)} %pad_maximum_fusion.refs_0_), channel_id=1, source_target_pairs={{0,4},{4,0},{8,12},{12,8},{1,5},{5,1},{9,13},{13,9},{2,6},{6,2},{1... | collective-permute-start | bytes 49160 | tf_op jit(solution)/shard_map/ppermute | solution.py:298
  37.8 3.4 %collective-permute-start.14 = (bf16[6,2048]{1,0:T(8,128)(2,1)S(1)}, bf16[6,2048]{1,0:T(8,128)(2,1)S(1)}, u32[]{:S(2)}, u32[]{:S(2)}) collective-permute-start(bf16[6,2048]{1,0:T(8,128)(2,1)S(1)} %get-tuple-element.20), channel_id=1, source_target_pairs={{0,3},{1,2},{2,1},{3,0},{4,7},{5,6},{6,5},{7,4},{8,11},{9,10},{10,... | collective-permute-start | bytes 73736 | tf_op jit(solution)/shard_map/ppermute | solution.py:298
  37.9 4.3 %collective-permute-start.13 = (bf16[6,2048]{1,0:T(8,128)(2,1)S(1)}, bf16[6,2048]{1,0:T(8,128)(2,1)S(1)}, u32[]{:S(2)}, u32[]{:S(2)}) collective-permute-start(bf16[6,2048]{1,0:T(8,128)(2,1)S(1)} %get-tuple-element.20), channel_id=1, source_target_pairs={{0,2},{1,3},{2,0},{3,1},{4,6},{5,7},{6,4},{7,5},{8,10},{9,11},{10,... | collective-permute-start | bytes 73736 | tf_op jit(solution)/shard_map/ppermute | solution.py:298
  38.9 3.3 %collective-permute-start.12 = (bf16[6,2048]{1,0:T(8,128)(2,1)S(1)}, bf16[6,2048]{1,0:T(8,128)(2,1)S(1)}, u32[]{:S(2)}, u32[]{:S(2)}) collective-permute-start(bf16[6,2048]{1,0:T(8,128)(2,1)S(1)} %get-tuple-element.20), channel_id=1, source_target_pairs={{0,1},{1,0},{2,3},{3,2},{4,5},{5,4},{6,7},{7,6},{8,9},{9,8},{10,11... | collective-permute-start | bytes 73736 | tf_op jit(solution)/shard_map/ppermute | solution.py:298
  (10 other events, 57.4 us)

commit v5 on v4

--- a/solution.py
+++ b/solution.py
@@ -110,15 +110,10 @@
     return total
 
 
-def product(lhs, weight, store, slab=512):
-    slab = min(slab, weight.shape[1])
-
-    def step(index, _):
-        part = pl.ds(pl.multiple_of(index * slab, slab), slab)
+def product(lhs, weight, store, slab=1024):
+    for start in range(0, weight.shape[1], slab):
+        part = slice(start, min(start + slab, weight.shape[1]))
         store(part, jnp.dot(lhs, weight[:, part], preferred_element_type=F32))
-        return 0
-
-    lax.fori_loop(0, weight.shape[1] // slab, step, 0)
 
 
 def gate_kernel(lhs, weight, sums):

time: 42.9 us -> 41 us (0.956)
  Pallas kernels: 12.8 us -> 10.6 us
    pallas_call x1, Pallas kernels: 3.1 us -> 2.27 us  [body(): pl.pallas_call(up_kernel, out_shape=jax.ShapeDtypeStruct((2 * rows, ff_de...]
    pallas_call x1, Pallas kernels: 3.1 us -> 2.28 us  [body(): pl.pallas_call(gate_kernel, out_shape=jax.ShapeDtypeStruct((rows, ff_dev)...]
    pallas_call x1, Pallas kernels: 2.89 us -> 2.35 us  [body(): pl.pallas_call(functools.partial(down_kernel, (gx, seq_dev)), out_shape=j...]
  transfers between devices with their start and end apart: 15 -> 15, of which waited for: 5 -> 5; matrix products, arithmetic and copies ran while one was open for 0% -> 0% of each run, Pallas kernels for 26% -> 22%
where the time goes in v5:
time: 41 us; the launch traced here: 40.9 us
  starting transfers between devices  18.4 us (45%)
  Pallas kernels  10.6 us (26%)
  waiting for transfers between devices  7.11 us (17%)
  local copies, waits for them, and re-layouts  3.14 us (8%)
  between operations  0.9 us (2%)
  other arithmetic  0.73 us (2%)
    ppermute x14, starting transfers between devices, with_others(): lax.ppermute(values, axis, [(place, place ^ step) for place in range(size)])  17.9 us
    ppermute x14, waiting for transfers between devices, with_others(): lax.ppermute(values, axis, [(place, place ^ step) for place in range(size)])  3.99 us
    ppermute x1, waiting for transfers between devices, body(): lax.ppermute(pieces[step], 'gy', [(place, place ^ step) for place in rang...  3.12 us
    unnamed x38, local copies, waits for them, and re-layouts  3.09 us
    pallas_call x1, Pallas kernels, body(): pl.pallas_call(functools.partial(down_kernel, (gx, seq_dev)), out_shape=j...  2.35 us
    pallas_call x1, Pallas kernels, body(): pl.pallas_call(gate_kernel, out_shape=jax.ShapeDtypeStruct((rows, ff_dev)...  2.28 us
    pallas_call x1, Pallas kernels, body(): pl.pallas_call(up_kernel, out_shape=jax.ShapeDtypeStruct((2 * rows, ff_de...  2.27 us
    pallas_call x1, Pallas kernels, body(): pl.pallas_call(functools.partial(attention_kernel, (gy, gz, seq_dev)), ou...  1.78 us
  transfers between devices with their start and end apart: 15, of which 5 were waited for; matrix products, arithmetic and copies ran while one was open for 0% of the time, Pallas kernels for 22%

profile of v5, /device:TPU:0, one launch (start us, length us, event | category | flops | bytes accessed | tf_op | source)
XLA Modules:
  0.0 40.9 jit_solution(7721691516105138660)
XLA Ops:
  0.7 0.7 %copy-done.1 = bf16[6,2048]{1,0:T(8,128)(2,1)S(1)} copy-done((bf16[6,2048]{1,0:T(8,128)(2,1)S(1)}, bf16[6,2048]{1,0:T(8,128)(2,1)}, u32[]{:S(2)}) %copy-start.1) | copy-done | bytes 24600
  1.4 1.1 %copy-done.3 = bf16[2048,512]{1,0:T(8,128)(2,1)S(1)} copy-done((bf16[2048,512]{1,0:T(8,128)(2,1)S(1)}, bf16[2048,512]{1,0:T(8,128)(2,1)}, u32[]{:S(2)}) %copy-start.3) | copy-done | bytes 2097176
  2.5 1.2 %copy-done.2 = bf16[2048,1024]{1,0:T(8,128)(2,1)S(1)} copy-done((bf16[2048,1024]{1,0:T(8,128)(2,1)S(1)}, bf16[2048,1024]{1,0:T(8,128)(2,1)}, u32[]{:S(2)}) %copy-start.2) | copy-done | bytes 4194328
  3.8 1.0 %norm_query.1 = (bf16[8,1664]{1,0:T(8,128)(2,1)S(1)}, bf16[8,2048]{1,0:T(8,128)(2,1)S(1)}) custom-call(bf16[6,2048]{1,0:T(8,128)(2,1)S(1)} %copy-done.1, f32[1,2048]{1,0:T(1,128)S(1)} %bitcast.16, bf16[2048,1024]{1,0:T(8,128)(2,1)S(1)} %copy-done.2, bf16[2048,512]{1,0:T(8,128)(2,1)S(1)} %copy-done.3, f32[1,128]{1,0:T(1,128)S(1)} %exponents.1.after), custom_call_target="tpu_custom_call" | custom-call | flops 7000000000 | tf_op jit(solution)/shard_map/norm_query/pallas_call | solution.py:334
  4.8 5.1 %collective-permute-start.2 = (bf16[8,1664]{1,0:T(8,128)(2,1)S(1)}, bf16[8,1664]{1,0:T(8,128)(2,1)S(1)}, u32[]{:S(2)}, u32[]{:S(2)}) collective-permute-start(bf16[8,1664]{1,0:T(8,128)(2,1)S(1)} %get-tuple-element.12.refs_0_), channel_id=1, source_target_pairs={{0,12},{4,8},{8,4},{12,0},{1,13},{5,9},{9,5},{13,1},{2,14},{6,10},... | collective-permute-start | bytes 79880 | tf_op jit(solution)/shard_map/ppermute | solution.py:293
  9.8 0.6 %collective-permute-start = (bf16[8,1664]{1,0:T(8,128)(2,1)S(1)}, bf16[8,1664]{1,0:T(8,128)(2,1)S(1)}, u32[]{:S(2)}, u32[]{:S(2)}) collective-permute-start(bf16[8,1664]{1,0:T(8,128)(2,1)S(1)} %get-tuple-element.12.refs_0_), channel_id=1, source_target_pairs={{0,4},{4,0},{8,12},{12,8},{1,5},{5,1},{9,13},{13,9},{2,6},{6,2},{1... | collective-permute-start | bytes 79880 | tf_op jit(solution)/shard_map/ppermute | solution.py:293
  10.6 2.3 %gate.1 = bf16[8,4096]{1,0:T(8,128)(2,1)S(1)} custom-call(bf16[8,2048]{1,0:T(8,128)(2,1)S(1)} %get-tuple-element.15.lhs, bf16[2048,4096]{1,0:T(8,128)(2,1)S(1)} %bitcast.13), custom_call_target="tpu_custom_call" | custom-call | flops 6000000000 | bytes 16800000 | tf_op jit(solution)/shard_map/gate/pallas_call | solution.py:349
  12.9 1.7 %collective-permute-done.1.refs_2_ = bf16[8,1664]{1,0:T(8,128)(2,1)S(1)} collective-permute-done((bf16[8,1664]{1,0:T(8,128)(2,1)S(1)}, bf16[8,1664]{1,0:T(8,128)(2,1)S(1)}, u32[]{:S(2)}, u32[]{:S(2)}) %collective-permute-start.1) | collective-permute-done | bytes 26656 | tf_op jit(solution)/shard_map/ppermute | solution.py:293
  14.7 1.6 %collective-permute-start.3 = (bf16[8,1024]{1,0:T(8,128)(2,1)S(1)}, bf16[8,1024]{1,0:T(8,128)(2,1)S(1)}, u32[]{:S(2)}, u32[]{:S(2)}) collective-permute-start(bf16[8,1024]{1,0:T(8,128)(2,1)S(1)} %get-tuple-element.13.after.refs_0_), channel_id=1, source_target_pairs={{0,2},{2,0},{1,3},{3,1},{4,6},{6,4},{5,7},{7,5},{8,10},{10,8},{9,1... | collective-permute-start | bytes 49160 | tf_op jit(solution)/shard_map/ppermute | solution.py:293
  16.3 2.3 %up.1.refs_7_.refs_0_ = bf16[16,4096]{1,0:T(8,128)(2,1)S(1)} custom-call(bf16[8,2048]{1,0:T(8,128)(2,1)S(1)} %get-tuple-element.15.lhs, bf16[2048,4096]{1,0:T(8,128)(2,1)S(1)} %bitcast.15, bf16[8,4096]{1,0:T(8,128)(2,1)S(1)} %gate.1, bf16[8,1024]{1,0:T(8,128)(2,1)S(1)} %get-tuple-element.13.after.refs_0_), custom_call_target="tpu_custom_call" | custom-call | flops 6000000000 | bytes 16800000 | tf_op jit(solution)/shard_map/up/pallas_call | solution.py:372
  18.6 2.3 %collective-permute-start.11 = (bf16[16,4096]{1,0:T(8,128)(2,1)S(1)}, bf16[16,4096]{1,0:T(8,128)(2,1)S(1)}, u32[]{:S(2)}, u32[]{:S(2)}) collective-permute-start(bf16[16,4096]{1,0:T(8,128)(2,1)S(1)} %up.1.refs_7_.refs_0_), channel_id=1, source_target_pairs={{0,12},{4,8},{8,4},{12,0},{1,13},{5,9},{9,5},{13,1},{2,14},{6,10},... | collective-permute-start | bytes 393224 | tf_op jit(solution)/shard_map/ppermute | solution.py:293
  20.9 2.1 %collective-permute-start.9 = (bf16[16,4096]{1,0:T(8,128)(2,1)S(1)}, bf16[16,4096]{1,0:T(8,128)(2,1)S(1)}, u32[]{:S(2)}, u32[]{:S(2)}) collective-permute-start(bf16[16,4096]{1,0:T(8,128)(2,1)S(1)} %up.1.refs_7_.refs_0_), channel_id=1, source_target_pairs={{0,4},{4,0},{8,12},{12,8},{1,5},{5,1},{9,13},{13,9},{2,6},{6,2},{1... | collective-permute-start | bytes 393224 | tf_op jit(solution)/shard_map/ppermute | solution.py:293
  23.0 1.8 %attention.1 = (bf16[16,256]{1,0:T(8,128)(2,1)S(1)}, bf16[16,256]{1,0:T(8,128)(2,1)S(1)}, bf16[3,512]{1,0:T(4,128)(2,1)}) custom-call(bf16[8,1024]{1,0:T(8,128)(2,1)S(1)} %get-tuple-element.13.after.refs_0_, bf16[8,1024]{1,0:T(8,128)(2,1)S(1)} %collective-permute-done.3.refs_1_, bf16[3,256,512]{2,1,0:T(8,128)(2,1)S(1)} %copy-done.4, ...), custom_call_target="tpu_custom_call" | custom-call | flops 7000000000 | bytes 2000000 | tf_op jit(solution)/shard_map/attention/pallas_call | solution.py:386
  24.8 0.5 %collective-permute-start.5 = (bf16[16,256]{1,0:T(8,128)(2,1)S(1)}, bf16[16,256]{1,0:T(8,128)(2,1)S(1)}, u32[]{:S(2)}, u32[]{:S(2)}) collective-permute-start(bf16[16,256]{1,0:T(8,128)(2,1)S(1)} %get-tuple-element.17), channel_id=1, source_target_pairs={{0,2},{2,0},{1,3},{3,1},{4,6},{6,4},{5,7},{7,5},{8,10},{10,8},{9,1... | collective-permute-start | bytes 24584 | tf_op jit(solution)/shard_map/ppermute | solution.py:398
  25.3 3.1 %collective-permute-done.5 = bf16[16,256]{1,0:T(8,128)(2,1)S(1)} collective-permute-done((bf16[16,256]{1,0:T(8,128)(2,1)S(1)}, bf16[16,256]{1,0:T(8,128)(2,1)S(1)}, u32[]{:S(2)}, u32[]{:S(2)}) %collective-permute-start.5) | collective-permute-done | bytes 8224 | tf_op jit(solution)/shard_map/ppermute | solution.py:398
  28.5 2.3 %collective-permute-start.8 = (bf16[2,16,256]{2,1,0:T(8,128)(2,1)S(1)}, bf16[2,16,256]{2,1,0:T(8,128)(2,1)S(1)}, u32[]{:S(2)}, u32[]{:S(2)}) collective-permute-start(bf16[2,16,256]{2,1,0:T(8,128)(2,1)S(1)} %pad_maximum_fusion.refs_0_), channel_id=1, source_target_pairs={{0,12},{4,8},{8,4},{12,0},{1,13},{5,9},{9,5},{13,1},{2,14},{6,10},... | collective-permute-start | bytes 49160 | tf_op jit(solution)/shard_map/ppermute | solution.py:293
  30.7 2.1 %collective-permute-start.6 = (bf16[2,16,256]{2,1,0:T(8,128)(2,1)S(1)}, bf16[2,16,256]{2,1,0:T(8,128)(2,1)S(1)}, u32[]{:S(2)}, u32[]{:S(2)}) collective-permute-start(bf16[2,16,256]{2,1,0:T(8,128)(2,1)S(1)} %pad_maximum_fusion.refs_0_), channel_id=1, source_target_pairs={{0,4},{4,0},{8,12},{12,8},{1,5},{5,1},{9,13},{13,9},{2,6},{6,2},{1... | collective-permute-start | bytes 49160 | tf_op jit(solution)/shard_map/ppermute | solution.py:293
  32.9 2.3 %hidden_down.1.refs_5_ = f32[8,2048]{1,0:T(8,128)S(1)} custom-call(f32[5,8,128]{2,1,0:T(8,128)S(1)} %get-tuple-element.18.stats, bf16[16,4096]{1,0:T(8,128)(2,1)S(1)} %up.1.refs_7_.refs_0_, bf16[16,4096]{1,0:T(8,128)(2,1)S(1)} %collective-permute-done.9.refs_1_, bf16[16,4096]{1,0:T(8,128)(2,1)S(1)} %collective-permute-done.10.refs_2_, ...), custom_call_target="tpu_custom_call" | custom-call | flops 4000000000 | bytes 16800000 | tf_op jit(solution)/shard_map/hidden_down/pallas_call | solution.py:403
  35.4 0.8 %out_projection.1 = (f32[6,2048]{1,0:T(8,128)S(1)}, bf16[6,2048]{1,0:T(8,128)(2,1)S(1)}) custom-call(bf16[2,16,256]{2,1,0:T(8,128)(2,1)S(1)} %pad_maximum_fusion.refs_0_, bf16[2,16,256]{2,1,0:T(8,128)(2,1)S(1)} %collective-permute-done.6.refs_1_, bf16[2,16,256]{2,1,0:T(8,128)(2,1)S(1)} %collective-permute-done.7.refs_2_, ...), custom_call_target="tpu_custom_call" | custom-call | flops 1000000000 | bytes 4000000 | tf_op jit(solution)/shard_map/out_projection/pallas_call | solution.py:413
  36.2 1.6 %collective-permute-start.13 = (bf16[6,2048]{1,0:T(8,128)(2,1)S(1)}, bf16[6,2048]{1,0:T(8,128)(2,1)S(1)}, u32[]{:S(2)}, u32[]{:S(2)}) collective-permute-start(bf16[6,2048]{1,0:T(8,128)(2,1)S(1)} %get-tuple-element.20), channel_id=1, source_target_pairs={{0,2},{1,3},{2,0},{3,1},{4,6},{5,7},{6,4},{7,5},{8,10},{9,11},{10,... | collective-permute-start | bytes 73736 | tf_op jit(solution)/shard_map/ppermute | solution.py:293
  37.8 0.3 collective-permute-start.12
  38.1 1.8 %collective-permute-done.14 = bf16[6,2048]{1,0:T(8,128)(2,1)S(1)} collective-permute-done((bf16[6,2048]{1,0:T(8,128)(2,1)S(1)}, bf16[6,2048]{1,0:T(8,128)(2,1)S(1)}, u32[]{:S(2)}, u32[]{:S(2)}) %collective-permute-start.14) | collective-permute-done | bytes 24608 | tf_op jit(solution)/shard_map/ppermute | solution.py:293
  39.9 0.4 collective-permute-done.13
  40.3 0.6 %add_convert_fusion = bf16[6,2048]{1,0:T(8,128)(2,1)} fusion(bf16[6,2048]{1,0:T(8,128)(2,1)S(1)} %collective-permute-done.14, bf16[6,2048]{1,0:T(8,128)(2,1)S(1)} %collective-permute-done.13, f32[6,2048]{1,0:T(8,128)S(1)} %get-tuple-element.19, bf16[6,2048]{1,0:T(8,128)(2,1)S(1)} %collective-permute-done.12, bf16[6,2048]{1,0:T(8,128)(2,1)S(1)} %copy-done.1), kind=kLoop, calls=%fused_computation | loop fusion | flops 110592 | bytes 172032 | tf_op jit(solution)/shard_map/convert_element_type | solution.py:428
  (62 shorter events, 0.6 us)
Async XLA Ops:
  0.7 9.9 %slice-start.4 = ((s8[16777216]{0:T(1024)(128)(4,1)}), s8[4194304]{0:T(1024)(128)(4,1)S(1)}, s32[]{:S(2)}) async-start(s8[16777216]{0:T(1024)(128)(4,1)} %bitcast.12), calls=%async_computation.4 | async-start | bytes 8388608
  3.7 12.5 %slice-start.8 = ((s8[16777216]{0:T(1024)(128)(4,1)}), s8[4194304]{0:T(1024)(128)(4,1)S(1)}, s32[]{:S(2)}) async-start(s8[16777216]{0:T(1024)(128)(4,1)} %bitcast.14), calls=%async_computation.8 | async-start | bytes 8388608
  3.7 12.5 %slice-start.9 = ((s8[16777216]{0:T(1024)(128)(4,1)}), s8[4194304]{0:T(1024)(128)(4,1)S(1)}, s32[]{:S(2)}) async-start(s8[16777216]{0:T(1024)(128)(4,1)} %bitcast.14), calls=%async_computation.9 | async-start | bytes 8388608
  3.7 12.5 %slice-start.10 = ((s8[16777216]{0:T(1024)(128)(4,1)}), s8[4194304]{0:T(1024)(128)(4,1)S(1)}, s32[]{:S(2)}) async-start(s8[16777216]{0:T(1024)(128)(4,1)} %bitcast.14), calls=%async_computation.10 | async-start | bytes 8388608
  4.8 8.1 %collective-permute-start.2 = (bf16[8,1664]{1,0:T(8,128)(2,1)S(1)}, bf16[8,1664]{1,0:T(8,128)(2,1)S(1)}, u32[]{:S(2)}, u32[]{:S(2)}) collective-permute-start(bf16[8,1664]{1,0:T(8,128)(2,1)S(1)} %get-tuple-element.12.refs_0_), channel_id=1, source_target_pairs={{0,12},{4,8},{8,4},{12,0},{1,13},{5,9},{9,5},{13,1},{2,14},{6,10},... | collective-permute-start | bytes 79880 | tf_op jit(solution)/shard_map/ppermute | solution.py:293
  9.8 4.7 %collective-permute-start.1 = (bf16[8,1664]{1,0:T(8,128)(2,1)S(1)}, bf16[8,1664]{1,0:T(8,128)(2,1)S(1)}, u32[]{:S(2)}, u32[]{:S(2)}) collective-permute-start(bf16[8,1664]{1,0:T(8,128)(2,1)S(1)} %get-tuple-element.12.refs_0_), channel_id=1, source_target_pairs={{0,8},{4,12},{8,0},{12,4},{1,9},{5,13},{9,1},{13,5},{2,10},{6,14},... | collective-permute-start | bytes 79880 | tf_op jit(solution)/shard_map/ppermute | solution.py:293
  9.8 4.7 %collective-permute-start = (bf16[8,1664]{1,0:T(8,128)(2,1)S(1)}, bf16[8,1664]{1,0:T(8,128)(2,1)S(1)}, u32[]{:S(2)}, u32[]{:S(2)}) collective-permute-start(bf16[8,1664]{1,0:T(8,128)(2,1)S(1)} %get-tuple-element.12.refs_0_), channel_id=1, source_target_pairs={{0,4},{4,0},{8,12},{12,8},{1,5},{5,1},{9,13},{13,9},{2,6},{6,2},{1... | collective-permute-start | bytes 79880 | tf_op jit(solution)/shard_map/ppermute | solution.py:293
  10.4 12.6 %collective-permute-start.4 = (bf16[3,256,512]{2,1,0:T(8,128)(2,1)S(1)}, bf16[3,256,512]{2,1,0:T(8,128)(2,1)S(1)}, u32[]{:S(2)}, u32[]{:S(2)}) collective-permute-start(bf16[3,256,512]{2,1,0:T(8,128)(2,1)S(1)} %copy-done.4), channel_id=1, source_target_pairs={{0,1},{1,0},{2,3},{3,2},{4,5},{5,4},{6,7},{7,6},{8,9},{9,8},{10,11... | collective-permute-start | bytes 2359304 | tf_op jit(solution)/shard_map/ppermute | solution.py:293
  14.7 8.3 %collective-permute-start.3 = (bf16[8,1024]{1,0:T(8,128)(2,1)S(1)}, bf16[8,1024]{1,0:T(8,128)(2,1)S(1)}, u32[]{:S(2)}, u32[]{:S(2)}) collective-permute-start(bf16[8,1024]{1,0:T(8,128)(2,1)S(1)} %get-tuple-element.13.after.refs_0_), channel_id=1, source_target_pairs={{0,2},{2,0},{1,3},{3,1},{4,6},{6,4},{5,7},{7,5},{8,10},{10,8},{9,1... | collective-permute-start | bytes 49160 | tf_op jit(solution)/shard_map/ppermute | solution.py:293
  16.3 16.6 %slice-start = ((s8[16777216]{0:T(1024)(128)(4,1)}), s8[4194304]{0:T(1024)(128)(4,1)S(1)}, s32[]{:S(2)}) async-start(s8[16777216]{0:T(1024)(128)(4,1)} %bitcast.9), calls=%async_computation | async-start | bytes 8388608
  16.3 16.6 %slice-start.1 = ((s8[16777216]{0:T(1024)(128)(4,1)}), s8[4194304]{0:T(1024)(128)(4,1)S(1)}, s32[]{:S(2)}) async-start(s8[16777216]{0:T(1024)(128)(4,1)} %bitcast.9), calls=%async_computation.1 | async-start | bytes 8388608
  18.6 12.2 %collective-permute-start.11 = (bf16[16,4096]{1,0:T(8,128)(2,1)S(1)}, bf16[16,4096]{1,0:T(8,128)(2,1)S(1)}, u32[]{:S(2)}, u32[]{:S(2)}) collective-permute-start(bf16[16,4096]{1,0:T(8,128)(2,1)S(1)} %up.1.refs_7_.refs_0_), channel_id=1, source_target_pairs={{0,12},{4,8},{8,4},{12,0},{1,13},{5,9},{9,5},{13,1},{2,14},{6,10},... | collective-permute-start | bytes 393224 | tf_op jit(solution)/shard_map/ppermute | solution.py:293
  20.9 12.0 %collective-permute-start.10 = (bf16[16,4096]{1,0:T(8,128)(2,1)S(1)}, bf16[16,4096]{1,0:T(8,128)(2,1)S(1)}, u32[]{:S(2)}, u32[]{:S(2)}) collective-permute-start(bf16[16,4096]{1,0:T(8,128)(2,1)S(1)} %up.1.refs_7_.refs_0_), channel_id=1, source_target_pairs={{0,8},{4,12},{8,0},{12,4},{1,9},{5,13},{9,1},{13,5},{2,10},{6,14},... | collective-permute-start | bytes 393224 | tf_op jit(solution)/shard_map/ppermute | solution.py:293
  20.9 12.0 %collective-permute-start.9 = (bf16[16,4096]{1,0:T(8,128)(2,1)S(1)}, bf16[16,4096]{1,0:T(8,128)(2,1)S(1)}, u32[]{:S(2)}, u32[]{:S(2)}) collective-permute-start(bf16[16,4096]{1,0:T(8,128)(2,1)S(1)} %up.1.refs_7_.refs_0_), channel_id=1, source_target_pairs={{0,4},{4,0},{8,12},{12,8},{1,5},{5,1},{9,13},{13,9},{2,6},{6,2},{1... | collective-permute-start | bytes 393224 | tf_op jit(solution)/shard_map/ppermute | solution.py:293
  23.0 9.9 %slice-start.2 = ((s8[16777216]{0:T(1024)(128)(4,1)}), s8[4194304]{0:T(1024)(128)(4,1)S(1)}, s32[]{:S(2)}) async-start(s8[16777216]{0:T(1024)(128)(4,1)} %bitcast.9), calls=%async_computation.2 | async-start | bytes 8388608
  23.0 9.9 %slice-start.3 = ((s8[16777216]{0:T(1024)(128)(4,1)}), s8[4194304]{0:T(1024)(128)(4,1)S(1)}, s32[]{:S(2)}) async-start(s8[16777216]{0:T(1024)(128)(4,1)} %bitcast.9), calls=%async_computation.3 | async-start | bytes 8388608
  23.0 12.4 %copy-start = (bf16[1024,2048]{1,0:T(8,128)(2,1)S(1)}, bf16[1024,2048]{1,0:T(8,128)(2,1)}, u32[]{:S(2)}) copy-start(bf16[1024,2048]{1,0:T(8,128)(2,1)} %refs_4_.5) | copy-start | bytes 12582916
  24.8 3.7 %collective-permute-start.5 = (bf16[16,256]{1,0:T(8,128)(2,1)S(1)}, bf16[16,256]{1,0:T(8,128)(2,1)S(1)}, u32[]{:S(2)}, u32[]{:S(2)}) collective-permute-start(bf16[16,256]{1,0:T(8,128)(2,1)S(1)} %get-tuple-element.17), channel_id=1, source_target_pairs={{0,2},{2,0},{1,3},{3,1},{4,6},{6,4},{5,7},{7,5},{8,10},{10,8},{9,1... | collective-permute-start | bytes 24584 | tf_op jit(solution)/shard_map/ppermute | solution.py:398
  28.5 6.8 %collective-permute-start.8 = (bf16[2,16,256]{2,1,0:T(8,128)(2,1)S(1)}, bf16[2,16,256]{2,1,0:T(8,128)(2,1)S(1)}, u32[]{:S(2)}, u32[]{:S(2)}) collective-permute-start(bf16[2,16,256]{2,1,0:T(8,128)(2,1)S(1)} %pad_maximum_fusion.refs_0_), channel_id=1, source_target_pairs={{0,12},{4,8},{8,4},{12,0},{1,13},{5,9},{9,5},{13,1},{2,14},{6,10},... | collective-permute-start | bytes 49160 | tf_op jit(solution)/shard_map/ppermute | solution.py:293
  30.7 4.6 %collective-permute-start.7 = (bf16[2,16,256]{2,1,0:T(8,128)(2,1)S(1)}, bf16[2,16,256]{2,1,0:T(8,128)(2,1)S(1)}, u32[]{:S(2)}, u32[]{:S(2)}) collective-permute-start(bf16[2,16,256]{2,1,0:T(8,128)(2,1)S(1)} %pad_maximum_fusion.refs_0_), channel_id=1, source_target_pairs={{0,8},{4,12},{8,0},{12,4},{1,9},{5,13},{9,1},{13,5},{2,10},{6,14},... | collective-permute-start | bytes 49160 | tf_op jit(solution)/shard_map/ppermute | solution.py:293
  30.7 4.6 %collective-permute-start.6 = (bf16[2,16,256]{2,1,0:T(8,128)(2,1)S(1)}, bf16[2,16,256]{2,1,0:T(8,128)(2,1)S(1)}, u32[]{:S(2)}, u32[]{:S(2)}) collective-permute-start(bf16[2,16,256]{2,1,0:T(8,128)(2,1)S(1)} %pad_maximum_fusion.refs_0_), channel_id=1, source_target_pairs={{0,4},{4,0},{8,12},{12,8},{1,5},{5,1},{9,13},{13,9},{2,6},{6,2},{1... | collective-permute-start | bytes 49160 | tf_op jit(solution)/shard_map/ppermute | solution.py:293
  36.2 3.7 %collective-permute-start.14 = (bf16[6,2048]{1,0:T(8,128)(2,1)S(1)}, bf16[6,2048]{1,0:T(8,128)(2,1)S(1)}, u32[]{:S(2)}, u32[]{:S(2)}) collective-permute-start(bf16[6,2048]{1,0:T(8,128)(2,1)S(1)} %get-tuple-element.20), channel_id=1, source_target_pairs={{0,3},{1,2},{2,1},{3,0},{4,7},{5,6},{6,5},{7,4},{8,11},{9,10},{10,... | collective-permute-start | bytes 73736 | tf_op jit(solution)/shard_map/ppermute | solution.py:293
  36.2 4.0 %collective-permute-start.13 = (bf16[6,2048]{1,0:T(8,128)(2,1)S(1)}, bf16[6,2048]{1,0:T(8,128)(2,1)S(1)}, u32[]{:S(2)}, u32[]{:S(2)}) collective-permute-start(bf16[6,2048]{1,0:T(8,128)(2,1)S(1)} %get-tuple-element.20), channel_id=1, source_target_pairs={{0,2},{1,3},{2,0},{3,1},{4,6},{5,7},{6,4},{7,5},{8,10},{9,11},{10,... | collective-permute-start | bytes 73736 | tf_op jit(solution)/shard_map/ppermute | solution.py:293
  37.8 2.5 %collective-permute-start.12 = (bf16[6,2048]{1,0:T(8,128)(2,1)S(1)}, bf16[6,2048]{1,0:T(8,128)(2,1)S(1)}, u32[]{:S(2)}, u32[]{:S(2)}) collective-permute-start(bf16[6,2048]{1,0:T(8,128)(2,1)S(1)} %get-tuple-element.20), channel_id=1, source_target_pairs={{0,1},{1,0},{2,3},{3,2},{4,5},{5,4},{6,7},{7,6},{8,9},{9,8},{10,11... | collective-permute-start | bytes 73736 | tf_op jit(solution)/shard_map/ppermute | solution.py:293
  (10 other events, 57.4 us)

commit v6 on v5

--- a/solution.py
+++ b/solution.py
@@ -225,12 +225,12 @@
 
 
 def down_kernel(dims, stats, *refs):
-    gx, seq_dev = dims
+    gx, seq_dev, order = dims
     parts, (down, result, hidden) = refs[:gx], refs[gx:]
     rows, ff_dev = hidden.shape
     slab = min(ff_dev, 1024)
     inverse = stats[gx][:, :1]
-    shifts = [stats[step][:, :1] for step in range(gx)]
+    shifts = [stats[step][:, :1] for step in (0, *order)]
     for start in range(0, ff_dev, slab):
         sums = []
         for base in (0, rows):
@@ -286,16 +286,19 @@
     share[...] = total[...].astype(BF16)
 
 
-def with_others(values, axis):
+def with_others(values, axis, order=None):
     size = lax.axis_size(axis)
     if size <= FEW:
         return [values] + [
             lax.ppermute(values, axis, [(place, place ^ step) for place in range(size)])
-            for step in range(1, size)
+            for step in (order or range(1, size))
         ]
     gathered = lax.all_gather(values, axis)
     here = lax.axis_index(axis)
-    return [lax.dynamic_index_in_dim(gathered, here ^ step, 0, False) for step in range(size)]
+    return [
+        lax.dynamic_index_in_dim(gathered, here ^ step, 0, False)
+        for step in (0, *(order or range(1, size)))
+    ]
 
 
 def body(
@@ -378,7 +381,8 @@
         cost_estimate=cost(6e9, 16.8e6),
         name="up",
     )(lhs, up_weight, gate, query)
-    parts = with_others(both, "gx")
+    order = (1, 3, 2) if gx == 4 else tuple(range(1, gx))
+    parts = with_others(both, "gx", order)
 
     angle = lengths.astype(F32)[:, None] * rotary_base**exponents
     angle = jnp.pad(angle, ((0, 1), (0, 0)))
@@ -401,7 +405,7 @@
     pieces = with_others(jnp.stack(pieces), "gx")
 
     partial = pl.pallas_call(
-        functools.partial(down_kernel, (gx, seq_dev)),
+        functools.partial(down_kernel, (gx, seq_dev, order)),
         out_shape=jax.ShapeDtypeStruct((rows, width), F32),
         in_specs=[VMEM] * (gx + 2),
         out_specs=VMEM,

time: 41 us -> 40.2 us (0.980)
  starting transfers between devices: 18.4 us -> 17.7 us
    ppermute x14, starting transfers between devices: 17.9 us -> 16.9 us  [with_others(): lax.ppermute(values, axis, [(place, place ^ step) for place in range(size)])]
  transfers between devices with their start and end apart: 15 -> 15, of which waited for: 5 -> 6; matrix products, arithmetic and copies ran while one was open for 0% -> 0% of each run, Pallas kernels for 22% -> 22%
where the time goes in v6:
time: 40.2 us; the launch traced here: 40.1 us
  starting transfers between devices  17.7 us (44%)
  Pallas kernels  10.6 us (26%)
  waiting for transfers between devices  7 us (17%)
  local copies, waits for them, and re-layouts  3.14 us (8%)
  between operations  0.9 us (2%)
  other arithmetic  0.73 us (2%)
    ppermute x14, starting transfers between devices, with_others(): lax.ppermute(values, axis, [(place, place ^ step) for place in range(size)])  16.9 us
    ppermute x14, waiting for transfers between devices, with_others(): lax.ppermute(values, axis, [(place, place ^ step) for place in range(size)])  4.21 us
    unnamed x38, local copies, waits for them, and re-layouts  3.09 us
    ppermute x1, waiting for transfers between devices, body(): lax.ppermute(pieces[step], 'gy', [(place, place ^ step) for place in rang...  2.79 us
    pallas_call x1, Pallas kernels, body(): pl.pallas_call(functools.partial(down_kernel, (gx, seq_dev, order)), out_...  2.35 us
    pallas_call x1, Pallas kernels, body(): pl.pallas_call(gate_kernel, out_shape=jax.ShapeDtypeStruct((rows, ff_dev)...  2.28 us
    pallas_call x1, Pallas kernels, body(): pl.pallas_call(up_kernel, out_shape=jax.ShapeDtypeStruct((2 * rows, ff_de...  2.27 us
    pallas_call x1, Pallas kernels, body(): pl.pallas_call(functools.partial(attention_kernel, (gy, gz, seq_dev)), ou...  1.79 us
  transfers between devices with their start and end apart: 15, of which 6 were waited for; matrix products, arithmetic and copies ran while one was open for 0% of the time, Pallas kernels for 22%

profile of v6, /device:TPU:0, one launch (start us, length us, event | category | flops | bytes accessed | tf_op | source)
XLA Modules:
  0.0 40.1 jit_solution(6043464961901922059)
XLA Ops:
  0.7 0.7 %copy-done.1 = bf16[6,2048]{1,0:T(8,128)(2,1)S(1)} copy-done((bf16[6,2048]{1,0:T(8,128)(2,1)S(1)}, bf16[6,2048]{1,0:T(8,128)(2,1)}, u32[]{:S(2)}) %copy-start.1) | copy-done | bytes 24600
  1.4 1.1 %copy-done.3 = bf16[2048,512]{1,0:T(8,128)(2,1)S(1)} copy-done((bf16[2048,512]{1,0:T(8,128)(2,1)S(1)}, bf16[2048,512]{1,0:T(8,128)(2,1)}, u32[]{:S(2)}) %copy-start.3) | copy-done | bytes 2097176
  2.5 1.2 %copy-done.2 = bf16[2048,1024]{1,0:T(8,128)(2,1)S(1)} copy-done((bf16[2048,1024]{1,0:T(8,128)(2,1)S(1)}, bf16[2048,1024]{1,0:T(8,128)(2,1)}, u32[]{:S(2)}) %copy-start.2) | copy-done | bytes 4194328
  3.8 1.0 %norm_query.1 = (bf16[8,1664]{1,0:T(8,128)(2,1)S(1)}, bf16[8,2048]{1,0:T(8,128)(2,1)S(1)}) custom-call(bf16[6,2048]{1,0:T(8,128)(2,1)S(1)} %copy-done.1, f32[1,2048]{1,0:T(1,128)S(1)} %bitcast.16, bf16[2048,1024]{1,0:T(8,128)(2,1)S(1)} %copy-done.2, bf16[2048,512]{1,0:T(8,128)(2,1)S(1)} %copy-done.3, f32[1,128]{1,0:T(1,128)S(1)} %exponents.1.after), custom_call_target="tpu_custom_call" | custom-call | flops 7000000000 | tf_op jit(solution)/shard_map/norm_query/pallas_call | solution.py:337
  4.8 5.1 %collective-permute-start.2 = (bf16[8,1664]{1,0:T(8,128)(2,1)S(1)}, bf16[8,1664]{1,0:T(8,128)(2,1)S(1)}, u32[]{:S(2)}, u32[]{:S(2)}) collective-permute-start(bf16[8,1664]{1,0:T(8,128)(2,1)S(1)} %get-tuple-element.12.refs_0_), channel_id=1, source_target_pairs={{0,12},{4,8},{8,4},{12,0},{1,13},{5,9},{9,5},{13,1},{2,14},{6,10},... | collective-permute-start | bytes 79880 | tf_op jit(solution)/shard_map/ppermute | solution.py:293
  9.8 0.6 %collective-permute-start = (bf16[8,1664]{1,0:T(8,128)(2,1)S(1)}, bf16[8,1664]{1,0:T(8,128)(2,1)S(1)}, u32[]{:S(2)}, u32[]{:S(2)}) collective-permute-start(bf16[8,1664]{1,0:T(8,128)(2,1)S(1)} %get-tuple-element.12.refs_0_), channel_id=1, source_target_pairs={{0,4},{4,0},{8,12},{12,8},{1,5},{5,1},{9,13},{13,9},{2,6},{6,2},{1... | collective-permute-start | bytes 79880 | tf_op jit(solution)/shard_map/ppermute | solution.py:293
  10.6 2.3 %gate.1 = bf16[8,4096]{1,0:T(8,128)(2,1)S(1)} custom-call(bf16[8,2048]{1,0:T(8,128)(2,1)S(1)} %get-tuple-element.15.lhs, bf16[2048,4096]{1,0:T(8,128)(2,1)S(1)} %bitcast.13), custom_call_target="tpu_custom_call" | custom-call | flops 6000000000 | bytes 16800000 | tf_op jit(solution)/shard_map/gate/pallas_call | solution.py:352
  12.9 1.7 %collective-permute-done.1.refs_2_ = bf16[8,1664]{1,0:T(8,128)(2,1)S(1)} collective-permute-done((bf16[8,1664]{1,0:T(8,128)(2,1)S(1)}, bf16[8,1664]{1,0:T(8,128)(2,1)S(1)}, u32[]{:S(2)}, u32[]{:S(2)}) %collective-permute-start.1) | collective-permute-done | bytes 26656 | tf_op jit(solution)/shard_map/ppermute | solution.py:293
  14.7 1.6 %collective-permute-start.3 = (bf16[8,1024]{1,0:T(8,128)(2,1)S(1)}, bf16[8,1024]{1,0:T(8,128)(2,1)S(1)}, u32[]{:S(2)}, u32[]{:S(2)}) collective-permute-start(bf16[8,1024]{1,0:T(8,128)(2,1)S(1)} %get-tuple-element.13.after.refs_0_), channel_id=1, source_target_pairs={{0,2},{2,0},{1,3},{3,1},{4,6},{6,4},{5,7},{7,5},{8,10},{10,8},{9,1... | collective-permute-start | bytes 49160 | tf_op jit(solution)/shard_map/ppermute | solution.py:293
  16.3 2.3 %up.1.refs_7_.refs_0_ = bf16[16,4096]{1,0:T(8,128)(2,1)S(1)} custom-call(bf16[8,2048]{1,0:T(8,128)(2,1)S(1)} %get-tuple-element.15.lhs, bf16[2048,4096]{1,0:T(8,128)(2,1)S(1)} %bitcast.15, bf16[8,4096]{1,0:T(8,128)(2,1)S(1)} %gate.1, bf16[8,1024]{1,0:T(8,128)(2,1)S(1)} %get-tuple-element.13.after.refs_0_), custom_call_target="tpu_custom_call" | custom-call | flops 6000000000 | bytes 16800000 | tf_op jit(solution)/shard_map/up/pallas_call | solution.py:375
  18.6 2.0 %collective-permute-start.11 = (bf16[16,4096]{1,0:T(8,128)(2,1)S(1)}, bf16[16,4096]{1,0:T(8,128)(2,1)S(1)}, u32[]{:S(2)}, u32[]{:S(2)}) collective-permute-start(bf16[16,4096]{1,0:T(8,128)(2,1)S(1)} %up.1.refs_7_.refs_0_), channel_id=1, source_target_pairs={{0,8},{4,12},{8,0},{12,4},{1,9},{5,13},{9,1},{13,5},{2,10},{6,14},... | collective-permute-start | bytes 393224 | tf_op jit(solution)/shard_map/ppermute | solution.py:293
  20.6 0.6 %collective-permute-start.10 = (bf16[16,4096]{1,0:T(8,128)(2,1)S(1)}, bf16[16,4096]{1,0:T(8,128)(2,1)S(1)}, u32[]{:S(2)}, u32[]{:S(2)}) collective-permute-start(bf16[16,4096]{1,0:T(8,128)(2,1)S(1)} %up.1.refs_7_.refs_0_), channel_id=1, source_target_pairs={{0,12},{4,8},{8,4},{12,0},{1,13},{5,9},{9,5},{13,1},{2,14},{6,10},... | collective-permute-start | bytes 393224 | tf_op jit(solution)/shard_map/ppermute | solution.py:293
  21.2 0.9 %collective-permute-start.9 = (bf16[16,4096]{1,0:T(8,128)(2,1)S(1)}, bf16[16,4096]{1,0:T(8,128)(2,1)S(1)}, u32[]{:S(2)}, u32[]{:S(2)}) collective-permute-start(bf16[16,4096]{1,0:T(8,128)(2,1)S(1)} %up.1.refs_7_.refs_0_), channel_id=1, source_target_pairs={{0,4},{4,0},{8,12},{12,8},{1,5},{5,1},{9,13},{13,9},{2,6},{6,2},{1... | collective-permute-start | bytes 393224 | tf_op jit(solution)/shard_map/ppermute | solution.py:293
  22.1 1.8 %attention.1 = (bf16[16,256]{1,0:T(8,128)(2,1)S(1)}, bf16[16,256]{1,0:T(8,128)(2,1)S(1)}, bf16[3,512]{1,0:T(4,128)(2,1)}) custom-call(bf16[8,1024]{1,0:T(8,128)(2,1)S(1)} %get-tuple-element.13.after.refs_0_, bf16[8,1024]{1,0:T(8,128)(2,1)S(1)} %collective-permute-done.3.refs_1_, bf16[3,256,512]{2,1,0:T(8,128)(2,1)S(1)} %copy-done.4, ...), custom_call_target="tpu_custom_call" | custom-call | flops 7000000000 | bytes 2000000 | tf_op jit(solution)/shard_map/attention/pallas_call | solution.py:390
  23.9 0.9 %collective-permute-start.5 = (bf16[16,256]{1,0:T(8,128)(2,1)S(1)}, bf16[16,256]{1,0:T(8,128)(2,1)S(1)}, u32[]{:S(2)}, u32[]{:S(2)}) collective-permute-start(bf16[16,256]{1,0:T(8,128)(2,1)S(1)} %get-tuple-element.17), channel_id=1, source_target_pairs={{0,2},{2,0},{1,3},{3,1},{4,6},{6,4},{5,7},{7,5},{8,10},{10,8},{9,1... | collective-permute-start | bytes 24584 | tf_op jit(solution)/shard_map/ppermute | solution.py:402
  24.8 2.8 %collective-permute-done.5 = bf16[16,256]{1,0:T(8,128)(2,1)S(1)} collective-permute-done((bf16[16,256]{1,0:T(8,128)(2,1)S(1)}, bf16[16,256]{1,0:T(8,128)(2,1)S(1)}, u32[]{:S(2)}, u32[]{:S(2)}) %collective-permute-start.5) | collective-permute-done | bytes 8224 | tf_op jit(solution)/shard_map/ppermute | solution.py:402
  27.6 2.4 %collective-permute-start.8 = (bf16[2,16,256]{2,1,0:T(8,128)(2,1)S(1)}, bf16[2,16,256]{2,1,0:T(8,128)(2,1)S(1)}, u32[]{:S(2)}, u32[]{:S(2)}) collective-permute-start(bf16[2,16,256]{2,1,0:T(8,128)(2,1)S(1)} %pad_maximum_fusion.refs_0_), channel_id=1, source_target_pairs={{0,12},{4,8},{8,4},{12,0},{1,13},{5,9},{9,5},{13,1},{2,14},{6,10},... | collective-permute-start | bytes 49160 | tf_op jit(solution)/shard_map/ppermute | solution.py:293
  29.9 0.6 %collective-permute-start.7 = (bf16[2,16,256]{2,1,0:T(8,128)(2,1)S(1)}, bf16[2,16,256]{2,1,0:T(8,128)(2,1)S(1)}, u32[]{:S(2)}, u32[]{:S(2)}) collective-permute-start(bf16[2,16,256]{2,1,0:T(8,128)(2,1)S(1)} %pad_maximum_fusion.refs_0_), channel_id=1, source_target_pairs={{0,8},{4,12},{8,0},{12,4},{1,9},{5,13},{9,1},{13,5},{2,10},{6,14},... | collective-permute-start | bytes 49160 | tf_op jit(solution)/shard_map/ppermute | solution.py:293
  30.6 1.3 %collective-permute-start.6 = (bf16[2,16,256]{2,1,0:T(8,128)(2,1)S(1)}, bf16[2,16,256]{2,1,0:T(8,128)(2,1)S(1)}, u32[]{:S(2)}, u32[]{:S(2)}) collective-permute-start(bf16[2,16,256]{2,1,0:T(8,128)(2,1)S(1)} %pad_maximum_fusion.refs_0_), channel_id=1, source_target_pairs={{0,4},{4,0},{8,12},{12,8},{1,5},{5,1},{9,13},{13,9},{2,6},{6,2},{1... | collective-permute-start | bytes 49160 | tf_op jit(solution)/shard_map/ppermute | solution.py:293
  32.0 2.3 %hidden_down.1.refs_5_ = f32[8,2048]{1,0:T(8,128)S(1)} custom-call(f32[5,8,128]{2,1,0:T(8,128)S(1)} %get-tuple-element.18.stats, bf16[16,4096]{1,0:T(8,128)(2,1)S(1)} %up.1.refs_7_.refs_0_, bf16[16,4096]{1,0:T(8,128)(2,1)S(1)} %collective-permute-done.9.refs_1_, bf16[16,4096]{1,0:T(8,128)(2,1)S(1)} %collective-permute-done.10.refs_2_, ...), custom_call_target="tpu_custom_call" | custom-call | flops 4000000000 | bytes 16800000 | tf_op jit(solution)/shard_map/hidden_down/pallas_call | solution.py:407
  34.6 0.8 %out_projection.1 = (f32[6,2048]{1,0:T(8,128)S(1)}, bf16[6,2048]{1,0:T(8,128)(2,1)S(1)}) custom-call(bf16[2,16,256]{2,1,0:T(8,128)(2,1)S(1)} %pad_maximum_fusion.refs_0_, bf16[2,16,256]{2,1,0:T(8,128)(2,1)S(1)} %collective-permute-done.6.refs_1_, bf16[2,16,256]{2,1,0:T(8,128)(2,1)S(1)} %collective-permute-done.7.refs_2_, ...), custom_call_target="tpu_custom_call" | custom-call | flops 1000000000 | bytes 4000000 | tf_op jit(solution)/shard_map/out_projection/pallas_call | solution.py:417
  35.4 1.5 %collective-permute-start.13 = (bf16[6,2048]{1,0:T(8,128)(2,1)S(1)}, bf16[6,2048]{1,0:T(8,128)(2,1)S(1)}, u32[]{:S(2)}, u32[]{:S(2)}) collective-permute-start(bf16[6,2048]{1,0:T(8,128)(2,1)S(1)} %get-tuple-element.20), channel_id=1, source_target_pairs={{0,2},{1,3},{2,0},{3,1},{4,6},{5,7},{6,4},{7,5},{8,10},{9,11},{10,... | collective-permute-start | bytes 73736 | tf_op jit(solution)/shard_map/ppermute | solution.py:293
  37.3 1.8 %collective-permute-done.14 = bf16[6,2048]{1,0:T(8,128)(2,1)S(1)} collective-permute-done((bf16[6,2048]{1,0:T(8,128)(2,1)S(1)}, bf16[6,2048]{1,0:T(8,128)(2,1)S(1)}, u32[]{:S(2)}, u32[]{:S(2)}) %collective-permute-start.14) | collective-permute-done | bytes 24608 | tf_op jit(solution)/shard_map/ppermute | solution.py:293
  39.4 0.6 %add_convert_fusion = bf16[6,2048]{1,0:T(8,128)(2,1)} fusion(bf16[6,2048]{1,0:T(8,128)(2,1)S(1)} %collective-permute-done.14, bf16[6,2048]{1,0:T(8,128)(2,1)S(1)} %collective-permute-done.13, f32[6,2048]{1,0:T(8,128)S(1)} %get-tuple-element.19, bf16[6,2048]{1,0:T(8,128)(2,1)S(1)} %collective-permute-done.12, bf16[6,2048]{1,0:T(8,128)(2,1)S(1)} %copy-done.1), kind=kLoop, calls=%fused_computation | loop fusion | flops 110592 | bytes 172032 | tf_op jit(solution)/shard_map/convert_element_type | solution.py:432
  (62 shorter events, 1.5 us)
Async XLA Ops:
  0.7 9.9 %slice-start.4 = ((s8[16777216]{0:T(1024)(128)(4,1)}), s8[4194304]{0:T(1024)(128)(4,1)S(1)}, s32[]{:S(2)}) async-start(s8[16777216]{0:T(1024)(128)(4,1)} %bitcast.12), calls=%async_computation.4 | async-start | bytes 8388608
  3.7 12.5 %slice-start.8 = ((s8[16777216]{0:T(1024)(128)(4,1)}), s8[4194304]{0:T(1024)(128)(4,1)S(1)}, s32[]{:S(2)}) async-start(s8[16777216]{0:T(1024)(128)(4,1)} %bitcast.14), calls=%async_computation.8 | async-start | bytes 8388608
  3.7 12.5 %slice-start.9 = ((s8[16777216]{0:T(1024)(128)(4,1)}), s8[4194304]{0:T(1024)(128)(4,1)S(1)}, s32[]{:S(2)}) async-start(s8[16777216]{0:T(1024)(128)(4,1)} %bitcast.14), calls=%async_computation.9 | async-start | bytes 8388608
  3.7 12.5 %slice-start.10 = ((s8[16777216]{0:T(1024)(128)(4,1)}), s8[4194304]{0:T(1024)(128)(4,1)S(1)}, s32[]{:S(2)}) async-start(s8[16777216]{0:T(1024)(128)(4,1)} %bitcast.14), calls=%async_computation.10 | async-start | bytes 8388608
  4.8 8.1 %collective-permute-start.2 = (bf16[8,1664]{1,0:T(8,128)(2,1)S(1)}, bf16[8,1664]{1,0:T(8,128)(2,1)S(1)}, u32[]{:S(2)}, u32[]{:S(2)}) collective-permute-start(bf16[8,1664]{1,0:T(8,128)(2,1)S(1)} %get-tuple-element.12.refs_0_), channel_id=1, source_target_pairs={{0,12},{4,8},{8,4},{12,0},{1,13},{5,9},{9,5},{13,1},{2,14},{6,10},... | collective-permute-start | bytes 79880 | tf_op jit(solution)/shard_map/ppermute | solution.py:293
  9.8 4.7 %collective-permute-start.1 = (bf16[8,1664]{1,0:T(8,128)(2,1)S(1)}, bf16[8,1664]{1,0:T(8,128)(2,1)S(1)}, u32[]{:S(2)}, u32[]{:S(2)}) collective-permute-start(bf16[8,1664]{1,0:T(8,128)(2,1)S(1)} %get-tuple-element.12.refs_0_), channel_id=1, source_target_pairs={{0,8},{4,12},{8,0},{12,4},{1,9},{5,13},{9,1},{13,5},{2,10},{6,14},... | collective-permute-start | bytes 79880 | tf_op jit(solution)/shard_map/ppermute | solution.py:293
  9.8 4.7 %collective-permute-start = (bf16[8,1664]{1,0:T(8,128)(2,1)S(1)}, bf16[8,1664]{1,0:T(8,128)(2,1)S(1)}, u32[]{:S(2)}, u32[]{:S(2)}) collective-permute-start(bf16[8,1664]{1,0:T(8,128)(2,1)S(1)} %get-tuple-element.12.refs_0_), channel_id=1, source_target_pairs={{0,4},{4,0},{8,12},{12,8},{1,5},{5,1},{9,13},{13,9},{2,6},{6,2},{1... | collective-permute-start | bytes 79880 | tf_op jit(solution)/shard_map/ppermute | solution.py:293
  10.4 11.7 %collective-permute-start.4 = (bf16[3,256,512]{2,1,0:T(8,128)(2,1)S(1)}, bf16[3,256,512]{2,1,0:T(8,128)(2,1)S(1)}, u32[]{:S(2)}, u32[]{:S(2)}) collective-permute-start(bf16[3,256,512]{2,1,0:T(8,128)(2,1)S(1)} %copy-done.4), channel_id=1, source_target_pairs={{0,1},{1,0},{2,3},{3,2},{4,5},{5,4},{6,7},{7,6},{8,9},{9,8},{10,11... | collective-permute-start | bytes 2359304 | tf_op jit(solution)/shard_map/ppermute | solution.py:293
  14.7 7.4 %collective-permute-start.3 = (bf16[8,1024]{1,0:T(8,128)(2,1)S(1)}, bf16[8,1024]{1,0:T(8,128)(2,1)S(1)}, u32[]{:S(2)}, u32[]{:S(2)}) collective-permute-start(bf16[8,1024]{1,0:T(8,128)(2,1)S(1)} %get-tuple-element.13.after.refs_0_), channel_id=1, source_target_pairs={{0,2},{2,0},{1,3},{3,1},{4,6},{6,4},{5,7},{7,5},{8,10},{10,8},{9,1... | collective-permute-start | bytes 49160 | tf_op jit(solution)/shard_map/ppermute | solution.py:293
  16.3 15.7 %slice-start = ((s8[16777216]{0:T(1024)(128)(4,1)}), s8[4194304]{0:T(1024)(128)(4,1)S(1)}, s32[]{:S(2)}) async-start(s8[16777216]{0:T(1024)(128)(4,1)} %bitcast.9), calls=%async_computation | async-start | bytes 8388608
  16.3 15.7 %slice-start.1 = ((s8[16777216]{0:T(1024)(128)(4,1)}), s8[4194304]{0:T(1024)(128)(4,1)S(1)}, s32[]{:S(2)}) async-start(s8[16777216]{0:T(1024)(128)(4,1)} %bitcast.9), calls=%async_computation.1 | async-start | bytes 8388608
  18.6 12.0 %collective-permute-start.11 = (bf16[16,4096]{1,0:T(8,128)(2,1)S(1)}, bf16[16,4096]{1,0:T(8,128)(2,1)S(1)}, u32[]{:S(2)}, u32[]{:S(2)}) collective-permute-start(bf16[16,4096]{1,0:T(8,128)(2,1)S(1)} %up.1.refs_7_.refs_0_), channel_id=1, source_target_pairs={{0,8},{4,12},{8,0},{12,4},{1,9},{5,13},{9,1},{13,5},{2,10},{6,14},... | collective-permute-start | bytes 393224 | tf_op jit(solution)/shard_map/ppermute | solution.py:293
  20.6 11.3 %collective-permute-start.10 = (bf16[16,4096]{1,0:T(8,128)(2,1)S(1)}, bf16[16,4096]{1,0:T(8,128)(2,1)S(1)}, u32[]{:S(2)}, u32[]{:S(2)}) collective-permute-start(bf16[16,4096]{1,0:T(8,128)(2,1)S(1)} %up.1.refs_7_.refs_0_), channel_id=1, source_target_pairs={{0,12},{4,8},{8,4},{12,0},{1,13},{5,9},{9,5},{13,1},{2,14},{6,10},... | collective-permute-start | bytes 393224 | tf_op jit(solution)/shard_map/ppermute | solution.py:293
  21.2 10.7 %collective-permute-start.9 = (bf16[16,4096]{1,0:T(8,128)(2,1)S(1)}, bf16[16,4096]{1,0:T(8,128)(2,1)S(1)}, u32[]{:S(2)}, u32[]{:S(2)}) collective-permute-start(bf16[16,4096]{1,0:T(8,128)(2,1)S(1)} %up.1.refs_7_.refs_0_), channel_id=1, source_target_pairs={{0,4},{4,0},{8,12},{12,8},{1,5},{5,1},{9,13},{13,9},{2,6},{6,2},{1... | collective-permute-start | bytes 393224 | tf_op jit(solution)/shard_map/ppermute | solution.py:293
  22.1 9.9 %slice-start.2 = ((s8[16777216]{0:T(1024)(128)(4,1)}), s8[4194304]{0:T(1024)(128)(4,1)S(1)}, s32[]{:S(2)}) async-start(s8[16777216]{0:T(1024)(128)(4,1)} %bitcast.9), calls=%async_computation.2 | async-start | bytes 8388608
  22.1 9.9 %slice-start.3 = ((s8[16777216]{0:T(1024)(128)(4,1)}), s8[4194304]{0:T(1024)(128)(4,1)S(1)}, s32[]{:S(2)}) async-start(s8[16777216]{0:T(1024)(128)(4,1)} %bitcast.9), calls=%async_computation.3 | async-start | bytes 8388608
  22.1 12.5 %copy-start = (bf16[1024,2048]{1,0:T(8,128)(2,1)S(1)}, bf16[1024,2048]{1,0:T(8,128)(2,1)}, u32[]{:S(2)}) copy-start(bf16[1024,2048]{1,0:T(8,128)(2,1)} %refs_4_.5) | copy-start | bytes 12582916
  23.9 3.7 %collective-permute-start.5 = (bf16[16,256]{1,0:T(8,128)(2,1)S(1)}, bf16[16,256]{1,0:T(8,128)(2,1)S(1)}, u32[]{:S(2)}, u32[]{:S(2)}) collective-permute-start(bf16[16,256]{1,0:T(8,128)(2,1)S(1)} %get-tuple-element.17), channel_id=1, source_target_pairs={{0,2},{2,0},{1,3},{3,1},{4,6},{6,4},{5,7},{7,5},{8,10},{10,8},{9,1... | collective-permute-start | bytes 24584 | tf_op jit(solution)/shard_map/ppermute | solution.py:402
  27.6 6.8 %collective-permute-start.8 = (bf16[2,16,256]{2,1,0:T(8,128)(2,1)S(1)}, bf16[2,16,256]{2,1,0:T(8,128)(2,1)S(1)}, u32[]{:S(2)}, u32[]{:S(2)}) collective-permute-start(bf16[2,16,256]{2,1,0:T(8,128)(2,1)S(1)} %pad_maximum_fusion.refs_0_), channel_id=1, source_target_pairs={{0,12},{4,8},{8,4},{12,0},{1,13},{5,9},{9,5},{13,1},{2,14},{6,10},... | collective-permute-start | bytes 49160 | tf_op jit(solution)/shard_map/ppermute | solution.py:293
  29.9 4.6 %collective-permute-start.7 = (bf16[2,16,256]{2,1,0:T(8,128)(2,1)S(1)}, bf16[2,16,256]{2,1,0:T(8,128)(2,1)S(1)}, u32[]{:S(2)}, u32[]{:S(2)}) collective-permute-start(bf16[2,16,256]{2,1,0:T(8,128)(2,1)S(1)} %pad_maximum_fusion.refs_0_), channel_id=1, source_target_pairs={{0,8},{4,12},{8,0},{12,4},{1,9},{5,13},{9,1},{13,5},{2,10},{6,14},... | collective-permute-start | bytes 49160 | tf_op jit(solution)/shard_map/ppermute | solution.py:293
  30.6 3.9 %collective-permute-start.6 = (bf16[2,16,256]{2,1,0:T(8,128)(2,1)S(1)}, bf16[2,16,256]{2,1,0:T(8,128)(2,1)S(1)}, u32[]{:S(2)}, u32[]{:S(2)}) collective-permute-start(bf16[2,16,256]{2,1,0:T(8,128)(2,1)S(1)} %pad_maximum_fusion.refs_0_), channel_id=1, source_target_pairs={{0,4},{4,0},{8,12},{12,8},{1,5},{5,1},{9,13},{13,9},{2,6},{6,2},{1... | collective-permute-start | bytes 49160 | tf_op jit(solution)/shard_map/ppermute | solution.py:293
  35.4 3.7 %collective-permute-start.14 = (bf16[6,2048]{1,0:T(8,128)(2,1)S(1)}, bf16[6,2048]{1,0:T(8,128)(2,1)S(1)}, u32[]{:S(2)}, u32[]{:S(2)}) collective-permute-start(bf16[6,2048]{1,0:T(8,128)(2,1)S(1)} %get-tuple-element.20), channel_id=1, source_target_pairs={{0,3},{1,2},{2,1},{3,0},{4,7},{5,6},{6,5},{7,4},{8,11},{9,10},{10,... | collective-permute-start | bytes 73736 | tf_op jit(solution)/shard_map/ppermute | solution.py:293
  35.4 4.0 %collective-permute-start.13 = (bf16[6,2048]{1,0:T(8,128)(2,1)S(1)}, bf16[6,2048]{1,0:T(8,128)(2,1)S(1)}, u32[]{:S(2)}, u32[]{:S(2)}) collective-permute-start(bf16[6,2048]{1,0:T(8,128)(2,1)S(1)} %get-tuple-element.20), channel_id=1, source_target_pairs={{0,2},{1,3},{2,0},{3,1},{4,6},{5,7},{6,4},{7,5},{8,10},{9,11},{10,... | collective-permute-start | bytes 73736 | tf_op jit(solution)/shard_map/ppermute | solution.py:293
  37.0 2.5 %collective-permute-start.12 = (bf16[6,2048]{1,0:T(8,128)(2,1)S(1)}, bf16[6,2048]{1,0:T(8,128)(2,1)S(1)}, u32[]{:S(2)}, u32[]{:S(2)}) collective-permute-start(bf16[6,2048]{1,0:T(8,128)(2,1)S(1)} %get-tuple-element.20), channel_id=1, source_target_pairs={{0,1},{1,0},{2,3},{3,2},{4,5},{5,4},{6,7},{7,6},{8,9},{9,8},{10,11... | collective-permute-start | bytes 73736 | tf_op jit(solution)/shard_map/ppermute | solution.py:293
  (10 other events, 57.4 us)

commit v7 on v6

--- a/solution.py
+++ b/solution.py
@@ -12,10 +12,10 @@
 rotary_base = 10000.0
 FEW = 8
 LIMIT = 3
+SPARE = 512
 F32 = jnp.float32
 BF16 = jnp.bfloat16
 VMEM = pl.BlockSpec(memory_space=pltpu.VMEM)
-SMEM = pl.BlockSpec(memory_space=pltpu.SMEM)
 ANY = pl.BlockSpec(memory_space=pl.ANY)
 HBM = pl.BlockSpec(memory_space=pltpu.HBM)
 MIB = 2**20
@@ -123,14 +123,29 @@
     product(lhs[...], weight, store)
 
 
-def up_kernel(lhs, weight, gate, after, both):
-    rows = lhs.shape[0]
-    both[:rows, :] = gate[...]
+def packed_split(rows, each, ff_dev):
+    slab = ff_dev // rows * 2
+    if rows == 2 * each and (rows - 1) * slab == 2 * ff_dev - slab and slab % 128 == 0:
+        return ff_dev - slab
+    return ff_dev
+
+
+def up_kernel(lhs, weight, gate, after, both, wide):
+    rows, ff_dev = gate.shape
+    stay = wide.shape[1] - ff_dev
+    wide[:, :ff_dev] = gate[...].astype(F32)
 
     def store(part, value):
-        both[rows:, part] = value.astype(BF16)
-
-    product(lhs[...], weight, store)
+        if part.start < stay:
+            wide[:, ff_dev + part.start : ff_dev + part.stop] = value
+        else:
+            size = part.stop - part.start
+            for r in range(rows - 1):
+                wide[rows - 1 :, r * size : (r + 1) * size] = value[r : r + 1]
+
+    product(lhs[...], weight, store, ff_dev - stay or 1024)
+    both[:, : wide.shape[1]] = wide[...].astype(BF16)
+    both[:, wide.shape[1] :] = jnp.zeros_like(both[:, wide.shape[1] :])
 
 
 def query_kernel(dims, *refs):
@@ -151,8 +166,8 @@
     each = seq_dev + 1
     parts, refs = refs[:gy], refs[gy:]
     caches, refs = refs[:gz], refs[gz:]
-    lengths, keyval, tables, after = refs[:4]
-    pieces, (new_kv, qs, ks, vs) = refs[4 : 4 + gy], refs[4 + gy :]
+    keyval, tables, after = refs[:3]
+    pieces, (new_kv, qs, ks, vs) = refs[3 : 3 + gy], refs[3 + gy :]
     ctx_dev, head_dim = caches[0].shape[1], caches[0].shape[2] // 2
     heads_dev = parts[0].shape[1] // head_dim
     row = lax.axis_index("gy")
@@ -163,7 +178,7 @@
             mine = jnp.where(row == a, values[a * each : (a + 1) * each], mine)
         return mine
 
-    cosine, sine = tables[0], tables[1]
+    cosine, sine, lengths = tables[0], tables[1], tables[2]
     fresh = own_rows(keyval[...])
     fresh = jnp.concatenate(
         [rotated_halves(fresh[:, :head_dim], cosine, sine), fresh[:, head_dim:]], 1
@@ -188,7 +203,7 @@
     scores = []
     for db in range(gz):
         block = lax.axis_index("gx") * gz + (lax.axis_index("gz") ^ db)
-        positions = block * ctx_dev + iota((many, ctx_dev), 1)
+        positions = (block * ctx_dev + iota((many, ctx_dev), 1)).astype(F32)
         found = jnp.full((many, ctx_dev), masked_fill, F32)
         for s in range(seq_dev):
             value = lax.dot_general(
@@ -197,7 +212,7 @@
                 (((1,), (1,)), ((), ())),
                 preferred_element_type=F32,
             )
-            found = jnp.where((positions < lengths[s]) & (sequence == s), value * scale, found)
+            found = jnp.where((positions < lengths[s : s + 1, :1]) & (sequence == s), value * scale, found)
         scores.append(found)
     top = own
     for found in scores:
@@ -226,17 +241,30 @@
 
 def down_kernel(dims, stats, *refs):
     gx, seq_dev, order = dims
-    parts, (down, result, hidden) = refs[:gx], refs[gx:]
+    parts, (down, result, hidden, left) = refs[:gx], refs[gx:]
     rows, ff_dev = hidden.shape
-    slab = min(ff_dev, 1024)
+    stay = parts[0].shape[1] - ff_dev - SPARE
+    slab = ff_dev - stay or min(ff_dev, 1024)
     inverse = stats[gx][:, :1]
     shifts = [stats[step][:, :1] for step in (0, *order)]
+
+    def summed(start):
+        found = [part[:, start : start + slab] for part in parts]
+        return shifted_sum(found, shifts, seq_dev)
+
+    if stay < ff_dev:
+        left[...] = jnp.zeros_like(left)
+        blocks = [
+            [part[:, r * slab : (r + 1) * slab].astype(F32)[rows - 1 :] for r in range(rows - 1)]
+            for part in parts
+        ]
+        for r in range(rows - 1):
+            left[r : r + 1, :] = sum(
+                block[r] + shift[r : r + 1] * block[seq_dev] for block, shift in zip(blocks, shifts)
+            )
     for start in range(0, ff_dev, slab):
-        sums = []
-        for base in (0, rows):
-            found = [part[base : base + rows, start : start + slab] for part in parts]
-            sums.append(shifted_sum(found, shifts, seq_dev) * inverse)
-        gate, upward = sums
+        gate = summed(start) * inverse
+        upward = (summed(ff_dev + start) if start < stay else left[...]) * inverse
         hidden[:, start : start + slab] = (gate / (1.0 + jnp.exp(-gate)) * upward).astype(BF16)
 
     def store(part, value):
@@ -368,15 +396,17 @@
         in_specs=[VMEM] * gx,
         out_specs=(VMEM,) * 3,
         compiler_params=params(LIMIT),
-        cost_estimate=cost(1e8, 1e5),
+        cost_estimate=cost(100000000, 100000),
         name="query_sum",
     )(*sums)
     queries = with_others(query, "gy")
+    stay = packed_split(rows, each, ff_dev)
     both = pl.pallas_call(
         up_kernel,
-        out_shape=jax.ShapeDtypeStruct((2 * rows, ff_dev), BF16),
+        out_shape=jax.ShapeDtypeStruct((rows, ff_dev + stay + SPARE), BF16),
         in_specs=[VMEM] * 3 + [ANY],
         out_specs=VMEM,
+        scratch_shapes=[pltpu.VMEM((rows, ff_dev + stay), F32)],
         compiler_params=params(LIMIT),
         cost_estimate=cost(6e9, 16.8e6),
         name="up",
@@ -384,20 +414,22 @@
     order = (1, 3, 2) if gx == 4 else tuple(range(1, gx))
     parts = with_others(both, "gx", order)
 
-    angle = lengths.astype(F32)[:, None] * rotary_base**exponents
-    angle = jnp.pad(angle, ((0, 1), (0, 0)))
-    tables = jnp.stack([jnp.cos(angle), jnp.sin(angle)])
+    position = jnp.pad(lengths.astype(F32)[:, None], ((0, 1), (0, 0)))
+    angle = position * rotary_base**exponents
+    tables = jnp.stack(
+        [jnp.cos(angle), jnp.sin(angle), jnp.broadcast_to(position, angle.shape)]
+    )
     *pieces, new_kv = pl.pallas_call(
         functools.partial(attention_kernel, (gy, gz, seq_dev)),
         out_shape=(jax.ShapeDtypeStruct((count, head_dim), BF16),) * gy
         + (jax.ShapeDtypeStruct((seq_dev, 2 * head_dim), BF16),),
-        in_specs=[VMEM] * (gz + gy) + [SMEM, VMEM, VMEM, ANY],
+        in_specs=[VMEM] * (gz + gy) + [VMEM, VMEM, ANY],
         out_specs=(VMEM,) * (gy + 1),
         scratch_shapes=[pltpu.VMEM((gy * count, head_dim), F32)] * 3,
         compiler_params=params(LIMIT),
         cost_estimate=cost(7e9, 2e6),
         name="attention",
-    )(*queries, *caches, lengths, keyval, tables, both)
+    )(*queries, *caches, keyval, tables, both)
     pieces = pieces[:1] + [
         lax.ppermute(pieces[step], "gy", [(place, place ^ step) for place in range(gy)])
         for step in range(1, gy)
@@ -409,7 +441,10 @@
         out_shape=jax.ShapeDtypeStruct((rows, width), F32),
         in_specs=[VMEM] * (gx + 2),
         out_specs=VMEM,
-        scratch_shapes=[pltpu.VMEM((rows, ff_dev), BF16)],
+        scratch_shapes=[
+            pltpu.VMEM((rows, ff_dev), BF16),
+            pltpu.VMEM((rows, max(ff_dev - stay, 128)), F32),
+        ],
         compiler_params=params(LIMIT),
         cost_estimate=cost(4e9, 16.8e6),
         name="hidden_down",

time: 40.2 us -> 39.8 us (0.990)
    pallas_call x1, Pallas kernels: 1.79 us -> 1.24 us  [body(): pl.pallas_call(functools.partial(attention_kernel, (gy, gz, seq_dev)), ou...]
  transfers between devices with their start and end apart: 15 -> 15, of which waited for: 6 -> 6; matrix products, arithmetic and copies ran while one was open for 0% -> 1% of each run, Pallas kernels for 22% -> 21%
where the time goes in v7:
time: 39.8 us; the launch traced here: 39.7 us
  starting transfers between devices  17.7 us (44%)
  Pallas kernels  10.3 us (26%)
  waiting for transfers between devices  6.84 us (17%)
  local copies, waits for them, and re-layouts  3.17 us (8%)
  between operations  0.92 us (2%)
  other arithmetic  0.77 us (2%)
    ppermute x14, starting transfers between devices, with_others(): lax.ppermute(values, axis, [(place, place ^ step) for place in range(size)])  16.8 us
    ppermute x14, waiting for transfers between devices, with_others(): lax.ppermute(values, axis, [(place, place ^ step) for place in range(size)])  4.05 us
    unnamed x38, local copies, waits for them, and re-layouts  3.09 us
    ppermute x1, waiting for transfers between devices, body(): lax.ppermute(pieces[step], 'gy', [(place, place ^ step) for place in rang...  2.79 us
    pallas_call x1, Pallas kernels, body(): pl.pallas_call(functools.partial(down_kernel, (gx, seq_dev, order)), out_...  2.55 us
    pallas_call x1, Pallas kernels, body(): pl.pallas_call(up_kernel, out_shape=jax.ShapeDtypeStruct((rows, ff_dev +...  2.3 us
    pallas_call x1, Pallas kernels, body(): pl.pallas_call(gate_kernel, out_shape=jax.ShapeDtypeStruct((rows, ff_dev)...  2.28 us
    pallas_call x1, Pallas kernels, body(): pl.pallas_call(functools.partial(attention_kernel, (gy, gz, seq_dev)), ou...  1.24 us
  transfers between devices with their start and end apart: 15, of which 6 were waited for; matrix products, arithmetic and copies ran while one was open for 1% of the time, Pallas kernels for 21%

profile of v7, /device:TPU:0, one launch (start us, length us, event | category | flops | bytes accessed | tf_op | source)
XLA Modules:
  0.0 39.7 jit_solution(16092051202430796210)
XLA Ops:
  0.7 0.7 %copy-done.1 = bf16[6,2048]{1,0:T(8,128)(2,1)S(1)} copy-done((bf16[6,2048]{1,0:T(8,128)(2,1)S(1)}, bf16[6,2048]{1,0:T(8,128)(2,1)}, u32[]{:S(2)}) %copy-start.1) | copy-done | bytes 24600
  1.4 1.1 %copy-done.3 = bf16[2048,512]{1,0:T(8,128)(2,1)S(1)} copy-done((bf16[2048,512]{1,0:T(8,128)(2,1)S(1)}, bf16[2048,512]{1,0:T(8,128)(2,1)}, u32[]{:S(2)}) %copy-start.3) | copy-done | bytes 2097176
  2.5 1.2 %copy-done.2 = bf16[2048,1024]{1,0:T(8,128)(2,1)S(1)} copy-done((bf16[2048,1024]{1,0:T(8,128)(2,1)S(1)}, bf16[2048,1024]{1,0:T(8,128)(2,1)}, u32[]{:S(2)}) %copy-start.2) | copy-done | bytes 4194328
  3.8 1.0 %norm_query.1 = (bf16[8,1664]{1,0:T(8,128)(2,1)S(1)}, bf16[8,2048]{1,0:T(8,128)(2,1)S(1)}) custom-call(bf16[6,2048]{1,0:T(8,128)(2,1)S(1)} %copy-done.1, f32[1,2048]{1,0:T(1,128)S(1)} %bitcast.16, bf16[2048,1024]{1,0:T(8,128)(2,1)S(1)} %copy-done.2, bf16[2048,512]{1,0:T(8,128)(2,1)S(1)} %copy-done.3, f32[1,128]{1,0:T(1,128)S(1)} %exponents.1.after), custom_call_target="tpu_custom_call" | custom-call | flops 7000000000 | tf_op jit(solution)/shard_map/norm_query/pallas_call | solution.py:365
  4.8 5.1 %collective-permute-start.2 = (bf16[8,1664]{1,0:T(8,128)(2,1)S(1)}, bf16[8,1664]{1,0:T(8,128)(2,1)S(1)}, u32[]{:S(2)}, u32[]{:S(2)}) collective-permute-start(bf16[8,1664]{1,0:T(8,128)(2,1)S(1)} %get-tuple-element.12.refs_0_), channel_id=1, source_target_pairs={{0,12},{4,8},{8,4},{12,0},{1,13},{5,9},{9,5},{13,1},{2,14},{6,10},... | collective-permute-start | bytes 79880 | tf_op jit(solution)/shard_map/ppermute | solution.py:321
  9.8 0.6 %collective-permute-start = (bf16[8,1664]{1,0:T(8,128)(2,1)S(1)}, bf16[8,1664]{1,0:T(8,128)(2,1)S(1)}, u32[]{:S(2)}, u32[]{:S(2)}) collective-permute-start(bf16[8,1664]{1,0:T(8,128)(2,1)S(1)} %get-tuple-element.12.refs_0_), channel_id=1, source_target_pairs={{0,4},{4,0},{8,12},{12,8},{1,5},{5,1},{9,13},{13,9},{2,6},{6,2},{1... | collective-permute-start | bytes 79880 | tf_op jit(solution)/shard_map/ppermute | solution.py:321
  10.5 2.3 %gate.1 = bf16[8,4096]{1,0:T(8,128)(2,1)S(1)} custom-call(bf16[8,2048]{1,0:T(8,128)(2,1)S(1)} %get-tuple-element.15.lhs, bf16[2048,4096]{1,0:T(8,128)(2,1)S(1)} %bitcast.13), custom_call_target="tpu_custom_call" | custom-call | flops 6000000000 | bytes 16800000 | tf_op jit(solution)/shard_map/gate/pallas_call | solution.py:380
  13.0 1.6 %collective-permute-done.1.refs_2_ = bf16[8,1664]{1,0:T(8,128)(2,1)S(1)} collective-permute-done((bf16[8,1664]{1,0:T(8,128)(2,1)S(1)}, bf16[8,1664]{1,0:T(8,128)(2,1)S(1)}, u32[]{:S(2)}, u32[]{:S(2)}) %collective-permute-start.1) | collective-permute-done | bytes 26656 | tf_op jit(solution)/shard_map/ppermute | solution.py:321
  14.7 1.6 %collective-permute-start.3 = (bf16[8,1024]{1,0:T(8,128)(2,1)S(1)}, bf16[8,1024]{1,0:T(8,128)(2,1)S(1)}, u32[]{:S(2)}, u32[]{:S(2)}) collective-permute-start(bf16[8,1024]{1,0:T(8,128)(2,1)S(1)} %get-tuple-element.13.after.refs_0_), channel_id=1, source_target_pairs={{0,2},{2,0},{1,3},{3,1},{4,6},{6,4},{5,7},{7,5},{8,10},{10,8},{9,1... | collective-permute-start | bytes 49160 | tf_op jit(solution)/shard_map/ppermute | solution.py:321
  16.3 2.3 %up.1.refs_6_.refs_0_ = bf16[8,7680]{1,0:T(8,128)(2,1)S(1)} custom-call(bf16[8,2048]{1,0:T(8,128)(2,1)S(1)} %get-tuple-element.15.lhs, bf16[2048,4096]{1,0:T(8,128)(2,1)S(1)} %bitcast.15, bf16[8,4096]{1,0:T(8,128)(2,1)S(1)} %gate.1, bf16[8,1024]{1,0:T(8,128)(2,1)S(1)} %get-tuple-element.13.after.refs_0_), custom_call_target="tpu_custom_call" | custom-call | flops 6000000000 | bytes 16800000 | tf_op jit(solution)/shard_map/up/pallas_call | solution.py:404
  18.6 2.1 %collective-permute-start.11 = (bf16[8,7680]{1,0:T(8,128)(2,1)S(1)}, bf16[8,7680]{1,0:T(8,128)(2,1)S(1)}, u32[]{:S(2)}, u32[]{:S(2)}) collective-permute-start(bf16[8,7680]{1,0:T(8,128)(2,1)S(1)} %up.1.refs_6_.refs_0_), channel_id=1, source_target_pairs={{0,8},{4,12},{8,0},{12,4},{1,9},{5,13},{9,1},{13,5},{2,10},{6,14},... | collective-permute-start | bytes 368648 | tf_op jit(solution)/shard_map/ppermute | solution.py:321
  20.7 0.6 %collective-permute-start.10 = (bf16[8,7680]{1,0:T(8,128)(2,1)S(1)}, bf16[8,7680]{1,0:T(8,128)(2,1)S(1)}, u32[]{:S(2)}, u32[]{:S(2)}) collective-permute-start(bf16[8,7680]{1,0:T(8,128)(2,1)S(1)} %up.1.refs_6_.refs_0_), channel_id=1, source_target_pairs={{0,12},{4,8},{8,4},{12,0},{1,13},{5,9},{9,5},{13,1},{2,14},{6,10},... | collective-permute-start | bytes 368648 | tf_op jit(solution)/shard_map/ppermute | solution.py:321
  21.3 0.9 %collective-permute-start.9 = (bf16[8,7680]{1,0:T(8,128)(2,1)S(1)}, bf16[8,7680]{1,0:T(8,128)(2,1)S(1)}, u32[]{:S(2)}, u32[]{:S(2)}) collective-permute-start(bf16[8,7680]{1,0:T(8,128)(2,1)S(1)} %up.1.refs_6_.refs_0_), channel_id=1, source_target_pairs={{0,4},{4,0},{8,12},{12,8},{1,5},{5,1},{9,13},{13,9},{2,6},{6,2},{1... | collective-permute-start | bytes 368648 | tf_op jit(solution)/shard_map/ppermute | solution.py:321
  22.2 1.2 %attention.1 = (bf16[16,256]{1,0:T(8,128)(2,1)S(1)}, bf16[16,256]{1,0:T(8,128)(2,1)S(1)}, bf16[3,512]{1,0:T(4,128)(2,1)}) custom-call(bf16[8,1024]{1,0:T(8,128)(2,1)S(1)} %get-tuple-element.13.after.refs_0_, bf16[8,1024]{1,0:T(8,128)(2,1)S(1)} %collective-permute-done.3.refs_1_, bf16[3,256,512]{2,1,0:T(8,128)(2,1)S(1)} %copy-done.4, ...), custom_call_target="tpu_custom_call" | custom-call | flops 7000000000 | bytes 2000000 | tf_op jit(solution)/shard_map/attention/pallas_call | solution.py:422
  23.4 0.9 %collective-permute-start.5 = (bf16[16,256]{1,0:T(8,128)(2,1)S(1)}, bf16[16,256]{1,0:T(8,128)(2,1)S(1)}, u32[]{:S(2)}, u32[]{:S(2)}) collective-permute-start(bf16[16,256]{1,0:T(8,128)(2,1)S(1)} %get-tuple-element.17), channel_id=1, source_target_pairs={{0,2},{2,0},{1,3},{3,1},{4,6},{6,4},{5,7},{7,5},{8,10},{10,8},{9,1... | collective-permute-start | bytes 24584 | tf_op jit(solution)/shard_map/ppermute | solution.py:434
  24.3 2.8 %collective-permute-done.5 = bf16[16,256]{1,0:T(8,128)(2,1)S(1)} collective-permute-done((bf16[16,256]{1,0:T(8,128)(2,1)S(1)}, bf16[16,256]{1,0:T(8,128)(2,1)S(1)}, u32[]{:S(2)}, u32[]{:S(2)}) %collective-permute-start.5) | collective-permute-done | bytes 8224 | tf_op jit(solution)/shard_map/ppermute | solution.py:434
  27.1 2.4 %collective-permute-start.8 = (bf16[2,16,256]{2,1,0:T(8,128)(2,1)S(1)}, bf16[2,16,256]{2,1,0:T(8,128)(2,1)S(1)}, u32[]{:S(2)}, u32[]{:S(2)}) collective-permute-start(bf16[2,16,256]{2,1,0:T(8,128)(2,1)S(1)} %pad_maximum_fusion.refs_0_), channel_id=1, source_target_pairs={{0,12},{4,8},{8,4},{12,0},{1,13},{5,9},{9,5},{13,1},{2,14},{6,10},... | collective-permute-start | bytes 49160 | tf_op jit(solution)/shard_map/ppermute | solution.py:321
  29.5 0.5 %collective-permute-start.7 = (bf16[2,16,256]{2,1,0:T(8,128)(2,1)S(1)}, bf16[2,16,256]{2,1,0:T(8,128)(2,1)S(1)}, u32[]{:S(2)}, u32[]{:S(2)}) collective-permute-start(bf16[2,16,256]{2,1,0:T(8,128)(2,1)S(1)} %pad_maximum_fusion.refs_0_), channel_id=1, source_target_pairs={{0,8},{4,12},{8,0},{12,4},{1,9},{5,13},{9,1},{13,5},{2,10},{6,14},... | collective-permute-start | bytes 49160 | tf_op jit(solution)/shard_map/ppermute | solution.py:321
  30.3 1.2 %collective-permute-start.6 = (bf16[2,16,256]{2,1,0:T(8,128)(2,1)S(1)}, bf16[2,16,256]{2,1,0:T(8,128)(2,1)S(1)}, u32[]{:S(2)}, u32[]{:S(2)}) collective-permute-start(bf16[2,16,256]{2,1,0:T(8,128)(2,1)S(1)} %pad_maximum_fusion.refs_0_), channel_id=1, source_target_pairs={{0,4},{4,0},{8,12},{12,8},{1,5},{5,1},{9,13},{13,9},{2,6},{6,2},{1... | collective-permute-start | bytes 49160 | tf_op jit(solution)/shard_map/ppermute | solution.py:321
  31.5 2.6 %hidden_down.1.refs_5_ = f32[8,2048]{1,0:T(8,128)S(1)} custom-call(f32[5,8,128]{2,1,0:T(8,128)S(1)} %get-tuple-element.18.stats, bf16[8,7680]{1,0:T(8,128)(2,1)S(1)} %up.1.refs_6_.refs_0_, bf16[8,7680]{1,0:T(8,128)(2,1)S(1)} %collective-permute-done.9.refs_1_, bf16[8,7680]{1,0:T(8,128)(2,1)S(1)} %collective-permute-done.10.refs_2_, ...), custom_call_target="tpu_custom_call" | custom-call | flops 4000000000 | bytes 16800000 | tf_op jit(solution)/shard_map/hidden_down/pallas_call | solution.py:439
  34.2 0.8 %out_projection.1 = (f32[6,2048]{1,0:T(8,128)S(1)}, bf16[6,2048]{1,0:T(8,128)(2,1)S(1)}) custom-call(bf16[2,16,256]{2,1,0:T(8,128)(2,1)S(1)} %pad_maximum_fusion.refs_0_, bf16[2,16,256]{2,1,0:T(8,128)(2,1)S(1)} %collective-permute-done.6.refs_1_, bf16[2,16,256]{2,1,0:T(8,128)(2,1)S(1)} %collective-permute-done.7.refs_2_, ...), custom_call_target="tpu_custom_call" | custom-call | flops 1000000000 | bytes 4000000 | tf_op jit(solution)/shard_map/out_projection/pallas_call | solution.py:452
  35.0 1.5 %collective-permute-start.13 = (bf16[6,2048]{1,0:T(8,128)(2,1)S(1)}, bf16[6,2048]{1,0:T(8,128)(2,1)S(1)}, u32[]{:S(2)}, u32[]{:S(2)}) collective-permute-start(bf16[6,2048]{1,0:T(8,128)(2,1)S(1)} %get-tuple-element.20), channel_id=1, source_target_pairs={{0,2},{1,3},{2,0},{3,1},{4,6},{5,7},{6,4},{7,5},{8,10},{9,11},{10,... | collective-permute-start | bytes 73736 | tf_op jit(solution)/shard_map/ppermute | solution.py:321
  36.9 1.8 %collective-permute-done.14 = bf16[6,2048]{1,0:T(8,128)(2,1)S(1)} collective-permute-done((bf16[6,2048]{1,0:T(8,128)(2,1)S(1)}, bf16[6,2048]{1,0:T(8,128)(2,1)S(1)}, u32[]{:S(2)}, u32[]{:S(2)}) %collective-permute-start.14) | collective-permute-done | bytes 24608 | tf_op jit(solution)/shard_map/ppermute | solution.py:321
  39.0 0.6 %add_convert_fusion = bf16[6,2048]{1,0:T(8,128)(2,1)} fusion(bf16[6,2048]{1,0:T(8,128)(2,1)S(1)} %collective-permute-done.14, bf16[6,2048]{1,0:T(8,128)(2,1)S(1)} %collective-permute-done.13, f32[6,2048]{1,0:T(8,128)S(1)} %get-tuple-element.19, bf16[6,2048]{1,0:T(8,128)(2,1)S(1)} %collective-permute-done.12, bf16[6,2048]{1,0:T(8,128)(2,1)S(1)} %copy-done.1), kind=kLoop, calls=%fused_computation | loop fusion | flops 110592 | bytes 172032 | tf_op jit(solution)/shard_map/convert_element_type | solution.py:467
  (63 shorter events, 1.6 us)
Async XLA Ops:
  0.7 9.8 %slice-start.4 = ((s8[16777216]{0:T(1024)(128)(4,1)}), s8[4194304]{0:T(1024)(128)(4,1)S(1)}, s32[]{:S(2)}) async-start(s8[16777216]{0:T(1024)(128)(4,1)} %bitcast.12), calls=%async_computation.4 | async-start | bytes 8388608
  0.7 9.8 %slice-start.5 = ((s8[16777216]{0:T(1024)(128)(4,1)}), s8[4194304]{0:T(1024)(128)(4,1)S(1)}, s32[]{:S(2)}) async-start(s8[16777216]{0:T(1024)(128)(4,1)} %bitcast.12), calls=%async_computation.5 | async-start | bytes 8388608
  0.7 9.7 %copy-start.6 = (s32[3]{0:T(128)S(1)}, s32[3]{0:T(128)}, u32[]{:S(2)}) copy-start(s32[3]{0:T(128)} %param.19) | copy-start | bytes 40
  3.7 12.5 %slice-start.8 = ((s8[16777216]{0:T(1024)(128)(4,1)}), s8[4194304]{0:T(1024)(128)(4,1)S(1)}, s32[]{:S(2)}) async-start(s8[16777216]{0:T(1024)(128)(4,1)} %bitcast.14), calls=%async_computation.8 | async-start | bytes 8388608
  3.7 12.5 %slice-start.9 = ((s8[16777216]{0:T(1024)(128)(4,1)}), s8[4194304]{0:T(1024)(128)(4,1)S(1)}, s32[]{:S(2)}) async-start(s8[16777216]{0:T(1024)(128)(4,1)} %bitcast.14), calls=%async_computation.9 | async-start | bytes 8388608
  3.7 12.5 %slice-start.10 = ((s8[16777216]{0:T(1024)(128)(4,1)}), s8[4194304]{0:T(1024)(128)(4,1)S(1)}, s32[]{:S(2)}) async-start(s8[16777216]{0:T(1024)(128)(4,1)} %bitcast.14), calls=%async_computation.10 | async-start | bytes 8388608
  4.8 8.2 %collective-permute-start.2 = (bf16[8,1664]{1,0:T(8,128)(2,1)S(1)}, bf16[8,1664]{1,0:T(8,128)(2,1)S(1)}, u32[]{:S(2)}, u32[]{:S(2)}) collective-permute-start(bf16[8,1664]{1,0:T(8,128)(2,1)S(1)} %get-tuple-element.12.refs_0_), channel_id=1, source_target_pairs={{0,12},{4,8},{8,4},{12,0},{1,13},{5,9},{9,5},{13,1},{2,14},{6,10},... | collective-permute-start | bytes 79880 | tf_op jit(solution)/shard_map/ppermute | solution.py:321
  9.8 4.7 %collective-permute-start.1 = (bf16[8,1664]{1,0:T(8,128)(2,1)S(1)}, bf16[8,1664]{1,0:T(8,128)(2,1)S(1)}, u32[]{:S(2)}, u32[]{:S(2)}) collective-permute-start(bf16[8,1664]{1,0:T(8,128)(2,1)S(1)} %get-tuple-element.12.refs_0_), channel_id=1, source_target_pairs={{0,8},{4,12},{8,0},{12,4},{1,9},{5,13},{9,1},{13,5},{2,10},{6,14},... | collective-permute-start | bytes 79880 | tf_op jit(solution)/shard_map/ppermute | solution.py:321
  9.8 4.7 %collective-permute-start = (bf16[8,1664]{1,0:T(8,128)(2,1)S(1)}, bf16[8,1664]{1,0:T(8,128)(2,1)S(1)}, u32[]{:S(2)}, u32[]{:S(2)}) collective-permute-start(bf16[8,1664]{1,0:T(8,128)(2,1)S(1)} %get-tuple-element.12.refs_0_), channel_id=1, source_target_pairs={{0,4},{4,0},{8,12},{12,8},{1,5},{5,1},{9,13},{13,9},{2,6},{6,2},{1... | collective-permute-start | bytes 79880 | tf_op jit(solution)/shard_map/ppermute | solution.py:321
  10.4 11.8 %collective-permute-start.4 = (bf16[3,256,512]{2,1,0:T(8,128)(2,1)S(1)}, bf16[3,256,512]{2,1,0:T(8,128)(2,1)S(1)}, u32[]{:S(2)}, u32[]{:S(2)}) collective-permute-start(bf16[3,256,512]{2,1,0:T(8,128)(2,1)S(1)} %copy-done.4), channel_id=1, source_target_pairs={{0,1},{1,0},{2,3},{3,2},{4,5},{5,4},{6,7},{7,6},{8,9},{9,8},{10,11... | collective-permute-start | bytes 2359304 | tf_op jit(solution)/shard_map/ppermute | solution.py:321
  14.7 7.5 %collective-permute-start.3 = (bf16[8,1024]{1,0:T(8,128)(2,1)S(1)}, bf16[8,1024]{1,0:T(8,128)(2,1)S(1)}, u32[]{:S(2)}, u32[]{:S(2)}) collective-permute-start(bf16[8,1024]{1,0:T(8,128)(2,1)S(1)} %get-tuple-element.13.after.refs_0_), channel_id=1, source_target_pairs={{0,2},{2,0},{1,3},{3,1},{4,6},{6,4},{5,7},{7,5},{8,10},{10,8},{9,1... | collective-permute-start | bytes 49160 | tf_op jit(solution)/shard_map/ppermute | solution.py:321
  16.3 15.2 %slice-start = ((s8[16777216]{0:T(1024)(128)(4,1)}), s8[4194304]{0:T(1024)(128)(4,1)S(1)}, s32[]{:S(2)}) async-start(s8[16777216]{0:T(1024)(128)(4,1)} %bitcast.9), calls=%async_computation | async-start | bytes 8388608
  16.3 15.2 %slice-start.1 = ((s8[16777216]{0:T(1024)(128)(4,1)}), s8[4194304]{0:T(1024)(128)(4,1)S(1)}, s32[]{:S(2)}) async-start(s8[16777216]{0:T(1024)(128)(4,1)} %bitcast.9), calls=%async_computation.1 | async-start | bytes 8388608
  18.6 11.7 %collective-permute-start.11 = (bf16[8,7680]{1,0:T(8,128)(2,1)S(1)}, bf16[8,7680]{1,0:T(8,128)(2,1)S(1)}, u32[]{:S(2)}, u32[]{:S(2)}) collective-permute-start(bf16[8,7680]{1,0:T(8,128)(2,1)S(1)} %up.1.refs_6_.refs_0_), channel_id=1, source_target_pairs={{0,8},{4,12},{8,0},{12,4},{1,9},{5,13},{9,1},{13,5},{2,10},{6,14},... | collective-permute-start | bytes 368648 | tf_op jit(solution)/shard_map/ppermute | solution.py:321
  20.7 10.8 %collective-permute-start.10 = (bf16[8,7680]{1,0:T(8,128)(2,1)S(1)}, bf16[8,7680]{1,0:T(8,128)(2,1)S(1)}, u32[]{:S(2)}, u32[]{:S(2)}) collective-permute-start(bf16[8,7680]{1,0:T(8,128)(2,1)S(1)} %up.1.refs_6_.refs_0_), channel_id=1, source_target_pairs={{0,12},{4,8},{8,4},{12,0},{1,13},{5,9},{9,5},{13,1},{2,14},{6,10},... | collective-permute-start | bytes 368648 | tf_op jit(solution)/shard_map/ppermute | solution.py:321
  21.3 10.2 %collective-permute-start.9 = (bf16[8,7680]{1,0:T(8,128)(2,1)S(1)}, bf16[8,7680]{1,0:T(8,128)(2,1)S(1)}, u32[]{:S(2)}, u32[]{:S(2)}) collective-permute-start(bf16[8,7680]{1,0:T(8,128)(2,1)S(1)} %up.1.refs_6_.refs_0_), channel_id=1, source_target_pairs={{0,4},{4,0},{8,12},{12,8},{1,5},{5,1},{9,13},{13,9},{2,6},{6,2},{1... | collective-permute-start | bytes 368648 | tf_op jit(solution)/shard_map/ppermute | solution.py:321
  22.2 12.0 %copy-start = (bf16[1024,2048]{1,0:T(8,128)(2,1)S(1)}, bf16[1024,2048]{1,0:T(8,128)(2,1)}, u32[]{:S(2)}) copy-start(bf16[1024,2048]{1,0:T(8,128)(2,1)} %refs_4_.3) | copy-start | bytes 12582916
  23.4 3.7 %collective-permute-start.5 = (bf16[16,256]{1,0:T(8,128)(2,1)S(1)}, bf16[16,256]{1,0:T(8,128)(2,1)S(1)}, u32[]{:S(2)}, u32[]{:S(2)}) collective-permute-start(bf16[16,256]{1,0:T(8,128)(2,1)S(1)} %get-tuple-element.17), channel_id=1, source_target_pairs={{0,2},{2,0},{1,3},{3,1},{4,6},{6,4},{5,7},{7,5},{8,10},{10,8},{9,1... | collective-permute-start | bytes 24584 | tf_op jit(solution)/shard_map/ppermute | solution.py:434
  27.1 7.0 %collective-permute-start.8 = (bf16[2,16,256]{2,1,0:T(8,128)(2,1)S(1)}, bf16[2,16,256]{2,1,0:T(8,128)(2,1)S(1)}, u32[]{:S(2)}, u32[]{:S(2)}) collective-permute-start(bf16[2,16,256]{2,1,0:T(8,128)(2,1)S(1)} %pad_maximum_fusion.refs_0_), channel_id=1, source_target_pairs={{0,12},{4,8},{8,4},{12,0},{1,13},{5,9},{9,5},{13,1},{2,14},{6,10},... | collective-permute-start | bytes 49160 | tf_op jit(solution)/shard_map/ppermute | solution.py:321
  29.5 4.7 %collective-permute-start.7 = (bf16[2,16,256]{2,1,0:T(8,128)(2,1)S(1)}, bf16[2,16,256]{2,1,0:T(8,128)(2,1)S(1)}, u32[]{:S(2)}, u32[]{:S(2)}) collective-permute-start(bf16[2,16,256]{2,1,0:T(8,128)(2,1)S(1)} %pad_maximum_fusion.refs_0_), channel_id=1, source_target_pairs={{0,8},{4,12},{8,0},{12,4},{1,9},{5,13},{9,1},{13,5},{2,10},{6,14},... | collective-permute-start | bytes 49160 | tf_op jit(solution)/shard_map/ppermute | solution.py:321
  30.3 3.9 %collective-permute-start.6 = (bf16[2,16,256]{2,1,0:T(8,128)(2,1)S(1)}, bf16[2,16,256]{2,1,0:T(8,128)(2,1)S(1)}, u32[]{:S(2)}, u32[]{:S(2)}) collective-permute-start(bf16[2,16,256]{2,1,0:T(8,128)(2,1)S(1)} %pad_maximum_fusion.refs_0_), channel_id=1, source_target_pairs={{0,4},{4,0},{8,12},{12,8},{1,5},{5,1},{9,13},{13,9},{2,6},{6,2},{1... | collective-permute-start | bytes 49160 | tf_op jit(solution)/shard_map/ppermute | solution.py:321
  35.0 3.7 %collective-permute-start.14 = (bf16[6,2048]{1,0:T(8,128)(2,1)S(1)}, bf16[6,2048]{1,0:T(8,128)(2,1)S(1)}, u32[]{:S(2)}, u32[]{:S(2)}) collective-permute-start(bf16[6,2048]{1,0:T(8,128)(2,1)S(1)} %get-tuple-element.20), channel_id=1, source_target_pairs={{0,3},{1,2},{2,1},{3,0},{4,7},{5,6},{6,5},{7,4},{8,11},{9,10},{10,... | collective-permute-start | bytes 73736 | tf_op jit(solution)/shard_map/ppermute | solution.py:321
  35.0 4.0 %collective-permute-start.13 = (bf16[6,2048]{1,0:T(8,128)(2,1)S(1)}, bf16[6,2048]{1,0:T(8,128)(2,1)S(1)}, u32[]{:S(2)}, u32[]{:S(2)}) collective-permute-start(bf16[6,2048]{1,0:T(8,128)(2,1)S(1)} %get-tuple-element.20), channel_id=1, source_target_pairs={{0,2},{1,3},{2,0},{3,1},{4,6},{5,7},{6,4},{7,5},{8,10},{9,11},{10,... | collective-permute-start | bytes 73736 | tf_op jit(solution)/shard_map/ppermute | solution.py:321
  36.5 2.5 %collective-permute-start.12 = (bf16[6,2048]{1,0:T(8,128)(2,1)S(1)}, bf16[6,2048]{1,0:T(8,128)(2,1)S(1)}, u32[]{:S(2)}, u32[]{:S(2)}) collective-permute-start(bf16[6,2048]{1,0:T(8,128)(2,1)S(1)} %get-tuple-element.20), channel_id=1, source_target_pairs={{0,1},{1,0},{2,3},{3,2},{4,5},{5,4},{6,7},{7,6},{8,9},{9,8},{10,11... | collective-permute-start | bytes 73736 | tf_op jit(solution)/shard_map/ppermute | solution.py:321
  (10 other events, 56.4 us)

commit v8 on v7

--- a/solution.py
+++ b/solution.py
@@ -275,7 +275,7 @@
 
 def out_kernel(dims, *refs):
     gx, gy, seq_dev = dims
-    parts, (out_weight, partial, total, share, turned, att) = refs[:gx], refs[gx:]
+    parts, (out_weight, partial, tokens, total, share, turned, att) = refs[:gx], refs[gx:]
     each = seq_dev + 1
     count, head_dim = parts[0].shape[1:]
     sequence = iota((count, 1), 0) % each
@@ -312,6 +312,7 @@
     for a in range(gy):
         total[a * seq_dev : (a + 1) * seq_dev, :] = result[a * each : a * each + seq_dev]
     share[...] = total[...].astype(BF16)
+    total[...] += tokens[...].astype(F32)
 
 
 def with_others(values, axis, order=None):
@@ -455,17 +456,16 @@
             jax.ShapeDtypeStruct((seqs, width), F32),
             jax.ShapeDtypeStruct((seqs, width), BF16),
         ),
-        in_specs=[VMEM] * (gx + 2),
+        in_specs=[VMEM] * (gx + 3),
         out_specs=(VMEM, VMEM),
         scratch_shapes=[pltpu.VMEM((gy, each, q_dev), F32), pltpu.VMEM((rows, q_dev), F32)],
         compiler_params=params(LIMIT if gx <= FEW else 4 * LIMIT),
         cost_estimate=cost(1e9, 4e6),
         name="out_projection",
-    )(*pieces, out_weight, partial)
+    )(*pieces, out_weight, partial, tokens)
     for other in with_others(share, ("gy", "gz"))[1:]:
         total = total + other.astype(F32)
-    mixed = (tokens.astype(F32) + total).astype(BF16)
-    return (mixed, new_kv)
+    return (total.astype(BF16), new_kv)
 
 
 def solution(mesh):

time: 39.8 us -> 39.8 us (level)
  no operation moved by 1% of the time
where the time goes in v8:
time: 39.8 us; the launch traced here: 39.7 us
  starting transfers between devices  17.7 us (44%)
  Pallas kernels  10.3 us (26%)
  waiting for transfers between devices  6.84 us (17%)
  local copies, waits for them, and re-layouts  3.17 us (8%)
  between operations  0.92 us (2%)
  other arithmetic  0.77 us (2%)
    ppermute x14, starting transfers between devices, with_others(): lax.ppermute(values, axis, [(place, place ^ step) for place in range(size)])  16.8 us
    ppermute x14, waiting for transfers between devices, with_others(): lax.ppermute(values, axis, [(place, place ^ step) for place in range(size)])  4.05 us
    unnamed x38, local copies, waits for them, and re-layouts  3.09 us
    ppermute x1, waiting for transfers between devices, body(): lax.ppermute(pieces[step], 'gy', [(place, place ^ step) for place in rang...  2.79 us
    pallas_call x1, Pallas kernels, body(): pl.pallas_call(functools.partial(down_kernel, (gx, seq_dev, order)), out_...  2.55 us
    pallas_call x1, Pallas kernels, body(): pl.pallas_call(up_kernel, out_shape=jax.ShapeDtypeStruct((rows, ff_dev +...  2.3 us
    pallas_call x1, Pallas kernels, body(): pl.pallas_call(gate_kernel, out_shape=jax.ShapeDtypeStruct((rows, ff_dev)...  2.28 us
    pallas_call x1, Pallas kernels, body(): pl.pallas_call(functools.partial(attention_kernel, (gy, gz, seq_dev)), ou...  1.24 us
  transfers between devices with their start and end apart: 15, of which 6 were waited for; matrix products, arithmetic and copies ran while one was open for 1% of the time, Pallas kernels for 21%

profile of v8, /device:TPU:0, one launch (start us, length us, event | category | flops | bytes accessed | tf_op | source)
XLA Modules:
  0.0 39.7 jit_solution(12354820315704419514)
XLA Ops:
  0.7 0.7 %copy-done.1 = bf16[6,2048]{1,0:T(8,128)(2,1)S(1)} copy-done((bf16[6,2048]{1,0:T(8,128)(2,1)S(1)}, bf16[6,2048]{1,0:T(8,128)(2,1)}, u32[]{:S(2)}) %copy-start.1) | copy-done | bytes 24600
  1.4 1.1 %copy-done.3 = bf16[2048,512]{1,0:T(8,128)(2,1)S(1)} copy-done((bf16[2048,512]{1,0:T(8,128)(2,1)S(1)}, bf16[2048,512]{1,0:T(8,128)(2,1)}, u32[]{:S(2)}) %copy-start.3) | copy-done | bytes 2097176
  2.5 1.2 %copy-done.2 = bf16[2048,1024]{1,0:T(8,128)(2,1)S(1)} copy-done((bf16[2048,1024]{1,0:T(8,128)(2,1)S(1)}, bf16[2048,1024]{1,0:T(8,128)(2,1)}, u32[]{:S(2)}) %copy-start.2) | copy-done | bytes 4194328
  3.8 1.0 %norm_query.1 = (bf16[8,1664]{1,0:T(8,128)(2,1)S(1)}, bf16[8,2048]{1,0:T(8,128)(2,1)S(1)}) custom-call(bf16[6,2048]{1,0:T(8,128)(2,1)S(1)} %copy-done.1, f32[1,2048]{1,0:T(1,128)S(1)} %bitcast.16, bf16[2048,1024]{1,0:T(8,128)(2,1)S(1)} %copy-done.2, bf16[2048,512]{1,0:T(8,128)(2,1)S(1)} %copy-done.3, f32[1,128]{1,0:T(1,128)S(1)} %exponents.1.after), custom_call_target="tpu_custom_call" | custom-call | flops 7000000000 | tf_op jit(solution)/shard_map/norm_query/pallas_call | solution.py:366
  4.8 5.1 %collective-permute-start.2 = (bf16[8,1664]{1,0:T(8,128)(2,1)S(1)}, bf16[8,1664]{1,0:T(8,128)(2,1)S(1)}, u32[]{:S(2)}, u32[]{:S(2)}) collective-permute-start(bf16[8,1664]{1,0:T(8,128)(2,1)S(1)} %get-tuple-element.12.refs_0_), channel_id=1, source_target_pairs={{0,12},{4,8},{8,4},{12,0},{1,13},{5,9},{9,5},{13,1},{2,14},{6,10},... | collective-permute-start | bytes 79880 | tf_op jit(solution)/shard_map/ppermute | solution.py:322
  9.8 0.6 %collective-permute-start = (bf16[8,1664]{1,0:T(8,128)(2,1)S(1)}, bf16[8,1664]{1,0:T(8,128)(2,1)S(1)}, u32[]{:S(2)}, u32[]{:S(2)}) collective-permute-start(bf16[8,1664]{1,0:T(8,128)(2,1)S(1)} %get-tuple-element.12.refs_0_), channel_id=1, source_target_pairs={{0,4},{4,0},{8,12},{12,8},{1,5},{5,1},{9,13},{13,9},{2,6},{6,2},{1... | collective-permute-start | bytes 79880 | tf_op jit(solution)/shard_map/ppermute | solution.py:322
  10.5 2.3 %gate.1 = bf16[8,4096]{1,0:T(8,128)(2,1)S(1)} custom-call(bf16[8,2048]{1,0:T(8,128)(2,1)S(1)} %get-tuple-element.15.lhs, bf16[2048,4096]{1,0:T(8,128)(2,1)S(1)} %bitcast.13), custom_call_target="tpu_custom_call" | custom-call | flops 6000000000 | bytes 16800000 | tf_op jit(solution)/shard_map/gate/pallas_call | solution.py:381
  13.0 1.6 %collective-permute-done.1.refs_2_ = bf16[8,1664]{1,0:T(8,128)(2,1)S(1)} collective-permute-done((bf16[8,1664]{1,0:T(8,128)(2,1)S(1)}, bf16[8,1664]{1,0:T(8,128)(2,1)S(1)}, u32[]{:S(2)}, u32[]{:S(2)}) %collective-permute-start.1) | collective-permute-done | bytes 26656 | tf_op jit(solution)/shard_map/ppermute | solution.py:322
  14.7 1.6 %collective-permute-start.3 = (bf16[8,1024]{1,0:T(8,128)(2,1)S(1)}, bf16[8,1024]{1,0:T(8,128)(2,1)S(1)}, u32[]{:S(2)}, u32[]{:S(2)}) collective-permute-start(bf16[8,1024]{1,0:T(8,128)(2,1)S(1)} %get-tuple-element.13.after.refs_0_), channel_id=1, source_target_pairs={{0,2},{2,0},{1,3},{3,1},{4,6},{6,4},{5,7},{7,5},{8,10},{10,8},{9,1... | collective-permute-start | bytes 49160 | tf_op jit(solution)/shard_map/ppermute | solution.py:322
  16.3 2.3 %up.1.refs_6_.refs_0_ = bf16[8,7680]{1,0:T(8,128)(2,1)S(1)} custom-call(bf16[8,2048]{1,0:T(8,128)(2,1)S(1)} %get-tuple-element.15.lhs, bf16[2048,4096]{1,0:T(8,128)(2,1)S(1)} %bitcast.15, bf16[8,4096]{1,0:T(8,128)(2,1)S(1)} %gate.1, bf16[8,1024]{1,0:T(8,128)(2,1)S(1)} %get-tuple-element.13.after.refs_0_), custom_call_target="tpu_custom_call" | custom-call | flops 6000000000 | bytes 16800000 | tf_op jit(solution)/shard_map/up/pallas_call | solution.py:405
  18.6 2.1 %collective-permute-start.11 = (bf16[8,7680]{1,0:T(8,128)(2,1)S(1)}, bf16[8,7680]{1,0:T(8,128)(2,1)S(1)}, u32[]{:S(2)}, u32[]{:S(2)}) collective-permute-start(bf16[8,7680]{1,0:T(8,128)(2,1)S(1)} %up.1.refs_6_.refs_0_), channel_id=1, source_target_pairs={{0,8},{4,12},{8,0},{12,4},{1,9},{5,13},{9,1},{13,5},{2,10},{6,14},... | collective-permute-start | bytes 368648 | tf_op jit(solution)/shard_map/ppermute | solution.py:322
  20.7 0.6 %collective-permute-start.10 = (bf16[8,7680]{1,0:T(8,128)(2,1)S(1)}, bf16[8,7680]{1,0:T(8,128)(2,1)S(1)}, u32[]{:S(2)}, u32[]{:S(2)}) collective-permute-start(bf16[8,7680]{1,0:T(8,128)(2,1)S(1)} %up.1.refs_6_.refs_0_), channel_id=1, source_target_pairs={{0,12},{4,8},{8,4},{12,0},{1,13},{5,9},{9,5},{13,1},{2,14},{6,10},... | collective-permute-start | bytes 368648 | tf_op jit(solution)/shard_map/ppermute | solution.py:322
  21.3 0.9 %collective-permute-start.9 = (bf16[8,7680]{1,0:T(8,128)(2,1)S(1)}, bf16[8,7680]{1,0:T(8,128)(2,1)S(1)}, u32[]{:S(2)}, u32[]{:S(2)}) collective-permute-start(bf16[8,7680]{1,0:T(8,128)(2,1)S(1)} %up.1.refs_6_.refs_0_), channel_id=1, source_target_pairs={{0,4},{4,0},{8,12},{12,8},{1,5},{5,1},{9,13},{13,9},{2,6},{6,2},{1... | collective-permute-start | bytes 368648 | tf_op jit(solution)/shard_map/ppermute | solution.py:322
  22.2 1.2 %attention.1 = (bf16[16,256]{1,0:T(8,128)(2,1)S(1)}, bf16[16,256]{1,0:T(8,128)(2,1)S(1)}, bf16[3,512]{1,0:T(4,128)(2,1)}) custom-call(bf16[8,1024]{1,0:T(8,128)(2,1)S(1)} %get-tuple-element.13.after.refs_0_, bf16[8,1024]{1,0:T(8,128)(2,1)S(1)} %collective-permute-done.3.refs_1_, bf16[3,256,512]{2,1,0:T(8,128)(2,1)S(1)} %copy-done.4, ...), custom_call_target="tpu_custom_call" | custom-call | flops 7000000000 | bytes 2000000 | tf_op jit(solution)/shard_map/attention/pallas_call | solution.py:423
  23.4 0.9 %collective-permute-start.5 = (bf16[16,256]{1,0:T(8,128)(2,1)S(1)}, bf16[16,256]{1,0:T(8,128)(2,1)S(1)}, u32[]{:S(2)}, u32[]{:S(2)}) collective-permute-start(bf16[16,256]{1,0:T(8,128)(2,1)S(1)} %get-tuple-element.17), channel_id=1, source_target_pairs={{0,2},{2,0},{1,3},{3,1},{4,6},{6,4},{5,7},{7,5},{8,10},{10,8},{9,1... | collective-permute-start | bytes 24584 | tf_op jit(solution)/shard_map/ppermute | solution.py:435
  24.3 2.8 %collective-permute-done.5 = bf16[16,256]{1,0:T(8,128)(2,1)S(1)} collective-permute-done((bf16[16,256]{1,0:T(8,128)(2,1)S(1)}, bf16[16,256]{1,0:T(8,128)(2,1)S(1)}, u32[]{:S(2)}, u32[]{:S(2)}) %collective-permute-start.5) | collective-permute-done | bytes 8224 | tf_op jit(solution)/shard_map/ppermute | solution.py:435
  27.1 2.4 %collective-permute-start.8 = (bf16[2,16,256]{2,1,0:T(8,128)(2,1)S(1)}, bf16[2,16,256]{2,1,0:T(8,128)(2,1)S(1)}, u32[]{:S(2)}, u32[]{:S(2)}) collective-permute-start(bf16[2,16,256]{2,1,0:T(8,128)(2,1)S(1)} %pad_maximum_fusion.refs_0_), channel_id=1, source_target_pairs={{0,12},{4,8},{8,4},{12,0},{1,13},{5,9},{9,5},{13,1},{2,14},{6,10},... | collective-permute-start | bytes 49160 | tf_op jit(solution)/shard_map/ppermute | solution.py:322
  29.5 0.5 %collective-permute-start.7 = (bf16[2,16,256]{2,1,0:T(8,128)(2,1)S(1)}, bf16[2,16,256]{2,1,0:T(8,128)(2,1)S(1)}, u32[]{:S(2)}, u32[]{:S(2)}) collective-permute-start(bf16[2,16,256]{2,1,0:T(8,128)(2,1)S(1)} %pad_maximum_fusion.refs_0_), channel_id=1, source_target_pairs={{0,8},{4,12},{8,0},{12,4},{1,9},{5,13},{9,1},{13,5},{2,10},{6,14},... | collective-permute-start | bytes 49160 | tf_op jit(solution)/shard_map/ppermute | solution.py:322
  30.3 1.2 %collective-permute-start.6 = (bf16[2,16,256]{2,1,0:T(8,128)(2,1)S(1)}, bf16[2,16,256]{2,1,0:T(8,128)(2,1)S(1)}, u32[]{:S(2)}, u32[]{:S(2)}) collective-permute-start(bf16[2,16,256]{2,1,0:T(8,128)(2,1)S(1)} %pad_maximum_fusion.refs_0_), channel_id=1, source_target_pairs={{0,4},{4,0},{8,12},{12,8},{1,5},{5,1},{9,13},{13,9},{2,6},{6,2},{1... | collective-permute-start | bytes 49160 | tf_op jit(solution)/shard_map/ppermute | solution.py:322
  31.5 2.6 %hidden_down.1.refs_5_ = f32[8,2048]{1,0:T(8,128)S(1)} custom-call(f32[5,8,128]{2,1,0:T(8,128)S(1)} %get-tuple-element.18.stats, bf16[8,7680]{1,0:T(8,128)(2,1)S(1)} %up.1.refs_6_.refs_0_, bf16[8,7680]{1,0:T(8,128)(2,1)S(1)} %collective-permute-done.9.refs_1_, bf16[8,7680]{1,0:T(8,128)(2,1)S(1)} %collective-permute-done.10.refs_2_, ...), custom_call_target="tpu_custom_call" | custom-call | flops 4000000000 | bytes 16800000 | tf_op jit(solution)/shard_map/hidden_down/pallas_call | solution.py:440
  34.2 0.8 %out_projection.1 = (f32[6,2048]{1,0:T(8,128)S(1)}, bf16[6,2048]{1,0:T(8,128)(2,1)S(1)}) custom-call(bf16[2,16,256]{2,1,0:T(8,128)(2,1)S(1)} %pad_maximum_fusion.refs_0_, bf16[2,16,256]{2,1,0:T(8,128)(2,1)S(1)} %collective-permute-done.6.refs_1_, bf16[2,16,256]{2,1,0:T(8,128)(2,1)S(1)} %collective-permute-done.7.refs_2_, ...), custom_call_target="tpu_custom_call" | custom-call | flops 1000000000 | bytes 4000000 | tf_op jit(solution)/shard_map/out_projection/pallas_call | solution.py:453
  35.0 1.5 %collective-permute-start.13 = (bf16[6,2048]{1,0:T(8,128)(2,1)S(1)}, bf16[6,2048]{1,0:T(8,128)(2,1)S(1)}, u32[]{:S(2)}, u32[]{:S(2)}) collective-permute-start(bf16[6,2048]{1,0:T(8,128)(2,1)S(1)} %get-tuple-element.20), channel_id=1, source_target_pairs={{0,2},{1,3},{2,0},{3,1},{4,6},{5,7},{6,4},{7,5},{8,10},{9,11},{10,... | collective-permute-start | bytes 73736 | tf_op jit(solution)/shard_map/ppermute | solution.py:322
  36.9 1.8 %collective-permute-done.14 = bf16[6,2048]{1,0:T(8,128)(2,1)S(1)} collective-permute-done((bf16[6,2048]{1,0:T(8,128)(2,1)S(1)}, bf16[6,2048]{1,0:T(8,128)(2,1)S(1)}, u32[]{:S(2)}, u32[]{:S(2)}) %collective-permute-start.14) | collective-permute-done | bytes 24608 | tf_op jit(solution)/shard_map/ppermute | solution.py:322
  39.0 0.6 %add_convert_fusion = bf16[6,2048]{1,0:T(8,128)(2,1)} fusion(bf16[6,2048]{1,0:T(8,128)(2,1)S(1)} %collective-permute-done.14, bf16[6,2048]{1,0:T(8,128)(2,1)S(1)} %collective-permute-done.13, f32[6,2048]{1,0:T(8,128)S(1)} %get-tuple-element.19, bf16[6,2048]{1,0:T(8,128)(2,1)S(1)} %collective-permute-done.12), kind=kLoop, calls=%fused_computation | loop fusion | flops 86016 | bytes 147456 | tf_op jit(solution)/shard_map/convert_element_type | solution.py:468
  (63 shorter events, 1.6 us)
Async XLA Ops:
  0.7 9.8 %slice-start.4 = ((s8[16777216]{0:T(1024)(128)(4,1)}), s8[4194304]{0:T(1024)(128)(4,1)S(1)}, s32[]{:S(2)}) async-start(s8[16777216]{0:T(1024)(128)(4,1)} %bitcast.12), calls=%async_computation.4 | async-start | bytes 8388608
  0.7 9.8 %slice-start.5 = ((s8[16777216]{0:T(1024)(128)(4,1)}), s8[4194304]{0:T(1024)(128)(4,1)S(1)}, s32[]{:S(2)}) async-start(s8[16777216]{0:T(1024)(128)(4,1)} %bitcast.12), calls=%async_computation.5 | async-start | bytes 8388608
  0.7 9.7 %copy-start.6 = (s32[3]{0:T(128)S(1)}, s32[3]{0:T(128)}, u32[]{:S(2)}) copy-start(s32[3]{0:T(128)} %param.19) | copy-start | bytes 40
  3.7 12.5 %slice-start.8 = ((s8[16777216]{0:T(1024)(128)(4,1)}), s8[4194304]{0:T(1024)(128)(4,1)S(1)}, s32[]{:S(2)}) async-start(s8[16777216]{0:T(1024)(128)(4,1)} %bitcast.14), calls=%async_computation.8 | async-start | bytes 8388608
  3.7 12.5 %slice-start.9 = ((s8[16777216]{0:T(1024)(128)(4,1)}), s8[4194304]{0:T(1024)(128)(4,1)S(1)}, s32[]{:S(2)}) async-start(s8[16777216]{0:T(1024)(128)(4,1)} %bitcast.14), calls=%async_computation.9 | async-start | bytes 8388608
  3.7 12.5 %slice-start.10 = ((s8[16777216]{0:T(1024)(128)(4,1)}), s8[4194304]{0:T(1024)(128)(4,1)S(1)}, s32[]{:S(2)}) async-start(s8[16777216]{0:T(1024)(128)(4,1)} %bitcast.14), calls=%async_computation.10 | async-start | bytes 8388608
  4.8 8.2 %collective-permute-start.2 = (bf16[8,1664]{1,0:T(8,128)(2,1)S(1)}, bf16[8,1664]{1,0:T(8,128)(2,1)S(1)}, u32[]{:S(2)}, u32[]{:S(2)}) collective-permute-start(bf16[8,1664]{1,0:T(8,128)(2,1)S(1)} %get-tuple-element.12.refs_0_), channel_id=1, source_target_pairs={{0,12},{4,8},{8,4},{12,0},{1,13},{5,9},{9,5},{13,1},{2,14},{6,10},... | collective-permute-start | bytes 79880 | tf_op jit(solution)/shard_map/ppermute | solution.py:322
  9.8 4.7 %collective-permute-start.1 = (bf16[8,1664]{1,0:T(8,128)(2,1)S(1)}, bf16[8,1664]{1,0:T(8,128)(2,1)S(1)}, u32[]{:S(2)}, u32[]{:S(2)}) collective-permute-start(bf16[8,1664]{1,0:T(8,128)(2,1)S(1)} %get-tuple-element.12.refs_0_), channel_id=1, source_target_pairs={{0,8},{4,12},{8,0},{12,4},{1,9},{5,13},{9,1},{13,5},{2,10},{6,14},... | collective-permute-start | bytes 79880 | tf_op jit(solution)/shard_map/ppermute | solution.py:322
  9.8 4.7 %collective-permute-start = (bf16[8,1664]{1,0:T(8,128)(2,1)S(1)}, bf16[8,1664]{1,0:T(8,128)(2,1)S(1)}, u32[]{:S(2)}, u32[]{:S(2)}) collective-permute-start(bf16[8,1664]{1,0:T(8,128)(2,1)S(1)} %get-tuple-element.12.refs_0_), channel_id=1, source_target_pairs={{0,4},{4,0},{8,12},{12,8},{1,5},{5,1},{9,13},{13,9},{2,6},{6,2},{1... | collective-permute-start | bytes 79880 | tf_op jit(solution)/shard_map/ppermute | solution.py:322
  10.4 11.8 %collective-permute-start.4 = (bf16[3,256,512]{2,1,0:T(8,128)(2,1)S(1)}, bf16[3,256,512]{2,1,0:T(8,128)(2,1)S(1)}, u32[]{:S(2)}, u32[]{:S(2)}) collective-permute-start(bf16[3,256,512]{2,1,0:T(8,128)(2,1)S(1)} %copy-done.4), channel_id=1, source_target_pairs={{0,1},{1,0},{2,3},{3,2},{4,5},{5,4},{6,7},{7,6},{8,9},{9,8},{10,11... | collective-permute-start | bytes 2359304 | tf_op jit(solution)/shard_map/ppermute | solution.py:322
  14.7 7.5 %collective-permute-start.3 = (bf16[8,1024]{1,0:T(8,128)(2,1)S(1)}, bf16[8,1024]{1,0:T(8,128)(2,1)S(1)}, u32[]{:S(2)}, u32[]{:S(2)}) collective-permute-start(bf16[8,1024]{1,0:T(8,128)(2,1)S(1)} %get-tuple-element.13.after.refs_0_), channel_id=1, source_target_pairs={{0,2},{2,0},{1,3},{3,1},{4,6},{6,4},{5,7},{7,5},{8,10},{10,8},{9,1... | collective-permute-start | bytes 49160 | tf_op jit(solution)/shard_map/ppermute | solution.py:322
  16.3 15.2 %slice-start = ((s8[16777216]{0:T(1024)(128)(4,1)}), s8[4194304]{0:T(1024)(128)(4,1)S(1)}, s32[]{:S(2)}) async-start(s8[16777216]{0:T(1024)(128)(4,1)} %bitcast.9), calls=%async_computation | async-start | bytes 8388608
  16.3 15.2 %slice-start.1 = ((s8[16777216]{0:T(1024)(128)(4,1)}), s8[4194304]{0:T(1024)(128)(4,1)S(1)}, s32[]{:S(2)}) async-start(s8[16777216]{0:T(1024)(128)(4,1)} %bitcast.9), calls=%async_computation.1 | async-start | bytes 8388608
  18.6 11.7 %collective-permute-start.11 = (bf16[8,7680]{1,0:T(8,128)(2,1)S(1)}, bf16[8,7680]{1,0:T(8,128)(2,1)S(1)}, u32[]{:S(2)}, u32[]{:S(2)}) collective-permute-start(bf16[8,7680]{1,0:T(8,128)(2,1)S(1)} %up.1.refs_6_.refs_0_), channel_id=1, source_target_pairs={{0,8},{4,12},{8,0},{12,4},{1,9},{5,13},{9,1},{13,5},{2,10},{6,14},... | collective-permute-start | bytes 368648 | tf_op jit(solution)/shard_map/ppermute | solution.py:322
  20.7 10.8 %collective-permute-start.10 = (bf16[8,7680]{1,0:T(8,128)(2,1)S(1)}, bf16[8,7680]{1,0:T(8,128)(2,1)S(1)}, u32[]{:S(2)}, u32[]{:S(2)}) collective-permute-start(bf16[8,7680]{1,0:T(8,128)(2,1)S(1)} %up.1.refs_6_.refs_0_), channel_id=1, source_target_pairs={{0,12},{4,8},{8,4},{12,0},{1,13},{5,9},{9,5},{13,1},{2,14},{6,10},... | collective-permute-start | bytes 368648 | tf_op jit(solution)/shard_map/ppermute | solution.py:322
  21.3 10.2 %collective-permute-start.9 = (bf16[8,7680]{1,0:T(8,128)(2,1)S(1)}, bf16[8,7680]{1,0:T(8,128)(2,1)S(1)}, u32[]{:S(2)}, u32[]{:S(2)}) collective-permute-start(bf16[8,7680]{1,0:T(8,128)(2,1)S(1)} %up.1.refs_6_.refs_0_), channel_id=1, source_target_pairs={{0,4},{4,0},{8,12},{12,8},{1,5},{5,1},{9,13},{13,9},{2,6},{6,2},{1... | collective-permute-start | bytes 368648 | tf_op jit(solution)/shard_map/ppermute | solution.py:322
  22.2 12.0 %copy-start = (bf16[1024,2048]{1,0:T(8,128)(2,1)S(1)}, bf16[1024,2048]{1,0:T(8,128)(2,1)}, u32[]{:S(2)}) copy-start(bf16[1024,2048]{1,0:T(8,128)(2,1)} %refs_4_.3) | copy-start | bytes 12582916
  23.4 3.7 %collective-permute-start.5 = (bf16[16,256]{1,0:T(8,128)(2,1)S(1)}, bf16[16,256]{1,0:T(8,128)(2,1)S(1)}, u32[]{:S(2)}, u32[]{:S(2)}) collective-permute-start(bf16[16,256]{1,0:T(8,128)(2,1)S(1)} %get-tuple-element.17), channel_id=1, source_target_pairs={{0,2},{2,0},{1,3},{3,1},{4,6},{6,4},{5,7},{7,5},{8,10},{10,8},{9,1... | collective-permute-start | bytes 24584 | tf_op jit(solution)/shard_map/ppermute | solution.py:435
  27.1 7.0 %collective-permute-start.8 = (bf16[2,16,256]{2,1,0:T(8,128)(2,1)S(1)}, bf16[2,16,256]{2,1,0:T(8,128)(2,1)S(1)}, u32[]{:S(2)}, u32[]{:S(2)}) collective-permute-start(bf16[2,16,256]{2,1,0:T(8,128)(2,1)S(1)} %pad_maximum_fusion.refs_0_), channel_id=1, source_target_pairs={{0,12},{4,8},{8,4},{12,0},{1,13},{5,9},{9,5},{13,1},{2,14},{6,10},... | collective-permute-start | bytes 49160 | tf_op jit(solution)/shard_map/ppermute | solution.py:322
  29.5 4.7 %collective-permute-start.7 = (bf16[2,16,256]{2,1,0:T(8,128)(2,1)S(1)}, bf16[2,16,256]{2,1,0:T(8,128)(2,1)S(1)}, u32[]{:S(2)}, u32[]{:S(2)}) collective-permute-start(bf16[2,16,256]{2,1,0:T(8,128)(2,1)S(1)} %pad_maximum_fusion.refs_0_), channel_id=1, source_target_pairs={{0,8},{4,12},{8,0},{12,4},{1,9},{5,13},{9,1},{13,5},{2,10},{6,14},... | collective-permute-start | bytes 49160 | tf_op jit(solution)/shard_map/ppermute | solution.py:322
  30.3 3.9 %collective-permute-start.6 = (bf16[2,16,256]{2,1,0:T(8,128)(2,1)S(1)}, bf16[2,16,256]{2,1,0:T(8,128)(2,1)S(1)}, u32[]{:S(2)}, u32[]{:S(2)}) collective-permute-start(bf16[2,16,256]{2,1,0:T(8,128)(2,1)S(1)} %pad_maximum_fusion.refs_0_), channel_id=1, source_target_pairs={{0,4},{4,0},{8,12},{12,8},{1,5},{5,1},{9,13},{13,9},{2,6},{6,2},{1... | collective-permute-start | bytes 49160 | tf_op jit(solution)/shard_map/ppermute | solution.py:322
  35.0 3.7 %collective-permute-start.14 = (bf16[6,2048]{1,0:T(8,128)(2,1)S(1)}, bf16[6,2048]{1,0:T(8,128)(2,1)S(1)}, u32[]{:S(2)}, u32[]{:S(2)}) collective-permute-start(bf16[6,2048]{1,0:T(8,128)(2,1)S(1)} %get-tuple-element.20), channel_id=1, source_target_pairs={{0,3},{1,2},{2,1},{3,0},{4,7},{5,6},{6,5},{7,4},{8,11},{9,10},{10,... | collective-permute-start | bytes 73736 | tf_op jit(solution)/shard_map/ppermute | solution.py:322
  35.0 4.0 %collective-permute-start.13 = (bf16[6,2048]{1,0:T(8,128)(2,1)S(1)}, bf16[6,2048]{1,0:T(8,128)(2,1)S(1)}, u32[]{:S(2)}, u32[]{:S(2)}) collective-permute-start(bf16[6,2048]{1,0:T(8,128)(2,1)S(1)} %get-tuple-element.20), channel_id=1, source_target_pairs={{0,2},{1,3},{2,0},{3,1},{4,6},{5,7},{6,4},{7,5},{8,10},{9,11},{10,... | collective-permute-start | bytes 73736 | tf_op jit(solution)/shard_map/ppermute | solution.py:322
  36.5 2.5 %collective-permute-start.12 = (bf16[6,2048]{1,0:T(8,128)(2,1)S(1)}, bf16[6,2048]{1,0:T(8,128)(2,1)S(1)}, u32[]{:S(2)}, u32[]{:S(2)}) collective-permute-start(bf16[6,2048]{1,0:T(8,128)(2,1)S(1)} %get-tuple-element.20), channel_id=1, source_target_pairs={{0,1},{1,0},{2,3},{3,2},{4,5},{5,4},{6,7},{7,6},{8,9},{9,8},{10,11... | collective-permute-start | bytes 73736 | tf_op jit(solution)/shard_map/ppermute | solution.py:322
  (10 other events, 56.4 us)
